TPU v7x, 32 devices: a whole 2x2x4 slice. The times are simulated.
32 devices in a mesh: seq: 8 (over z, y), head: 4 (over x, core).
Axes of the slice: x: 2, y: 2, z: 4, core: 2. Of those that a mesh axis runs over, the one named last changes fastest.
Arguments:
- queries: bfloat16 [16384, 4096], P('seq', 'head'), may hold values from -5 to 5
- keys: bfloat16 [16384, 1024], P('seq', 'head'), may hold values from -5 to 5
- values: bfloat16 [16384, 1024], P('seq', 'head'), may hold values from -6 to 6
- grad_out: bfloat16 [16384, 4096], P('seq', 'head'), may hold values from -6 to 6
- vertical: int32 [8], replicated, may hold values from 0 to 15
- columns: int32 [128, 2], P('seq'), may hold values from 0 to 7, as said below
- offsets: int32 [128, 2], P('seq'), may hold values from 1 to 32
Outputs:
- grad_queries: bfloat16 [16384, 4096], P(('seq', 'head'))
- grad_keys: bfloat16 [16384, 1024], P(('seq', 'head'))
- grad_values: bfloat16 [16384, 1024], P(('seq', 'head'))
Inputs may be any that keep to these rules, and one draw needn't show every extreme that they name: `columns`: entry c names vertical column c, held by seq index c; an entry of query block i is below (i // 16 + 1).
All inputs are finite; a program needn't handle non-finite values.
Results may differ from a plain program's by a relative error of at most 0.014.
Values may be sent and summed in bfloat16 or wider, within the bound.
No kernel may reach another device: no remote copies, remote signals or barrier semaphores. Data moves between devices by JAX's collectives and lax.ppermute only.
A program may use at most 192 MiB of HBM per device.

v0:
```python
import math

import jax
import jax.numpy as jnp
from jax import lax
from jax.sharding import PartitionSpec as P

HD = 128
BLK = 128
VERT_DEV = 1


NEGATIVE = -1e30


def passed_along(array, axis, by):
    peers = lax.axis_size(axis)
    pairs = [(i, i + by) for i in range(peers) if 0 <= i + by < peers]
    return lax.ppermute(array, axis, pairs)


def broadcast(value, axis, source):
    kept = jnp.where(lax.axis_index(axis) == source, value, 0).astype(value.dtype)
    return lax.psum(kept, axis)


def shards(queries, keys, values, grad_out, vertical, columns, offsets):
    seq_len = queries.shape[0]
    key_width = keys.shape[1]
    query_width = queries.shape[1]
    kv_local = key_width // HD
    group_size = query_width // key_width
    local_blocks = seq_len // BLK
    vert_total = vertical.shape[0]
    seq_index = lax.axis_index("seq")
    score_scale = 1.0 / math.sqrt(HD)
    key_blocks = keys.reshape(local_blocks, BLK, key_width)
    value_blocks = values.reshape(local_blocks, BLK, key_width)
    prev_keys, prev_values = passed_along((key_blocks, value_blocks), "seq", 1)
    back_keys, back_values = passed_along((key_blocks, value_blocks), "seq", 2)
    own_vertical = lax.dynamic_slice_in_dim(vertical, seq_index * VERT_DEV, VERT_DEV)
    vert_keys = jnp.take(key_blocks, own_vertical, axis=0)
    vert_values = jnp.take(value_blocks, own_vertical, axis=0)
    item_keys, item_values = (vert_keys, vert_values)
    per_device = item_keys.shape[0]
    far_keys, far_values = (
        lax.all_gather(item_keys, "seq", axis=0, tiled=True),
        lax.all_gather(item_values, "seq", axis=0, tiled=True),
    )
    sink_keys, sink_values = (
        broadcast(key_blocks[:1], "seq", 0),
        broadcast(value_blocks[:1], "seq", 0),
    )
    far_keys = jnp.concatenate([far_keys, sink_keys], axis=0)
    far_values = jnp.concatenate([far_values, sink_values], axis=0)
    block_ids = jnp.arange(local_blocks, dtype=jnp.int32)
    global_ids = seq_index * local_blocks + block_ids
    vert_ids = jnp.arange(vert_total, dtype=jnp.int32)
    vert_global = vert_ids // VERT_DEV * local_blocks + vertical

    def vertical_lookup(column):
        column_match = column[:, None] == vert_ids[None, :]
        return jnp.sum(jnp.where(column_match, vert_global[None, :], 0), axis=1)

    near_base = 2 * local_blocks
    far_base = 3 * local_blocks

    def far_place(column):
        return far_base + column // VERT_DEV * per_device + column % VERT_DEV

    slot_blocks = jnp.stack(
        [
            jnp.zeros_like(global_ids),
            global_ids,
            global_ids - offsets[:, 0],
            global_ids - offsets[:, 1],
            vertical_lookup(columns[:, 0]),
            vertical_lookup(columns[:, 1]),
        ],
        axis=1,
    )
    slot_index = jnp.stack(
        [
            jnp.full_like(global_ids, far_base + vert_total),
            near_base + block_ids,
            near_base + block_ids - offsets[:, 0],
            near_base + block_ids - offsets[:, 1],
            far_place(columns[:, 0]),
            far_place(columns[:, 1]),
        ],
        axis=1,
    )
    slot_flags = []
    for slot_number in range(6):
        current = slot_blocks[:, slot_number]
        slot_good = (current >= 0) & (current <= global_ids)
        for prior in range(slot_number):
            slot_good = slot_good & (current != slot_blocks[:, prior])
        slot_flags.append(slot_good)
    slot_valid = jnp.stack(slot_flags, axis=1)
    pool_keys = jnp.concatenate([back_keys, prev_keys, key_blocks, far_keys], axis=0)
    pool_values = jnp.concatenate([back_values, prev_values, value_blocks, far_values], axis=0)
    pool_size = pool_keys.shape[0]
    step_blocks = min(local_blocks, max(1, 512 // BLK))
    step_count = local_blocks // step_blocks
    query_groups = queries.reshape(step_count, step_blocks, BLK, kv_local, group_size, HD)
    grad_groups = grad_out.reshape(step_count, step_blocks, BLK, kv_local, group_size, HD)
    index_groups = slot_index.reshape(step_count, step_blocks, 6)
    block_groups = slot_blocks.reshape(step_count, step_blocks, 6)
    valid_groups = slot_valid.reshape(step_count, step_blocks, 6)
    global_groups = global_ids.reshape(step_count, step_blocks)
    positions = jnp.arange(BLK)
    causal = positions[None, :] <= positions[:, None]
    pool_range = jnp.arange(pool_size, dtype=jnp.int32)

    def group_step(accums, inputs):
        acc_keys, acc_values = accums
        query_rows, grad_rows, index_rows, block_rows, valid_rows, global_rows = inputs
        flat_index = index_rows.reshape(-1)
        slot_keys = jnp.take(pool_keys, flat_index, axis=0).reshape(
            step_blocks, 6, BLK, kv_local, HD
        )
        slot_values = jnp.take(pool_values, flat_index, axis=0).reshape(
            step_blocks, 6, BLK, kv_local, HD
        )
        scores = (
            jnp.einsum(
                "bqkgd,bsckd->bkgqsc", query_rows, slot_keys, preferred_element_type=jnp.float32
            )
            * score_scale
        )
        earlier = block_rows < global_rows[:, None]
        visible = valid_rows[:, None, :, None] & (
            earlier[:, None, :, None] | causal[None, :, None, :]
        )
        visible = visible[:, None, None]
        masked = jnp.where(visible, scores, NEGATIVE)
        row_top = jnp.max(masked, axis=(4, 5), keepdims=True)
        row_total = jnp.sum(
            jnp.where(visible, jnp.exp(masked - row_top), 0.0), axis=(4, 5), keepdims=True
        )
        prob_full = jnp.where(visible, jnp.exp(masked - (row_top + jnp.log(row_total))), 0.0)
        grad_prob = jnp.einsum(
            "bqkgd,bsckd->bkgqsc", grad_rows, slot_values, preferred_element_type=jnp.float32
        )
        row_delta = jnp.sum(prob_full * grad_prob, axis=(4, 5), keepdims=True)
        dscore = (prob_full * (grad_prob - row_delta) * score_scale).astype(jnp.bfloat16)
        prob_half = prob_full.astype(jnp.bfloat16)
        grad_query = jnp.einsum(
            "bkgqsc,bsckd->bqkgd", dscore, slot_keys, preferred_element_type=jnp.float32
        ).astype(jnp.bfloat16)
        key_terms = jnp.einsum(
            "bkgqsc,bqkgd->bsckd", dscore, query_rows, preferred_element_type=jnp.float32
        ).reshape(step_blocks * 6, BLK * key_width)
        value_terms = jnp.einsum(
            "bkgqsc,bqkgd->bsckd", prob_half, grad_rows, preferred_element_type=jnp.float32
        ).reshape(step_blocks * 6, BLK * key_width)
        onehot = (pool_range[:, None] == flat_index[None, :]).astype(jnp.float32)
        acc_keys = acc_keys + jnp.dot(onehot, key_terms, precision=lax.Precision.HIGHEST)
        acc_values = acc_values + jnp.dot(onehot, value_terms, precision=lax.Precision.HIGHEST)
        return ((acc_keys, acc_values), grad_query)

    zero_acc = jnp.zeros((pool_size, BLK * key_width), jnp.float32)
    (acc_keys, acc_values), grad_query = lax.scan(
        group_step,
        (zero_acc, zero_acc),
        (query_groups, grad_groups, index_groups, block_groups, valid_groups, global_groups),
    )
    grad_query = grad_query.reshape(seq_len, query_width)
    acc_keys = acc_keys.reshape(pool_size, BLK, key_width)
    acc_values = acc_values.reshape(pool_size, BLK, key_width)
    own_keys = acc_keys[near_base:far_base]
    own_values = acc_values[near_base:far_base]
    first_keys = acc_keys[local_blocks:near_base]
    first_values = acc_values[local_blocks:near_base]
    second_keys = acc_keys[:local_blocks]
    second_values = acc_values[:local_blocks]
    ret_keys, ret_values = (
        passed_along(first_keys.astype(jnp.bfloat16), "seq", -1).astype(first_keys.dtype),
        passed_along(first_values.astype(jnp.bfloat16), "seq", -1).astype(first_values.dtype),
    )
    far_ret_keys, far_ret_values = (
        passed_along(second_keys.astype(jnp.bfloat16), "seq", -2).astype(second_keys.dtype),
        passed_along(second_values.astype(jnp.bfloat16), "seq", -2).astype(second_values.dtype),
    )
    own_keys = own_keys + ret_keys + far_ret_keys
    own_values = own_values + ret_values + far_ret_values
    table_keys = acc_keys[far_base : far_base + vert_total]
    table_values = acc_values[far_base : far_base + vert_total]
    got_keys, got_values = (
        lax.psum_scatter(
            table_keys.astype(jnp.bfloat16), "seq", scatter_dimension=0, tiled=True
        ).astype(jnp.float32),
        lax.psum_scatter(
            table_values.astype(jnp.bfloat16), "seq", scatter_dimension=0, tiled=True
        ).astype(jnp.float32),
    )
    place_table = (block_ids[:, None] == own_vertical[None, :]).astype(jnp.float32)
    own_keys = own_keys + jnp.einsum(
        "nv,vck->nck", place_table, got_keys, precision=lax.Precision.HIGHEST
    )
    own_values = own_values + jnp.einsum(
        "nv,vck->nck", place_table, got_values, precision=lax.Precision.HIGHEST
    )
    first_block = (block_ids == 0).astype(jnp.float32)[:, None, None]
    sink_grad_keys, sink_grad_values = (
        lax.psum(
            acc_keys[far_base + vert_total : far_base + vert_total + 1].astype(jnp.bfloat16), "seq"
        ).astype(jnp.float32),
        lax.psum(
            acc_values[far_base + vert_total : far_base + vert_total + 1].astype(jnp.bfloat16),
            "seq",
        ).astype(jnp.float32),
    )
    weight = first_block * (seq_index == 0).astype(jnp.float32)
    own_keys = own_keys + weight * sink_grad_keys
    own_values = own_values + weight * sink_grad_values
    grad_keys = own_keys.reshape(seq_len, key_width).astype(jnp.bfloat16)
    grad_values = own_values.reshape(seq_len, key_width).astype(jnp.bfloat16)
    out_query, out_keys, out_values = (
        lax.all_to_all(grad_query, "head", split_axis=0, concat_axis=1, tiled=True),
        lax.all_to_all(grad_keys, "head", split_axis=0, concat_axis=1, tiled=True),
        lax.all_to_all(grad_values, "head", split_axis=0, concat_axis=1, tiled=True),
    )
    return (out_query, out_keys, out_values)


def solution(mesh):
    return jax.shard_map(
        shards,
        mesh=mesh,
        in_specs=(
            P("seq", "head"),
            P("seq", "head"),
            P("seq", "head"),
            P("seq", "head"),
            P(),
            P("seq", None),
            P("seq", None),
        ),
        out_specs=(P(("seq", "head"), None), P(("seq", "head"), None), P(("seq", "head"), None)),
        check_vma=False,
    )
```

profile of v0, /device:TPU:0, one launch (start us, length us, event | category | flops | bytes accessed | tf_op | source)
XLA Modules:
  0.0 863.8 jit_solution(1624516866888957959)
XLA Ops:
  7.2 6.0 collective-permute-start
  13.2 4.4 collective-permute-start.1
  19.1 3.5 collective-permute-start.3
  35.7 7.7 reshape.344
  43.5 7.7 reshape.347
  51.2 82.5 %all_gather.6 = bf16[8,128,256]{2,1,0:T(8,128)(2,1)S(1)} all-gather(bf16[1,128,256]{2,1,0:T(8,128)(2,1)S(1)} %dynamic-slice_select_fusion.1), channel_id=1, replica_groups=mesh['seq'=8,'head'=4] {'seq'}, dimensions={0}, use_global_device_ids=true | all-gather | bytes 589824 | tf_op jit(solution)/shard_map/all_gather | solution.py:47
  133.7 31.2 %all_gather.7 = bf16[8,128,256]{2,1,0:T(8,128)(2,1)S(1)} all-gather(bf16[1,128,256]{2,1,0:T(8,128)(2,1)S(1)} %dynamic-slice_select_fusion), channel_id=1, replica_groups=mesh['seq'=8,'head'=4] {'seq'}, dimensions={0}, use_global_device_ids=true | all-gather | bytes 589824 | tf_op jit(solution)/shard_map/all_gather | solution.py:48
  178.5 361.7 %while.16 = (s32[]{:T(128)}, f32[57,32768]{1,0:T(8,128)}, f32[57,32768]{1,0:T(8,128)}, bf16[4,4,128,2,4,128]{5,4,3,2,1,0:T(4,128)(2,1)}, s32[4,4,6]{2,1,0:T(4,12...) while((s32[]{:T(128)}, f32[57,32768]{1,0:T(8,128)}, ...), condition=%wide.region_8.11_spmd.clone, body=%wide.region_4.10_spmd.clone.sunk | while | flops 5197672448 | bytes 374828736 | solution.py:164
  182.0 3.9 gather_fusion.1
  195.9 3.2 select_reduce_fusion.4
  200.4 3.9 fusion.76
  204.3 3.4 copy.183
  207.8 4.1 reshape.502
  211.9 6.6 convolution_add_fusion.5
  220.9 11.4 %fusion.74 = (f32[4,2,4,128]{3,2,1,0:T(4,128)S(1)}, f32[4,2,6,128,128,4]{4,3,5,2,1,0:T(8,128)}) fusion(f32[4,2,4,128]{3,2,1,0:T(4,128)S(1)} %bitcast.240, f32[4,2,6,128,128,4]{4,3,5,2,1,0:T(8,128)} %copy-done, pred[4,128,6,128]{1,3,2,0:T(8,128)(4,1)S(1)} %or_and_fusion.2, bf16[1,4,128,2,4,128]{5,4,3,2,1,0:T(4,128)(2,1)} %copy-done.6, ...), kind=kOutput, calls=%fused_computation.8.clone.1 | convolution fusion | flops 824176640 | bytes 28213248 | tf_op jit(solution)/shard_map/while/body/eval_jaxpr/bqkgd,bsckd->bkgqsc/dot_general | solution.py:143
  233.8 7.7 fusion.75
  246.4 3.4 copy.182
  249.8 5.7 reshape.501
  255.5 8.1 convolution_add_fusion.4
  270.4 3.9 gather_fusion.1
  288.8 3.9 fusion.76
  292.7 3.4 copy.183
  296.2 4.1 reshape.502
  300.3 8.1 convolution_add_fusion.5
  310.8 11.4 %fusion.74 = (f32[4,2,4,128]{3,2,1,0:T(4,128)S(1)}, f32[4,2,6,128,128,4]{4,3,5,2,1,0:T(8,128)}) fusion(f32[4,2,4,128]{3,2,1,0:T(4,128)S(1)} %bitcast.240, f32[4,2,6,128,128,4]{4,3,5,2,1,0:T(8,128)} %copy-done, pred[4,128,6,128]{1,3,2,0:T(8,128)(4,1)S(1)} %or_and_fusion.2, bf16[1,4,128,2,4,128]{5,4,3,2,1,0:T(4,128)(2,1)} %copy-done.6, ...), kind=kOutput, calls=%fused_computation.8.clone.1 | convolution fusion | flops 824176640 | bytes 28213248 | tf_op jit(solution)/shard_map/while/body/eval_jaxpr/bqkgd,bsckd->bkgqsc/dot_general | solution.py:143
  323.7 7.7 fusion.75
  336.3 3.4 copy.182
  339.7 5.7 reshape.501
  345.4 9.4 %convolution_add_fusion.4 = f32[57,32768]{1,0:T(8,128)} fusion(f32[24,32768]{1,0:T(8,128)} %reshape.501, f32[57,32768]{1,0:T(8,128)} %get-tuple-element.367, pred[]{:T(512)S(6)} %compare.13, s32[24]{0:T(128)S(1)} %copy-done.12), kind=kOutput, calls=%fused_computation.5.clone.1 | convolution fusion | flops 541656384 | bytes 18088032 | tf_op jit(solution)/shard_map/while/body/eval_jaxpr/dot_general | solution.py:159
  361.5 3.9 gather_fusion.1
  375.4 3.2 select_reduce_fusion.4
  379.9 3.9 fusion.76
  383.8 3.4 copy.183
  387.3 4.1 reshape.502
  391.4 8.1 convolution_add_fusion.5
  401.9 11.4 %fusion.74 = (f32[4,2,4,128]{3,2,1,0:T(4,128)S(1)}, f32[4,2,6,128,128,4]{4,3,5,2,1,0:T(8,128)}) fusion(f32[4,2,4,128]{3,2,1,0:T(4,128)S(1)} %bitcast.240, f32[4,2,6,128,128,4]{4,3,5,2,1,0:T(8,128)} %copy-done, pred[4,128,6,128]{1,3,2,0:T(8,128)(4,1)S(1)} %or_and_fusion.2, bf16[1,4,128,2,4,128]{5,4,3,2,1,0:T(4,128)(2,1)} %copy-done.6, ...), kind=kOutput, calls=%fused_computation.8.clone.1 | convolution fusion | flops 824176640 | bytes 28213248 | tf_op jit(solution)/shard_map/while/body/eval_jaxpr/bqkgd,bsckd->bkgqsc/dot_general | solution.py:143
  414.8 7.7 fusion.75
  427.4 3.4 copy.182
  430.8 5.7 reshape.501
  436.5 9.4 %convolution_add_fusion.4 = f32[57,32768]{1,0:T(8,128)} fusion(f32[24,32768]{1,0:T(8,128)} %reshape.501, f32[57,32768]{1,0:T(8,128)} %get-tuple-element.367, pred[]{:T(512)S(6)} %compare.13, s32[24]{0:T(128)S(1)} %copy-done.12), kind=kOutput, calls=%fused_computation.5.clone.1 | convolution fusion | flops 541656384 | bytes 18088032 | tf_op jit(solution)/shard_map/while/body/eval_jaxpr/dot_general | solution.py:159
  452.7 3.9 gather_fusion.1
  471.0 3.9 fusion.76
  475.0 3.4 copy.183
  478.4 4.1 reshape.502
  482.5 8.1 convolution_add_fusion.5
  493.0 11.4 %fusion.74 = (f32[4,2,4,128]{3,2,1,0:T(4,128)S(1)}, f32[4,2,6,128,128,4]{4,3,5,2,1,0:T(8,128)}) fusion(f32[4,2,4,128]{3,2,1,0:T(4,128)S(1)} %bitcast.240, f32[4,2,6,128,128,4]{4,3,5,2,1,0:T(8,128)} %copy-done, pred[4,128,6,128]{1,3,2,0:T(8,128)(4,1)S(1)} %or_and_fusion.2, bf16[1,4,128,2,4,128]{5,4,3,2,1,0:T(4,128)(2,1)} %copy-done.6, ...), kind=kOutput, calls=%fused_computation.8.clone.1 | convolution fusion | flops 824176640 | bytes 28213248 | tf_op jit(solution)/shard_map/while/body/eval_jaxpr/bqkgd,bsckd->bkgqsc/dot_general | solution.py:143
  506.0 7.7 fusion.75
  518.5 3.4 copy.182
  521.9 5.7 reshape.501
  527.6 9.4 %convolution_add_fusion.4 = f32[57,32768]{1,0:T(8,128)} fusion(f32[24,32768]{1,0:T(8,128)} %reshape.501, f32[57,32768]{1,0:T(8,128)} %get-tuple-element.367, pred[]{:T(512)S(6)} %compare.13, s32[24]{0:T(128)S(1)} %copy-done.12), kind=kOutput, calls=%fused_computation.5.clone.1 | convolution fusion | flops 541656384 | bytes 18088032 | tf_op jit(solution)/shard_map/while/body/eval_jaxpr/dot_general | solution.py:159
  540.3 3.8 convert.30
  547.0 3.8 convert.33
  576.0 46.0 %all-reduce.5.cloned.1.call-done = (bf16[128,256]{1,0:T(8,128)(2,1)}, bf16[128,256]{1,0:T(8,128)(2,1)}) async-done(((bf16[128,256]{1,0:T(8,128)(2,1)}, bf16[128,256]{1,0:T(8,128)(2,1)}), (bf16[128,256]{1,0:T(8,128)(2,1)}, bf16[128,256]{1,0:T(8,128)(2,1)})) %all-reduce.5.cloned.1.call-update) | async-done | bytes 131088 | tf_op jit(solution)/shard_map/psum | solution.py:207
  623.7 62.5 %reduce-scatter.5.cloned.1.call-done = bf16[1,128,256]{2,1,0:T(8,128)(2,1)} async-done(((bf16[8,128,256]{2,1,0:T(8,128)(2,1)}), bf16[1,128,256]{2,1,0:T(8,128)(2,1)}) %reduce-scatter.5.cloned.1.call-update) | async-done | bytes 65552 | tf_op jit(solution)/shard_map/reduce_scatter | solution.py:194
  687.1 63.6 %reduce-scatter.3.cloned.1.call-done = bf16[1,128,256]{2,1,0:T(8,128)(2,1)} async-done(((bf16[8,128,256]{2,1,0:T(8,128)(2,1)}), bf16[1,128,256]{2,1,0:T(8,128)(2,1)}) %reduce-scatter.3.cloned.1.call-update) | async-done | bytes 65552 | tf_op jit(solution)/shard_map/reduce_scatter | solution.py:191
  751.6 5.1 fusion.34
  756.7 17.0 %all_to_all.51 = bf16[4,512,256]{2,1,0:T(8,128)(2,1)S(1)} all-to-all(bf16[4,512,256]{2,1,0:T(8,128)(2,1)S(1)} %bitcast.236), channel_id=1, replica_groups=mesh['seq'=8,'head'=4] {'head'}, dimensions={0} | all-to-all | bytes 2097152 | tf_op jit(solution)/shard_map/all_to_all | solution.py:222
  773.7 3.5 all-to-all-start.2
  777.2 7.8 all_to_all.38
  785.0 6.6 all-to-all-done.2
  791.6 4.8 all-to-all-start
  800.2 44.5 %all-to-all-done = bf16[4,512,1024]{2,1,0:T(8,128)(2,1)} async-done(((bf16[4,512,1024]{2,1,0:T(8,128)(2,1)}), bf16[4,512,1024]{2,1,0:T(8,128)(2,1)}, u32[]{:S(2)}, u32[]{:S(2)}) %all-to-all-start) | async-done | bytes 4194336 | tf_op jit(solution)/shard_map/all_to_all | solution.py:221
  844.7 6.3 copy.103
  850.9 6.3 copy.108
  (374 shorter events, 174.0 us)
Async XLA Ops:
  7.2 167.6 %all-reduce.7.cloned.1.call-start = ((), (), s32[]{:S(2)}) async-start(), calls=%async_computation.8 | async-start | bytes 262144 | tf_op jit(solution)/shard_map/psum | solution.py:24
  7.2 157.7 %collective-permute-start = (bf16[16,128,256]{2,1,0:T(8,128)(2,1)}, bf16[16,128,256]{2,1,0:T(8,128)(2,1)}, u32[]{:S(2)}, u32[]{:S(2)}) collective-permute-start(bf16[16,128,256]{2,1,0:T(8,128)(2,1)} %bitcast.243), channel_id=1, source_target_pairs={{0,8},{4,12},{8,16},{12,20},{16,24},{20,28},{1,9},{5,13},{9,17},{1... | collective-permute-start | bytes 3145736 | tf_op jit(solution)/shard_map/ppermute | solution.py:19
  13.2 154.0 %collective-permute-start.1 = (bf16[16,128,256]{2,1,0:T(8,128)(2,1)}, bf16[16,128,256]{2,1,0:T(8,128)(2,1)}, u32[]{:S(2)}, u32[]{:S(2)}) collective-permute-start(bf16[16,128,256]{2,1,0:T(8,128)(2,1)} %bitcast.244), channel_id=1, source_target_pairs={{0,4},{4,8},{8,12},{12,16},{16,20},{20,24},{24,28},{1,5},{5,9},{9,... | collective-permute-start | bytes 3145736 | tf_op jit(solution)/shard_map/ppermute | solution.py:19
  17.6 153.1 %collective-permute-start.2 = (bf16[16,128,256]{2,1,0:T(8,128)(2,1)}, bf16[16,128,256]{2,1,0:T(8,128)(2,1)S(1)}, u32[]{:S(2)}, u32[]{:S(2)}) collective-permute-start(bf16[16,128,256]{2,1,0:T(8,128)(2,1)} %bitcast.247), channel_id=1, source_target_pairs={{0,8},{4,12},{8,16},{12,20},{16,24},{20,28},{1,9},{5,13},{9,17},{1... | collective-permute-start | bytes 3145736 | tf_op jit(solution)/shard_map/ppermute | solution.py:19
  19.1 152.6 %collective-permute-start.3 = (bf16[16,128,256]{2,1,0:T(8,128)(2,1)}, bf16[16,128,256]{2,1,0:T(8,128)(2,1)S(1)}, u32[]{:S(2)}, u32[]{:S(2)}) collective-permute-start(bf16[16,128,256]{2,1,0:T(8,128)(2,1)} %bitcast.248), channel_id=1, source_target_pairs={{0,4},{4,8},{8,12},{12,16},{16,20},{20,24},{24,28},{1,5},{5,9},{9,... | collective-permute-start | bytes 3145736 | tf_op jit(solution)/shard_map/ppermute | solution.py:19
  25.6 596.4 %all-reduce.5.cloned.1.call-start = ((), (), s32[]{:S(2)}) async-start(), calls=%async_computation.7 | async-start | bytes 262144 | tf_op jit(solution)/shard_map/psum | solution.py:207
  51.2 118.5 %copy-start.9 = (bf16[2048,256]{1,0:T(8,128)(2,1)S(1)}, bf16[2048,256]{1,0:T(8,128)(2,1)}, u32[]{:S(2)}) copy-start(bf16[2048,256]{1,0:T(8,128)(2,1)} %param.14) | copy-start | bytes 3145732
  178.5 12.0 %copy-start.15 = (s32[4,4]{1,0:T(4,128)}, s32[4,4]{1,0:T(4,128)S(1)}, u32[]{:S(2)}) copy-start(s32[4,4]{1,0:T(4,128)S(1)} %get-tuple-element.388) | copy-start | bytes 196 | tf_op jit(solution)/shard_map/while
  178.5 12.1 %copy-start.13 = (s32[4,4,6]{2,1,0:T(4,128)}, s32[4,4,6]{2,1,0:T(4,128)S(1)}, u32[]{:S(2)}) copy-start(s32[4,4,6]{2,1,0:T(4,128)S(1)} %get-tuple-element.387) | copy-start | bytes 1156 | tf_op jit(solution)/shard_map/while
  178.5 12.1 %copy-start.17 = (pred[4,4,6]{2,1,0:T(4,128)(4,1)}, pred[4,4,6]{2,1,0:T(4,128)(4,1)S(1)}, u32[]{:S(2)}) copy-start(pred[4,4,6]{2,1,0:T(4,128)(4,1)S(1)} %get-tuple-element.386) | copy-start | bytes 292 | tf_op jit(solution)/shard_map/while
  179.3 6.6 copy-start.11
  193.3 5.7 copy-start.6
  220.9 11.5 %slice-start = ((s8[12582912]{0:T(1024)(128)(4,1)}), s8[4194304]{0:T(1024)(128)(4,1)S(1)}, s32[]{:S(2)}) async-start(s8[12582912]{0:T(1024)(128)(4,1)} %bitcast.218), calls=%async_computation.9 | async-start | bytes 8388608 | tf_op jit(solution)/shard_map/while
  220.9 11.5 %slice-start.1 = ((s8[12582912]{0:T(1024)(128)(4,1)}), s8[4194304]{0:T(1024)(128)(4,1)S(1)}, s32[]{:S(2)}) async-start(s8[12582912]{0:T(1024)(128)(4,1)} %bitcast.218), calls=%async_computation.10 | async-start | bytes 8388608 | tf_op jit(solution)/shard_map/while
  220.9 12.9 %slice-start.2 = ((s8[12582912]{0:T(1024)(128)(4,1)}), s8[4194304]{0:T(1024)(128)(4,1)S(1)}, s32[]{:S(2)}) async-start(s8[12582912]{0:T(1024)(128)(4,1)} %bitcast.218), calls=%async_computation.11 | async-start | bytes 8388608 | tf_op jit(solution)/shard_map/while
  233.8 10.3 %copy-start.3 = (bf16[1,4,128,2,4,128]{5,4,3,2,1,0:T(4,128)(2,1)S(1)}, bf16[1,4,128,2,4,128]{5,4,3,2,1,0:T(4,128)(2,1)}, u32[]{:S(2)}) copy-start(bf16[1,4,128,2,4,128]{5,4,3,2,1,0:T(4,128)(2,1)} %copy-done.2) | copy-start | bytes 3145732 | tf_op jit(solution)/shard_map/while
  249.8 5.7 copy-start.12
  249.8 13.9 %slice-start.3 = ((s8[6291456]{0:T(1024)(128)(4,1)}), s8[2097152]{0:T(1024)(128)(4,1)S(1)}, s32[]{:S(2)}) async-start(s8[6291456]{0:T(1024)(128)(4,1)} %bitcast.220), calls=%async_computation.12 | async-start | bytes 4194304 | tf_op jit(solution)/shard_map/while
  255.5 8.1 slice-start.4
  255.5 8.1 copy-start.5
  266.9 12.0 %copy-start.15 = (s32[4,4]{1,0:T(4,128)}, s32[4,4]{1,0:T(4,128)S(1)}, u32[]{:S(2)}) copy-start(s32[4,4]{1,0:T(4,128)S(1)} %get-tuple-element.388) | copy-start | bytes 196 | tf_op jit(solution)/shard_map/while
  266.9 12.1 %copy-start.13 = (s32[4,4,6]{2,1,0:T(4,128)}, s32[4,4,6]{2,1,0:T(4,128)S(1)}, u32[]{:S(2)}) copy-start(s32[4,4,6]{2,1,0:T(4,128)S(1)} %get-tuple-element.387) | copy-start | bytes 1156 | tf_op jit(solution)/shard_map/while
  266.9 12.1 %copy-start.17 = (pred[4,4,6]{2,1,0:T(4,128)(4,1)}, pred[4,4,6]{2,1,0:T(4,128)(4,1)S(1)}, u32[]{:S(2)}) copy-start(pred[4,4,6]{2,1,0:T(4,128)(4,1)S(1)} %get-tuple-element.386) | copy-start | bytes 292 | tf_op jit(solution)/shard_map/while
  267.7 6.6 copy-start.11
  281.7 5.7 copy-start.6
  310.8 11.5 %slice-start = ((s8[12582912]{0:T(1024)(128)(4,1)}), s8[4194304]{0:T(1024)(128)(4,1)S(1)}, s32[]{:S(2)}) async-start(s8[12582912]{0:T(1024)(128)(4,1)} %bitcast.218), calls=%async_computation.9 | async-start | bytes 8388608 | tf_op jit(solution)/shard_map/while
  310.8 11.5 %slice-start.1 = ((s8[12582912]{0:T(1024)(128)(4,1)}), s8[4194304]{0:T(1024)(128)(4,1)S(1)}, s32[]{:S(2)}) async-start(s8[12582912]{0:T(1024)(128)(4,1)} %bitcast.218), calls=%async_computation.10 | async-start | bytes 8388608 | tf_op jit(solution)/shard_map/while
  310.8 12.9 %slice-start.2 = ((s8[12582912]{0:T(1024)(128)(4,1)}), s8[4194304]{0:T(1024)(128)(4,1)S(1)}, s32[]{:S(2)}) async-start(s8[12582912]{0:T(1024)(128)(4,1)} %bitcast.218), calls=%async_computation.11 | async-start | bytes 8388608 | tf_op jit(solution)/shard_map/while
  323.7 10.3 %copy-start.3 = (bf16[1,4,128,2,4,128]{5,4,3,2,1,0:T(4,128)(2,1)S(1)}, bf16[1,4,128,2,4,128]{5,4,3,2,1,0:T(4,128)(2,1)}, u32[]{:S(2)}) copy-start(bf16[1,4,128,2,4,128]{5,4,3,2,1,0:T(4,128)(2,1)} %copy-done.2) | copy-start | bytes 3145732 | tf_op jit(solution)/shard_map/while
  339.7 15.1 %slice-start.3 = ((s8[6291456]{0:T(1024)(128)(4,1)}), s8[2097152]{0:T(1024)(128)(4,1)S(1)}, s32[]{:S(2)}) async-start(s8[6291456]{0:T(1024)(128)(4,1)} %bitcast.220), calls=%async_computation.12 | async-start | bytes 4194304 | tf_op jit(solution)/shard_map/while
  345.4 9.4 %slice-start.4 = ((s8[6291456]{0:T(1024)(128)(4,1)}), s8[4194304]{0:T(1024)(128)(4,1)S(1)}, s32[]{:S(2)}) async-start(s8[6291456]{0:T(1024)(128)(4,1)} %bitcast.220), calls=%async_computation.13 | async-start | bytes 8388608 | tf_op jit(solution)/shard_map/while
  345.4 9.4 %copy-start.5 = (bf16[4,6,128,2,128,1]{2,4,1,5,3,0:T(8,128)(2,1)S(1)}, bf16[4,6,128,2,128,1]{2,4,1,5,3,0:T(8,128)(2,1)}, u32[]{:S(2)}) copy-start(bf16[4,6,128,2,128,1]{2,4,1,5,3,0:T(8,128)(2,1)} %copy-done.4) | copy-start | bytes 4718596 | tf_op jit(solution)/shard_map/while
  358.0 12.0 %copy-start.15 = (s32[4,4]{1,0:T(4,128)}, s32[4,4]{1,0:T(4,128)S(1)}, u32[]{:S(2)}) copy-start(s32[4,4]{1,0:T(4,128)S(1)} %get-tuple-element.388) | copy-start | bytes 196 | tf_op jit(solution)/shard_map/while
  358.0 12.1 %copy-start.13 = (s32[4,4,6]{2,1,0:T(4,128)}, s32[4,4,6]{2,1,0:T(4,128)S(1)}, u32[]{:S(2)}) copy-start(s32[4,4,6]{2,1,0:T(4,128)S(1)} %get-tuple-element.387) | copy-start | bytes 1156 | tf_op jit(solution)/shard_map/while
  358.0 12.1 %copy-start.17 = (pred[4,4,6]{2,1,0:T(4,128)(4,1)}, pred[4,4,6]{2,1,0:T(4,128)(4,1)S(1)}, u32[]{:S(2)}) copy-start(pred[4,4,6]{2,1,0:T(4,128)(4,1)S(1)} %get-tuple-element.386) | copy-start | bytes 292 | tf_op jit(solution)/shard_map/while
  358.8 6.6 copy-start.11
  372.9 5.7 copy-start.6
  401.9 11.5 %slice-start = ((s8[12582912]{0:T(1024)(128)(4,1)}), s8[4194304]{0:T(1024)(128)(4,1)S(1)}, s32[]{:S(2)}) async-start(s8[12582912]{0:T(1024)(128)(4,1)} %bitcast.218), calls=%async_computation.9 | async-start | bytes 8388608 | tf_op jit(solution)/shard_map/while
  401.9 11.5 %slice-start.1 = ((s8[12582912]{0:T(1024)(128)(4,1)}), s8[4194304]{0:T(1024)(128)(4,1)S(1)}, s32[]{:S(2)}) async-start(s8[12582912]{0:T(1024)(128)(4,1)} %bitcast.218), calls=%async_computation.10 | async-start | bytes 8388608 | tf_op jit(solution)/shard_map/while
  401.9 12.9 %slice-start.2 = ((s8[12582912]{0:T(1024)(128)(4,1)}), s8[4194304]{0:T(1024)(128)(4,1)S(1)}, s32[]{:S(2)}) async-start(s8[12582912]{0:T(1024)(128)(4,1)} %bitcast.218), calls=%async_computation.11 | async-start | bytes 8388608 | tf_op jit(solution)/shard_map/while
  414.8 10.3 %copy-start.3 = (bf16[1,4,128,2,4,128]{5,4,3,2,1,0:T(4,128)(2,1)S(1)}, bf16[1,4,128,2,4,128]{5,4,3,2,1,0:T(4,128)(2,1)}, u32[]{:S(2)}) copy-start(bf16[1,4,128,2,4,128]{5,4,3,2,1,0:T(4,128)(2,1)} %copy-done.2) | copy-start | bytes 3145732 | tf_op jit(solution)/shard_map/while
  430.8 15.1 %slice-start.3 = ((s8[6291456]{0:T(1024)(128)(4,1)}), s8[2097152]{0:T(1024)(128)(4,1)S(1)}, s32[]{:S(2)}) async-start(s8[6291456]{0:T(1024)(128)(4,1)} %bitcast.220), calls=%async_computation.12 | async-start | bytes 4194304 | tf_op jit(solution)/shard_map/while
  436.5 9.4 %slice-start.4 = ((s8[6291456]{0:T(1024)(128)(4,1)}), s8[4194304]{0:T(1024)(128)(4,1)S(1)}, s32[]{:S(2)}) async-start(s8[6291456]{0:T(1024)(128)(4,1)} %bitcast.220), calls=%async_computation.13 | async-start | bytes 8388608 | tf_op jit(solution)/shard_map/while
  436.5 9.4 %copy-start.5 = (bf16[4,6,128,2,128,1]{2,4,1,5,3,0:T(8,128)(2,1)S(1)}, bf16[4,6,128,2,128,1]{2,4,1,5,3,0:T(8,128)(2,1)}, u32[]{:S(2)}) copy-start(bf16[4,6,128,2,128,1]{2,4,1,5,3,0:T(8,128)(2,1)} %copy-done.4) | copy-start | bytes 4718596 | tf_op jit(solution)/shard_map/while
  449.1 12.0 %copy-start.15 = (s32[4,4]{1,0:T(4,128)}, s32[4,4]{1,0:T(4,128)S(1)}, u32[]{:S(2)}) copy-start(s32[4,4]{1,0:T(4,128)S(1)} %get-tuple-element.388) | copy-start | bytes 196 | tf_op jit(solution)/shard_map/while
  449.1 12.0 %copy-start.13 = (s32[4,4,6]{2,1,0:T(4,128)}, s32[4,4,6]{2,1,0:T(4,128)S(1)}, u32[]{:S(2)}) copy-start(s32[4,4,6]{2,1,0:T(4,128)S(1)} %get-tuple-element.387) | copy-start | bytes 1156 | tf_op jit(solution)/shard_map/while
  449.2 12.1 %copy-start.17 = (pred[4,4,6]{2,1,0:T(4,128)(4,1)}, pred[4,4,6]{2,1,0:T(4,128)(4,1)S(1)}, u32[]{:S(2)}) copy-start(pred[4,4,6]{2,1,0:T(4,128)(4,1)S(1)} %get-tuple-element.386) | copy-start | bytes 292 | tf_op jit(solution)/shard_map/while
  449.9 6.6 copy-start.11
  464.0 5.7 copy-start.6
  493.0 11.5 %slice-start = ((s8[12582912]{0:T(1024)(128)(4,1)}), s8[4194304]{0:T(1024)(128)(4,1)S(1)}, s32[]{:S(2)}) async-start(s8[12582912]{0:T(1024)(128)(4,1)} %bitcast.218), calls=%async_computation.9 | async-start | bytes 8388608 | tf_op jit(solution)/shard_map/while
  493.0 11.5 %slice-start.1 = ((s8[12582912]{0:T(1024)(128)(4,1)}), s8[4194304]{0:T(1024)(128)(4,1)S(1)}, s32[]{:S(2)}) async-start(s8[12582912]{0:T(1024)(128)(4,1)} %bitcast.218), calls=%async_computation.10 | async-start | bytes 8388608 | tf_op jit(solution)/shard_map/while
  493.0 12.9 %slice-start.2 = ((s8[12582912]{0:T(1024)(128)(4,1)}), s8[4194304]{0:T(1024)(128)(4,1)S(1)}, s32[]{:S(2)}) async-start(s8[12582912]{0:T(1024)(128)(4,1)} %bitcast.218), calls=%async_computation.11 | async-start | bytes 8388608 | tf_op jit(solution)/shard_map/while
  506.0 10.3 %copy-start.3 = (bf16[1,4,128,2,4,128]{5,4,3,2,1,0:T(4,128)(2,1)S(1)}, bf16[1,4,128,2,4,128]{5,4,3,2,1,0:T(4,128)(2,1)}, u32[]{:S(2)}) copy-start(bf16[1,4,128,2,4,128]{5,4,3,2,1,0:T(4,128)(2,1)} %copy-done.2) | copy-start | bytes 3145732 | tf_op jit(solution)/shard_map/while
  521.9 15.1 %slice-start.3 = ((s8[6291456]{0:T(1024)(128)(4,1)}), s8[2097152]{0:T(1024)(128)(4,1)S(1)}, s32[]{:S(2)}) async-start(s8[6291456]{0:T(1024)(128)(4,1)} %bitcast.220), calls=%async_computation.12 | async-start | bytes 4194304 | tf_op jit(solution)/shard_map/while
  527.6 9.4 %slice-start.4 = ((s8[6291456]{0:T(1024)(128)(4,1)}), s8[4194304]{0:T(1024)(128)(4,1)S(1)}, s32[]{:S(2)}) async-start(s8[6291456]{0:T(1024)(128)(4,1)} %bitcast.220), calls=%async_computation.13 | async-start | bytes 8388608 | tf_op jit(solution)/shard_map/while
  527.6 9.4 %copy-start.5 = (bf16[4,6,128,2,128,1]{2,4,1,5,3,0:T(8,128)(2,1)S(1)}, bf16[4,6,128,2,128,1]{2,4,1,5,3,0:T(8,128)(2,1)}, u32[]{:S(2)}) copy-start(bf16[4,6,128,2,128,1]{2,4,1,5,3,0:T(8,128)(2,1)} %copy-done.4) | copy-start | bytes 4718596 | tf_op jit(solution)/shard_map/while
  553.8 132.4 %reduce-scatter.5.cloned.1.call-start = ((), (), s32[]{:S(2)}) async-start(), calls=%async_computation.6 | async-start | bytes 589824 | tf_op jit(solution)/shard_map/reduce_scatter | solution.py:194
  555.9 194.8 %reduce-scatter.3.cloned.1.call-start = ((), (), s32[]{:S(2)}) async-start(), calls=%async_computation.5 | async-start | bytes 589824 | tf_op jit(solution)/shard_map/reduce_scatter | solution.py:191
  561.5 190.1 %collective-permute-start.4 = (bf16[16,128,256]{2,1,0:T(8,128)(2,1)}, bf16[16,128,256]{2,1,0:T(8,128)(2,1)}, u32[]{:S(2)}, u32[]{:S(2)}) collective-permute-start(bf16[16,128,256]{2,1,0:T(8,128)(2,1)} %bitcast.69), channel_id=1, source_target_pairs={{4,0},{8,4},{12,8},{16,12},{20,16},{24,20},{28,24},{5,1},{9,5},{13... | collective-permute-start | bytes 3145736 | tf_op jit(solution)/shard_map/ppermute | solution.py:19
  563.0 188.6 %collective-permute-start.5 = (bf16[16,128,256]{2,1,0:T(8,128)(2,1)S(1)}, bf16[16,128,256]{2,1,0:T(8,128)(2,1)}, u32[]{:S(2)}, u32[]{:S(2)}) collective-permute-start(bf16[16,128,256]{2,1,0:T(8,128)(2,1)S(1)} %bitcast.251), channel_id=1, source_target_pairs={{8,0},{12,4},{16,8},{20,12},{24,16},{28,20},{9,1},{13,5},{17,9},{2... | collective-permute-start | bytes 3145736 | tf_op jit(solution)/shard_map/ppermute | solution.py:19
  565.5 186.1 %collective-permute-start.6 = (bf16[16,128,256]{2,1,0:T(8,128)(2,1)}, bf16[16,128,256]{2,1,0:T(8,128)(2,1)}, u32[]{:S(2)}, u32[]{:S(2)}) collective-permute-start(bf16[16,128,256]{2,1,0:T(8,128)(2,1)} %bitcast.75), channel_id=1, source_target_pairs={{4,0},{8,4},{12,8},{16,12},{20,16},{24,20},{28,24},{5,1},{9,5},{13... | collective-permute-start | bytes 3145736 | tf_op jit(solution)/shard_map/ppermute | solution.py:19
  568.0 183.6 %collective-permute-start.7 = (bf16[16,128,256]{2,1,0:T(8,128)(2,1)}, bf16[16,128,256]{2,1,0:T(8,128)(2,1)}, u32[]{:S(2)}, u32[]{:S(2)}) collective-permute-start(bf16[16,128,256]{2,1,0:T(8,128)(2,1)} %bitcast.77), channel_id=1, source_target_pairs={{8,0},{12,4},{16,8},{20,12},{24,16},{28,20},{9,1},{13,5},{17,9},{2... | collective-permute-start | bytes 3145736 | tf_op jit(solution)/shard_map/ppermute | solution.py:19
  773.7 18.0 %all-to-all-start.2 = ((bf16[4,512,256]{2,1,0:T(8,128)(2,1)}), bf16[4,512,256]{2,1,0:T(8,128)(2,1)S(1)}, u32[]{:S(2)}, u32[]{:S(2)}) async-start(bf16[4,512,256]{2,1,0:T(8,128)(2,1)} %bitcast.23), calls=%async_computation.4 | async-start | bytes 2097152 | tf_op jit(solution)/shard_map/all_to_all | solution.py:223
  791.6 53.1 %all-to-all-start = ((bf16[4,512,1024]{2,1,0:T(8,128)(2,1)}), bf16[4,512,1024]{2,1,0:T(8,128)(2,1)}, u32[]{:S(2)}, u32[]{:S(2)}) async-start(bf16[4,512,1024]{2,1,0:T(8,128)(2,1)} %all_to_all.38), calls=%async_computation | async-start | bytes 8388608 | tf_op jit(solution)/shard_map/all_to_all | solution.py:221
  (35 other events, 116.7 us)
Sparse Core Ops, SparseCore 0:
  25.8 78.5 all-reduce.6
  553.9 68.0 all-reduce.4
  625.4 60.8 reduce-scatter.4
  689.8 60.8 reduce-scatter.2
where the time goes:
time: 867 us; the launch traced here: 864 us
  local copies, waits for them, and re-layouts  230 us (27%)
  waiting for transfers between devices  223 us (26%)
  matrix products  152 us (18%)
  blocking collectives  131 us (15%)
  other arithmetic  81.3 us (9%)
  starting transfers between devices  29.1 us (3%)
  between operations  15.9 us (2%)
    all_gather x1, blocking collectives, shards(): lax.all_gather(item_keys, 'seq', axis=0, tiled=True)  82.5 us
    reduce_scatter x1, waiting for transfers between devices, shards(): lax.psum_scatter(table_keys.astype(jnp.bfloat16), 'seq', scatter_dimensio...  63.6 us
    reduce_scatter x1, waiting for transfers between devices, shards(): lax.psum_scatter(table_values.astype(jnp.bfloat16), 'seq', scatter_dimens...  62.5 us
    psum x1, waiting for transfers between devices, shards(): lax.psum(acc_keys[far_base + vert_total:far_base + vert_total + 1].astype...  46 us
    dot_general x4, matrix products, group_step(): jnp.einsum('bqkgd,bsckd->bkgqsc', grad_rows, slot_values, preferred_eleme...  45.7 us
    all_to_all x1, waiting for transfers between devices, shards(): lax.all_to_all(grad_query, 'head', split_axis=0, concat_axis=1, tiled=True)  44.5 us
    dot_general x4, matrix products, group_step(): jnp.dot(onehot, key_terms, precision=lax.Precision.HIGHEST)  36.3 us
    all_gather x1, blocking collectives, shards(): lax.all_gather(item_values, 'seq', axis=0, tiled=True)  31.2 us
  transfers between devices with their start and end apart: 14, of which 5 were waited for; matrix products, arithmetic and copies ran while one was open for 7% of the time, Pallas kernels for 0%

commit v1 on v0

v1 whole, which is shorter than its diff:
```python
import functools
import math

import jax
import jax.numpy as jnp
from jax import lax
from jax.experimental import pallas as pl
from jax.experimental.pallas import tpu as pltpu
from jax.sharding import PartitionSpec as P

HD = 128
BLK = 128
VERT_DEV = 1
FAR = 1e30


def attention_kernel(
    dims, place, vertical, columns, offsets, q_ref, do_ref, kv_own, kv_back, kv_even, kv_odd, kv_far,
    dq_ref, own_ref, prev_ref, back_ref, far_ref, pool_k, pool_v, acc_k, acc_v, sems,
):
    local_blocks, group, vert_total = dims
    step = pl.program_id(0)
    seq_index = place[0]
    rows = local_blocks * BLK
    far_rows = (vert_total + 1) * BLK
    total_rows = 3 * rows + far_rows
    scale = 1.0 / math.sqrt(HD)

    @pl.when(step == 0)
    def _():
        def copies(prev):
            made = []
            for side, pool in enumerate((pool_k, pool_v)):
                for number, (source, start, size) in enumerate(
                    ((kv_own, 0, rows), (prev, rows, rows), (kv_back, 2 * rows, rows), (kv_far, 3 * rows, far_rows))
                ):
                    made.append(
                        pltpu.make_async_copy(
                            source.at[side], pool.at[pl.ds(start, size)], sems.at[side * 4 + number]
                        )
                    )
            return made

        odd = lax.rem(seq_index, 2) == 1

        @pl.when(odd)
        def _():
            for copy in copies(kv_even):
                copy.start()

        @pl.when(jnp.logical_not(odd))
        def _():
            for copy in copies(kv_odd):
                copy.start()

        acc_k[...] = jnp.zeros_like(acc_k)
        acc_v[...] = jnp.zeros_like(acc_v)
        for copy in copies(kv_even):
            copy.wait()

    block = seq_index * local_blocks + step

    def column_block(column):
        return column // VERT_DEV * local_blocks + vertical[column]

    def near(offset):
        at = step - offset
        return jnp.where(at >= 0, at, jnp.where(at >= -local_blocks, at + 2 * local_blocks, at + 4 * local_blocks))

    first, second = offsets[step, 0], offsets[step, 1]
    left, right = columns[step, 0], columns[step, 1]
    b2, b3 = block - first, block - second
    b4, b5 = column_block(left), column_block(right)
    slots = [3 * local_blocks + vert_total, step, near(first), near(second), 3 * local_blocks + left, 3 * local_blocks + right]
    live = [
        block > 0,
        None,
        b2 > 0,
        (b3 > 0) & (b3 != b2),
        (b4 > 0) & (b4 < block) & (b4 != b2) & (b4 != b3),
        (b5 > 0) & (b5 < block) & (b5 != b2) & (b5 != b3) & (b5 != b4),
    ]
    spots = [pl.ds(pl.multiple_of(slot * BLK, BLK), BLK) for slot in slots]
    queries = jnp.concatenate([q_ref[:, g * HD : (g + 1) * HD] for g in range(group)], axis=0)
    grads = jnp.concatenate([do_ref[:, g * HD : (g + 1) * HD] for g in range(group)], axis=0)
    width = group * BLK
    keys = [pool_k[spot, :] for spot in spots]
    values = [pool_v[spot, :] for spot in spots]
    contract_last = (((1,), (1,)), ((), ()))
    contract_first = (((0,), (0,)), ((), ()))
    key_at = lax.broadcasted_iota(jnp.int32, (BLK, width), 0)
    query_at = lax.broadcasted_iota(jnp.int32, (BLK, width), 1) % BLK
    seen = key_at <= query_at
    turn = scale * math.log2(math.e)
    scores, tops = [], []
    for number in range(6):
        part = lax.dot_general(keys[number], queries, contract_last, preferred_element_type=jnp.float32)
        part = part * turn
        if number == 1:
            part = jnp.where(seen, part, -FAR)
        scores.append(part)
        top = jnp.max(part, axis=0, keepdims=True)
        if number != 1:
            top = jnp.where(live[number], top, -FAR)
        tops.append(top)
    top = functools.reduce(jnp.maximum, tops)
    weights, products = [], []
    total = jnp.zeros((1, width), jnp.float32)
    delta = jnp.zeros((1, width), jnp.float32)
    for number in range(6):
        base = top if number == 1 else jnp.where(live[number], top, FAR)
        weight = jnp.exp2(scores[number] - base)
        product = lax.dot_general(values[number], grads, contract_last, preferred_element_type=jnp.float32)
        total = total + jnp.sum(weight, axis=0, keepdims=True)
        delta = delta + jnp.sum(weight * product, axis=0, keepdims=True)
        weights.append(weight)
        products.append(product)
    inverse = 1.0 / total
    delta = delta * inverse
    dq = jnp.zeros((width, HD), jnp.float32)
    for number in range(6):
        prob = weights[number] * inverse
        dscore = (prob * (products[number] - delta)).astype(jnp.bfloat16)
        prob = prob.astype(jnp.bfloat16)
        acc_v[spots[number], :] += jnp.dot(prob, grads, preferred_element_type=jnp.float32)
        acc_k[spots[number], :] += jnp.dot(dscore, queries, preferred_element_type=jnp.float32)
        dq = dq + lax.dot_general(dscore, keys[number], contract_first, preferred_element_type=jnp.float32)
    dq = (dq * scale).astype(dq_ref.dtype)
    for g in range(group):
        dq_ref[:, g * HD : (g + 1) * HD] = dq[g * BLK : (g + 1) * BLK]

    @pl.when(step == local_blocks - 1)
    def _():
        for side, (acc, factor) in enumerate(((acc_k, scale), (acc_v, 1.0))):
            own_ref[side] = acc[:rows, :] * factor
            prev_ref[side] = (acc[rows : 2 * rows, :] * factor).astype(prev_ref.dtype)
            back_ref[side] = (acc[2 * rows : 3 * rows, :] * factor).astype(back_ref.dtype)
            far_ref[side] = (acc[3 * rows :, :] * factor).astype(far_ref.dtype)


def attention(head, kv_local, place, vertical, columns, offsets, queries, grad_out, kv_own, kv_back, kv_even, kv_odd, kv_far):
    seq_len = queries.shape[0]
    local_blocks = seq_len // BLK
    width = queries.shape[1] // kv_local
    group = width // HD
    vert_total = vertical.shape[0]
    far_rows = (vert_total + 1) * BLK
    total_rows = 3 * seq_len + far_rows
    anywhere = pl.BlockSpec(memory_space=pl.ANY)
    by_block = pl.BlockSpec((BLK, width), lambda i, *_: (i, head))

    def whole(*shape):
        return pl.BlockSpec(shape, lambda i, *_: (0,) * len(shape))

    near_shape = (2, seq_len, HD)
    far_shape = (2, far_rows, HD)
    flops = 2 * 5 * seq_len * group * 6 * BLK * HD
    return pl.pallas_call(
        functools.partial(attention_kernel, (local_blocks, group, vert_total)),
        grid_spec=pltpu.PrefetchScalarGridSpec(
            num_scalar_prefetch=4,
            grid=(local_blocks,),
            in_specs=[by_block, by_block] + [anywhere] * 5,
            out_specs=[
                pl.BlockSpec((BLK, width), lambda i, *_: (i, 0)),
                whole(*near_shape), whole(*near_shape), whole(*near_shape), whole(*far_shape),
            ],
            scratch_shapes=[
                pltpu.VMEM((total_rows, HD), jnp.bfloat16),
                pltpu.VMEM((total_rows, HD), jnp.bfloat16),
                pltpu.VMEM((total_rows, HD), jnp.float32),
                pltpu.VMEM((total_rows, HD), jnp.float32),
                pltpu.SemaphoreType.DMA((8,)),
            ],
        ),
        out_shape=[
            jax.ShapeDtypeStruct((seq_len, width), jnp.bfloat16),
            jax.ShapeDtypeStruct(near_shape, jnp.float32),
            jax.ShapeDtypeStruct(near_shape, jnp.bfloat16),
            jax.ShapeDtypeStruct(near_shape, jnp.bfloat16),
            jax.ShapeDtypeStruct(far_shape, jnp.bfloat16),
        ],
        compiler_params=pltpu.CompilerParams(vmem_limit_bytes=50 * 1024 * 1024),
        cost_estimate=pl.CostEstimate(flops=flops, bytes_accessed=20 * 1024 * 1024, transcendentals=seq_len * group * 6 * BLK),
        name="attention",
    )(place, vertical, columns, offsets, queries, grad_out, kv_own, kv_back, kv_even, kv_odd, kv_far)


def assemble_kernel(heads, kv_local, place, *refs):
    count = heads * kv_local
    outs = refs[3 * count :]
    for number, out in enumerate(outs):
        for at in range(count):
            piece = refs[number * count + at]
            width = piece.shape[1]
            source = place[1] ^ (at // kv_local)
            start = pl.multiple_of((source * kv_local + at % kv_local) * width, width)
            out[:, pl.ds(start, width)] = piece[...]


def assemble(place, heads, query_pieces, key_pieces, value_pieces):
    groups = (query_pieces, key_pieces, value_pieces)
    count = len(query_pieces)
    rows = query_pieces[0].shape[0]
    tile = min(rows, 128)

    def spec(width):
        return pl.BlockSpec((tile, width), lambda i, *_: (i, 0))

    return pl.pallas_call(
        functools.partial(assemble_kernel, heads, count // heads),
        grid_spec=pltpu.PrefetchScalarGridSpec(
            num_scalar_prefetch=1,
            grid=(rows // tile,),
            in_specs=[spec(piece.shape[1]) for group in groups for piece in group],
            out_specs=[spec(group[0].shape[1] * count) for group in groups],
        ),
        out_shape=[jax.ShapeDtypeStruct((rows, group[0].shape[1] * count), group[0].dtype) for group in groups],
        name="assemble",
    )(place, *(piece for group in groups for piece in group))


def shards(queries, keys, values, grad_out, vertical, columns, offsets):
    seq_len = queries.shape[0]
    seq_size = lax.axis_size("seq")
    head_size = lax.axis_size("head")
    kv_local = keys.shape[1] // HD
    seq_index = lax.axis_index("seq")
    head_index = lax.axis_index("head")
    place = jnp.stack([seq_index, head_index]).astype(jnp.int32)
    odd = seq_index % 2 == 1
    evens = range(0, seq_size, 2)

    def along(array, pairs):
        return lax.ppermute(array, "seq", pairs)

    forward = [(i, i + 2) for i in range(seq_size - 2)]
    backward = [(i + 2, i) for i in range(seq_size - 2)]
    exchange = [(i, i ^ 1) for i in range(seq_size)]
    even_to_odd = [(i, i + 1) for i in evens]
    odd_to_even = [(i + 1, i) for i in evens]
    steps = int(math.log2(seq_size))
    own_vertical = lax.dynamic_slice_in_dim(vertical, seq_index * VERT_DEV, VERT_DEV)

    def spread(kv):
        mine = lax.dynamic_slice_in_dim(kv, own_vertical[0] * BLK, BLK, axis=1)
        sink = kv[:, :BLK]
        held = mine
        for level in range(steps):
            hop = 1 << level
            got = along(jnp.concatenate([held, sink], axis=1), [(i, i ^ hop) for i in range(seq_size)])
            got_held, got_sink = got[:, :-BLK], got[:, -BLK:]
            upper = (seq_index & hop) != 0
            held = jnp.where(upper, jnp.concatenate([got_held, held], axis=1), jnp.concatenate([held, got_held], axis=1))
            sink = jnp.where(seq_index < hop, sink, got_sink)
        return jnp.concatenate([held, sink], axis=1)

    def collect(far):
        held, sink = far[:, :-BLK].astype(jnp.float32), far[:, -BLK:].astype(jnp.float32)
        for level in reversed(range(steps)):
            hop = 1 << level
            size = held.shape[1] // 2
            upper = (seq_index & hop) != 0
            low, high = held[:, :size], held[:, size:]
            sent = jnp.concatenate([jnp.where(upper, low, high), sink], axis=1).astype(jnp.bfloat16)
            got = along(sent, [(i, i ^ hop) for i in range(seq_size)]).astype(jnp.float32)
            held = jnp.where(upper, high, low) + got[:, :size]
            sink = sink + got[:, size:]
        return held, sink

    query_pieces, key_pieces, value_pieces = {}, {}, {}

    def to_tokens(array, k, axis):
        size = array.shape[axis] // head_size
        piece = lax.dynamic_slice_in_dim(array, (head_index ^ k) * size, size, axis=axis)
        if k == 0:
            return piece
        return lax.ppermute(piece, "head", [(i, i ^ k) for i in range(head_size)])

    for head in range(kv_local):
        span = slice(head * HD, (head + 1) * HD)
        kv = jnp.stack([keys[:, span], values[:, span]])
        kv_even = along(kv, even_to_odd)
        kv_back = along(kv, forward)
        kv_odd = along(kv_back, odd_to_even)
        kv_far = spread(kv)
        dq, own, prev, back, far = attention(
            head, kv_local, place, vertical, columns, offsets, queries, grad_out, kv, kv_back, kv_even, kv_odd, kv_far
        )
        for k in range(head_size):
            query_pieces[k, head] = to_tokens(dq, k, 0)
        side = along(prev, exchange)
        onward = jnp.where(odd, back.astype(jnp.float32) + side.astype(jnp.float32), back.astype(jnp.float32))
        returned = along(onward.astype(jnp.bfloat16), backward)
        mine, sink = collect(far)
        own = own + returned.astype(jnp.float32) + jnp.where(odd, 0.0, side.astype(jnp.float32))
        at = own_vertical[0] * BLK
        own = lax.dynamic_update_slice_in_dim(own, lax.dynamic_slice_in_dim(own, at, BLK, axis=1) + mine, at, axis=1)
        own = own.at[:, :BLK].add(jnp.where(seq_index == 0, sink, 0.0))
        own = own.astype(jnp.bfloat16)
        for k in range(head_size):
            piece = to_tokens(own, k, 1)
            key_pieces[k, head] = piece[0]
            value_pieces[k, head] = piece[1]
    order = [(k, head) for k in range(head_size) for head in range(kv_local)]
    return tuple(
        assemble(
            place, head_size, [query_pieces[o] for o in order], [key_pieces[o] for o in order], [value_pieces[o] for o in order]
        )
    )


def solution(mesh):
    return jax.shard_map(
        shards,
        mesh=mesh,
        in_specs=(
            P("seq", "head"),
            P("seq", "head"),
            P("seq", "head"),
            P("seq", "head"),
            P(),
            P("seq", None),
            P("seq", None),
        ),
        out_specs=(P(("seq", "head"), None), P(("seq", "head"), None), P(("seq", "head"), None)),
        check_vma=False,
    )
```

time: 867 us -> 305 us (0.35)
  local copies, waits for them, and re-layouts: 230 us -> 16.3 us
  matrix products: 152 us -> 0 us
  blocking collectives: 131 us -> 0 us
  other arithmetic: 81.3 us -> 7.87 us
  Pallas kernels: 0 us -> 71.2 us
  waiting for transfers between devices: 223 us -> 164 us
  between operations: 15.9 us -> 2.2 us
  starting transfers between devices: 29.1 us -> 42.6 us
    ppermute x8 -> x34, waiting for transfers between devices: 0.02 us -> 164 us  [the longest x22 116 us: along(): return lax.ppermute(array, 'seq', pairs)]
    dot_general x28 -> x0, matrix products: 152 us -> none  [the longest x4 45.7 us: group_step(): jnp.einsum('bqkgd,bsckd->bkgqsc', grad_rows, slot_values, preferred_eleme...]
    reduce_scatter x2 -> x0, waiting for transfers between devices: 126 us -> none  [the longest x1 63.6 us: shards(): lax.psum_scatter(table_keys.astype(jnp.bfloat16), 'seq', scatter_dimensio...]
    all_gather x2 -> x0, blocking collectives: 114 us -> none  [the longest x1 82.5 us: shards(): lax.all_gather(item_keys, 'seq', axis=0, tiled=True)]
    pallas_call x0 -> x3, Pallas kernels: none -> 71.2 us  [the longest x2 64.6 us: attention(): pl.pallas_call(functools.partial(attention_kernel, (local_blocks, group,...]
    reshape x22 -> x0, local copies, waits for them, and re-layouts: 71 us -> none  [the longest x4 22.9 us: group_step(): key_terms = jnp.einsum('bkgqsc,bqkgd->bsckd', dscore, query_rows, preferr...]
    all_to_all x2 -> x0, waiting for transfers between devices: 51.2 us -> none  [the longest x1 44.5 us: shards(): lax.all_to_all(grad_query, 'head', split_axis=0, concat_axis=1, tiled=True)]
    psum x2 -> x0, waiting for transfers between devices: 46 us -> none  [the longest x1 46 us: shards(): lax.psum(acc_keys[far_base + vert_total:far_base + vert_total + 1].astype...]
  transfers between devices with their start and end apart: 14 -> 34, of which waited for: 5 -> 18; matrix products, arithmetic and copies ran while one was open for 7% -> 6% of each run, Pallas kernels for 0% -> 21%
where the time goes in v1:
time: 305 us; the launch traced here: 304 us
  waiting for transfers between devices  164 us (54%)
  Pallas kernels  71.2 us (23%)
  starting transfers between devices  42.6 us (14%)
  local copies, waits for them, and re-layouts  16.3 us (5%)
  other arithmetic  7.87 us (3%)
    ppermute x22, waiting for transfers between devices, along(): return lax.ppermute(array, 'seq', pairs)  116 us
    pallas_call x2, Pallas kernels, attention(): pl.pallas_call(functools.partial(attention_kernel, (local_blocks, group,...  64.6 us
    ppermute x12, waiting for transfers between devices, to_tokens(): return lax.ppermute(piece, 'head', [(i, i ^ k) for i in range(head_size)])  47.9 us
    ppermute x22, starting transfers between devices, along(): return lax.ppermute(array, 'seq', pairs)  34.7 us
    ppermute x12, starting transfers between devices, to_tokens(): return lax.ppermute(piece, 'head', [(i, i ^ k) for i in range(head_size)])  7.91 us
    pallas_call x1, Pallas kernels, assemble(): pl.pallas_call(functools.partial(assemble_kernel, heads, count // heads),...  6.6 us
  transfers between devices with their start and end apart: 34, of which 18 were waited for; matrix products, arithmetic and copies ran while one was open for 6% of the time, Pallas kernels for 21%

profile of v1, /device:TPU:0, one launch (start us, length us, event | category | flops | bytes accessed | tf_op | source)
XLA Modules:
  0.0 304.0 jit_solution(14932976775507172185)
XLA Ops:
  0.6 1.3 dynamic_slice.63
  2.6 1.3 slice_bitcast_fusion.1
  4.0 0.7 pad_maximum_fusion.15
  4.7 3.0 collective-permute-start.9
  7.8 4.5 %collective-permute-start.6 = (bf16[2,2048,128]{2,1,0:T(8,128)(2,1)S(1)}, bf16[2,2048,128]{2,1,0:T(8,128)(2,1)}, u32[]{:S(2)}, u32[]{:S(2)}) collective-permute-start(bf16[2,2048,128]{2,1,0:T(8,128)(2,1)S(1)} %pad_maximum_fusion.1.kv_own), channel_id=1, source_target_pairs={{0,8},{4,12},{8,16},{12,20},{16,24},{20,28},{1,9},{5,13},{9,17},{1... | collective-permute-start | bytes 3145736 | tf_op jit(solution)/shard_map/ppermute | solution.py:235
  12.3 3.4 %collective-permute-start.7 = (bf16[2,2048,128]{2,1,0:T(8,128)(2,1)S(1)}, bf16[2,2048,128]{2,1,0:T(8,128)(2,1)}, u32[]{:S(2)}, u32[]{:S(2)}) collective-permute-start(bf16[2,2048,128]{2,1,0:T(8,128)(2,1)S(1)} %pad_maximum_fusion.1.kv_own), channel_id=1, source_target_pairs={{0,4},{8,12},{16,20},{24,28},{1,5},{9,13},{17,21},{25,29},{2,6},{1... | collective-permute-start | bytes 3145736 | tf_op jit(solution)/shard_map/ppermute | solution.py:235
  16.5 22.8 %collective-permute-done.3 = bf16[2,256,128]{2,1,0:T(8,128)(2,1)S(1)} collective-permute-done((bf16[2,256,128]{2,1,0:T(8,128)(2,1)S(1)}, bf16[2,256,128]{2,1,0:T(8,128)(2,1)S(1)}, u32[]{:S(2)}, u32[]{:S(2)}) %collective-permute-start.3) | collective-permute-done | bytes 131104 | tf_op jit(solution)/shard_map/ppermute | solution.py:235
  40.2 1.1 collective-permute-start.11
  41.3 7.0 %collective-permute-done.4 = bf16[2,384,128]{2,1,0:T(8,128)(2,1)S(1)} collective-permute-done((bf16[2,384,128]{2,1,0:T(8,128)(2,1)S(1)}, bf16[2,384,128]{2,1,0:T(8,128)(2,1)S(1)}, u32[]{:S(2)}, u32[]{:S(2)}) %collective-permute-start.4) | collective-permute-done | bytes 196640 | tf_op jit(solution)/shard_map/ppermute | solution.py:235
  48.5 0.7 pad_maximum_fusion.4
  49.8 1.1 pad_maximum_fusion.kv_own
  50.9 2.5 collective-permute-start
  53.7 11.5 %collective-permute-done.11 = bf16[2,640,128]{2,1,0:T(8,128)(2,1)} collective-permute-done((bf16[2,640,128]{2,1,0:T(8,128)(2,1)S(1)}, bf16[2,640,128]{2,1,0:T(8,128)(2,1)}, u32[]{:S(2)}, u32[]{:S(2)}) %collective-permute-start.11) | collective-permute-done | bytes 327712 | tf_op jit(solution)/shard_map/ppermute | solution.py:235
  65.1 4.5 %collective-permute-start.1 = (bf16[2,2048,128]{2,1,0:T(8,128)(2,1)}, bf16[2,2048,128]{2,1,0:T(8,128)(2,1)S(1)}, u32[]{:S(2)}, u32[]{:S(2)}) collective-permute-start(bf16[2,2048,128]{2,1,0:T(8,128)(2,1)} %pad_maximum_fusion.kv_own), channel_id=1, source_target_pairs={{0,4},{8,12},{16,20},{24,28},{1,5},{9,13},{17,21},{25,29},{2,6},{1... | collective-permute-start | bytes 3145736 | tf_op jit(solution)/shard_map/ppermute | solution.py:235
  69.7 1.0 slice.312
  70.7 1.0 slice.304
  71.8 1.3 collective-permute-start.8
  73.2 0.9 slice_select_fusion
  74.1 0.9 slice_select_fusion.3
  75.0 4.3 %collective-permute-done.kv_back = bf16[2,2048,128]{2,1,0:T(8,128)(2,1)} collective-permute-done((bf16[2,2048,128]{2,1,0:T(8,128)(2,1)}, bf16[2,2048,128]{2,1,0:T(8,128)(2,1)}, u32[]{:S(2)}, u32[]{:S(2)}) %collective-permute-start) | collective-permute-done | bytes 1048608 | tf_op jit(solution)/shard_map/ppermute | solution.py:235
  79.4 1.3 collective-permute-start.2
  80.7 19.3 %collective-permute-done.8.kv_odd = bf16[2,2048,128]{2,1,0:T(8,128)(2,1)S(1)} collective-permute-done((bf16[2,2048,128]{2,1,0:T(8,128)(2,1)}, bf16[2,2048,128]{2,1,0:T(8,128)(2,1)S(1)}, u32[]{:S(2)}, u32[]{:S(2)}) %collective-permute-start.8) | collective-permute-done | bytes 1048608 | tf_op jit(solution)/shard_map/ppermute | solution.py:235
  100.0 1.0 copy-done.18
  101.0 32.3 %attention.3 = (bf16[2048,512]{1,0:T(8,128)(2,1)}, f32[2,2048,128]{2,1,0:T(8,128)}, bf16[2,2048,128]{2,1,0:T(8,128)(2,1)S(1)}, bf16[2,2048,128]{2,1,0:T(8,128)(2,1)S(1)}, bf16[2,1152,128]{2,1,0:T(8,128)(2,1)S(1)}) custom-call(s32[2]{0:T(128)S(1)} %pad_add_fusion.place, s32[8]{0:T(128)S(1)} %copy-done.1, s32[16,2]{1,0:T(8,128)S(1)} %copy.10.columns, ...), custom_call_target="tpu_custom_call" | custom-call | flops 8053063680 | bytes 20971520 | tf_op jit(solution)/shard_map/attention/pallas_call | solution.py:158
  133.6 0.9 copy-done.16
  134.6 1.0 copy-done.17
  135.6 32.3 %attention.2 = (bf16[2048,512]{1,0:T(8,128)(2,1)}, f32[2,2048,128]{2,1,0:T(8,128)}, bf16[2,2048,128]{2,1,0:T(8,128)(2,1)S(1)}, bf16[2,2048,128]{2,1,0:T(8,128)(2,1)S(1)}, bf16[2,1152,128]{2,1,0:T(8,128)(2,1)S(1)}) custom-call(s32[2]{0:T(128)S(1)} %pad_add_fusion.place, s32[8]{0:T(128)S(1)} %copy-done.1, s32[16,2]{1,0:T(8,128)S(1)} %copy.10.columns, ...), custom_call_target="tpu_custom_call" | custom-call | flops 8053063680 | bytes 20971520 | tf_op jit(solution)/shard_map/attention/pallas_call | solution.py:158
  168.1 2.9 collective-permute-start.20
  171.0 2.0 collective-permute-start.18
  173.1 0.9 constant_dynamic-slice_fusion.6
  174.2 1.2 collective-permute-start.26
  175.4 6.3 %collective-permute-done.20 = bf16[2,640,128]{2,1,0:T(8,128)(2,1)S(1)} collective-permute-done((bf16[2,640,128]{2,1,0:T(8,128)(2,1)S(1)}, bf16[2,640,128]{2,1,0:T(8,128)(2,1)S(1)}, u32[]{:S(2)}, u32[]{:S(2)}) %collective-permute-start.20) | collective-permute-done | bytes 327712 | tf_op jit(solution)/shard_map/ppermute | solution.py:235
  182.0 1.9 collective-permute-done.26
  184.1 1.1 collective-permute-start.27
  185.2 2.6 collective-permute-done.21
  188.2 1.4 collective-permute-start.24
  189.7 0.9 collective-permute-start.22
  190.6 0.9 constant_dynamic-slice_fusion.7
  191.6 2.1 collective-permute-done.27
  193.7 1.4 collective-permute-done.22
  195.5 1.5 collective-permute-start.19
  196.9 19.4 %collective-permute-done.24 = bf16[2,2048,128]{2,1,0:T(8,128)(2,1)S(1)} collective-permute-done((bf16[2,2048,128]{2,1,0:T(8,128)(2,1)S(1)}, bf16[2,2048,128]{2,1,0:T(8,128)(2,1)S(1)}, u32[]{:S(2)}, u32[]{:S(2)}) %collective-permute-start.24) | collective-permute-done | bytes 1048608 | tf_op jit(solution)/shard_map/ppermute | solution.py:235
  217.1 1.5 collective-permute-start.31
  218.7 17.2 %collective-permute-done.19 = bf16[2,2048,128]{2,1,0:T(8,128)(2,1)S(1)} collective-permute-done((bf16[2,2048,128]{2,1,0:T(8,128)(2,1)S(1)}, bf16[2,2048,128]{2,1,0:T(8,128)(2,1)S(1)}, u32[]{:S(2)}, u32[]{:S(2)}) %collective-permute-start.19) | collective-permute-done | bytes 1048608 | tf_op jit(solution)/shard_map/ppermute | solution.py:235
  236.3 0.7 dynamic-slice_bitcast_fusion
  237.2 0.7 dynamic-slice_bitcast_fusion.1
  238.0 1.6 collective-permute-start.32
  240.1 0.7 slice_bitcast_fusion.4
  240.8 0.7 slice_bitcast_fusion.6
  241.6 1.5 collective-permute-start.15
  243.0 0.7 slice_bitcast_fusion.8
  244.1 2.0 collective-permute-done.32
  246.2 0.8 collective-permute-start.12
  247.0 5.8 %collective-permute-done.30 = bf16[2,512,128]{2,1,0:T(8,128)(2,1)S(1)} collective-permute-done((bf16[2,512,128]{2,1,0:T(8,128)(2,1)S(1)}, bf16[2,512,128]{2,1,0:T(8,128)(2,1)S(1)}, u32[]{:S(2)}, u32[]{:S(2)}) %collective-permute-start.30) | collective-permute-done | bytes 262176 | tf_op jit(solution)/shard_map/ppermute | solution.py:278
  252.8 1.5 collective-permute-start.14
  254.3 0.7 slice_bitcast_fusion.5
  255.0 0.7 slice_bitcast_fusion.7
  255.7 0.7 slice_bitcast_fusion.9
  256.4 7.6 %collective-permute-done.15.refs_5_ = bf16[512,512]{1,0:T(8,128)(2,1)S(1)} collective-permute-done((bf16[512,512]{1,0:T(8,128)(2,1)S(1)}, bf16[512,512]{1,0:T(8,128)(2,1)S(1)}, u32[]{:S(2)}, u32[]{:S(2)}) %collective-permute-start.15) | collective-permute-done | bytes 524320 | tf_op jit(solution)/shard_map/ppermute | solution.py:278
  264.1 10.2 %collective-permute-done.17.refs_7_ = bf16[512,512]{1,0:T(8,128)(2,1)S(1)} collective-permute-done((bf16[512,512]{1,0:T(8,128)(2,1)S(1)}, bf16[512,512]{1,0:T(8,128)(2,1)S(1)}, u32[]{:S(2)}, u32[]{:S(2)}) %collective-permute-start.17) | collective-permute-done | bytes 524320 | tf_op jit(solution)/shard_map/ppermute | solution.py:278
  274.3 12.3 %collective-permute-done.14.refs_4_ = bf16[512,512]{1,0:T(8,128)(2,1)S(1)} collective-permute-done((bf16[512,512]{1,0:T(8,128)(2,1)S(1)}, bf16[512,512]{1,0:T(8,128)(2,1)S(1)}, u32[]{:S(2)}, u32[]{:S(2)}) %collective-permute-start.14) | collective-permute-done | bytes 524320 | tf_op jit(solution)/shard_map/ppermute | solution.py:278
  286.5 9.9 %collective-permute-done.16.refs_6_ = bf16[512,512]{1,0:T(8,128)(2,1)S(1)} collective-permute-done((bf16[512,512]{1,0:T(8,128)(2,1)S(1)}, bf16[512,512]{1,0:T(8,128)(2,1)S(1)}, u32[]{:S(2)}, u32[]{:S(2)}) %collective-permute-start.16) | collective-permute-done | bytes 524320 | tf_op jit(solution)/shard_map/ppermute | solution.py:278
  296.5 0.8 copy-done.13
  297.3 6.6 %assemble.1 = (bf16[512,4096]{1,0:T(8,128)(2,1)}, bf16[512,1024]{1,0:T(8,128)(2,1)}, bf16[512,1024]{1,0:T(8,128)(2,1)}) custom-call(s32[2]{0:T(128)} %copy-done, bf16[512,512]{1,0:T(8,128)(2,1)} %get-tuple-element.54.refs_0_, bf16[512,512]{1,0:T(8,128)(2,1)} %get-tuple-element.50.refs_1_, bf16[512,512]{1,0:T(8,128)(2,1)} %copy-done.11, ...), custom_call_target="tpu_custom_call" | custom-call | tf_op jit(solution)/shard_map/assemble/pallas_call | solution.py:210
  (130 shorter events, 7.4 us)
Async XLA Ops:
  0.6 3.3 %copy-start.6 = (bf16[2048,256]{1,0:T(8,128)(2,1)S(1)}, bf16[2048,256]{1,0:T(8,128)(2,1)}, u32[]{:S(2)}) copy-start(bf16[2048,256]{1,0:T(8,128)(2,1)} %param.13) | copy-start | bytes 3145732
  4.7 11.1 %collective-permute-start.9 = (bf16[2,256,128]{2,1,0:T(8,128)(2,1)}, bf16[2,256,128]{2,1,0:T(8,128)(2,1)S(1)}, u32[]{:S(2)}, u32[]{:S(2)}) collective-permute-start(bf16[2,256,128]{2,1,0:T(8,128)(2,1)} %pad_maximum_fusion.15), channel_id=1, source_target_pairs={{0,4},{4,0},{8,12},{12,8},{16,20},{20,16},{24,28},{28,24},{1,5},{5... | collective-permute-start | bytes 393224 | tf_op jit(solution)/shard_map/ppermute | solution.py:235
  7.8 40.7 %copy-start.7 = (bf16[2,2048,128]{2,1,0:T(8,128)(2,1)}, bf16[2,2048,128]{2,1,0:T(8,128)(2,1)S(1)}, u32[]{:S(2)}) copy-start(bf16[2,2048,128]{2,1,0:T(8,128)(2,1)S(1)} %pad_maximum_fusion.1.kv_own) | copy-start | bytes 3145732
  7.8 64.0 %collective-permute-start.6 = (bf16[2,2048,128]{2,1,0:T(8,128)(2,1)S(1)}, bf16[2,2048,128]{2,1,0:T(8,128)(2,1)}, u32[]{:S(2)}, u32[]{:S(2)}) collective-permute-start(bf16[2,2048,128]{2,1,0:T(8,128)(2,1)S(1)} %pad_maximum_fusion.1.kv_own), channel_id=1, source_target_pairs={{0,8},{4,12},{8,16},{12,20},{16,24},{20,28},{1,9},{5,13},{9,17},{1... | collective-permute-start | bytes 3145736 | tf_op jit(solution)/shard_map/ppermute | solution.py:235
  12.3 68.4 %collective-permute-start.7 = (bf16[2,2048,128]{2,1,0:T(8,128)(2,1)S(1)}, bf16[2,2048,128]{2,1,0:T(8,128)(2,1)}, u32[]{:S(2)}, u32[]{:S(2)}) collective-permute-start(bf16[2,2048,128]{2,1,0:T(8,128)(2,1)S(1)} %pad_maximum_fusion.1.kv_own), channel_id=1, source_target_pairs={{0,4},{8,12},{16,20},{24,28},{1,5},{9,13},{17,21},{25,29},{2,6},{1... | collective-permute-start | bytes 3145736 | tf_op jit(solution)/shard_map/ppermute | solution.py:235
  15.7 23.6 %collective-permute-start.3 = (bf16[2,256,128]{2,1,0:T(8,128)(2,1)S(1)}, bf16[2,256,128]{2,1,0:T(8,128)(2,1)S(1)}, u32[]{:S(2)}, u32[]{:S(2)}) collective-permute-start(bf16[2,256,128]{2,1,0:T(8,128)(2,1)S(1)} %pad_maximum_fusion.13), channel_id=1, source_target_pairs={{0,4},{4,0},{8,12},{12,8},{16,20},{20,16},{24,28},{28,24},{1,5},{5... | collective-permute-start | bytes 393224 | tf_op jit(solution)/shard_map/ppermute | solution.py:235
  15.9 24.2 %collective-permute-start.10 = (bf16[2,384,128]{2,1,0:T(8,128)(2,1)S(1)}, bf16[2,384,128]{2,1,0:T(8,128)(2,1)S(1)}, u32[]{:S(2)}, u32[]{:S(2)}) collective-permute-start(bf16[2,384,128]{2,1,0:T(8,128)(2,1)S(1)} %pad_maximum_fusion.9), channel_id=1, source_target_pairs={{0,8},{4,12},{8,0},{12,4},{16,24},{20,28},{24,16},{28,20},{1,9},{5... | collective-permute-start | bytes 589832 | tf_op jit(solution)/shard_map/ppermute | solution.py:235
  39.4 9.0 %collective-permute-start.4 = (bf16[2,384,128]{2,1,0:T(8,128)(2,1)S(1)}, bf16[2,384,128]{2,1,0:T(8,128)(2,1)S(1)}, u32[]{:S(2)}, u32[]{:S(2)}) collective-permute-start(bf16[2,384,128]{2,1,0:T(8,128)(2,1)S(1)} %pad_maximum_fusion.8), channel_id=1, source_target_pairs={{0,8},{4,12},{8,0},{12,4},{16,24},{20,28},{24,16},{28,20},{1,9},{5... | collective-permute-start | bytes 589832 | tf_op jit(solution)/shard_map/ppermute | solution.py:235
  40.2 13.2 %copy-start.14 = (s32[16,2]{0,1:T(2,128)S(1)}, s32[16,2]{0,1:T(2,128)}, u32[]{:S(2)}) copy-start(s32[16,2]{0,1:T(2,128)} %param.16) | copy-start | bytes 388
  40.2 13.3 %copy-start.15 = (s32[16,2]{0,1:T(2,128)S(1)}, s32[16,2]{0,1:T(2,128)}, u32[]{:S(2)}) copy-start(s32[16,2]{0,1:T(2,128)} %param.17) | copy-start | bytes 388
  40.2 24.9 %collective-permute-start.11 = (bf16[2,640,128]{2,1,0:T(8,128)(2,1)S(1)}, bf16[2,640,128]{2,1,0:T(8,128)(2,1)}, u32[]{:S(2)}, u32[]{:S(2)}) collective-permute-start(bf16[2,640,128]{2,1,0:T(8,128)(2,1)S(1)} %pad_maximum_fusion.5), channel_id=1, source_target_pairs={{0,16},{4,20},{8,24},{12,28},{16,0},{20,4},{24,8},{28,12},{1,17},{... | collective-permute-start | bytes 983048 | tf_op jit(solution)/shard_map/ppermute | solution.py:235
  49.3 21.4 %collective-permute-start.5 = (bf16[2,640,128]{2,1,0:T(8,128)(2,1)}, bf16[2,640,128]{2,1,0:T(8,128)(2,1)}, u32[]{:S(2)}, u32[]{:S(2)}) collective-permute-start(bf16[2,640,128]{2,1,0:T(8,128)(2,1)} %pad_maximum_fusion.4), channel_id=1, source_target_pairs={{0,16},{4,20},{8,24},{12,28},{16,0},{20,4},{24,8},{28,12},{1,17},{... | collective-permute-start | bytes 983048 | tf_op jit(solution)/shard_map/ppermute | solution.py:235
  50.9 28.5 %collective-permute-start = (bf16[2,2048,128]{2,1,0:T(8,128)(2,1)}, bf16[2,2048,128]{2,1,0:T(8,128)(2,1)}, u32[]{:S(2)}, u32[]{:S(2)}) collective-permute-start(bf16[2,2048,128]{2,1,0:T(8,128)(2,1)} %pad_maximum_fusion.kv_own), channel_id=1, source_target_pairs={{0,8},{4,12},{8,16},{12,20},{16,24},{20,28},{1,9},{5,13},{9,17},{1... | collective-permute-start | bytes 3145736 | tf_op jit(solution)/shard_map/ppermute | solution.py:235
  53.6 80.0 %copy-start = (s32[2]{0:T(128)}, s32[2]{0:T(128)S(1)}, u32[]{:S(2)}) copy-start(s32[2]{0:T(128)S(1)} %pad_add_fusion.place) | copy-start | bytes 28
  65.1 68.5 %collective-permute-start.1 = (bf16[2,2048,128]{2,1,0:T(8,128)(2,1)}, bf16[2,2048,128]{2,1,0:T(8,128)(2,1)S(1)}, u32[]{:S(2)}, u32[]{:S(2)}) collective-permute-start(bf16[2,2048,128]{2,1,0:T(8,128)(2,1)} %pad_maximum_fusion.kv_own), channel_id=1, source_target_pairs={{0,4},{8,12},{16,20},{24,28},{1,5},{9,13},{17,21},{25,29},{2,6},{1... | collective-permute-start | bytes 3145736 | tf_op jit(solution)/shard_map/ppermute | solution.py:235
  71.8 29.2 %copy-start.1 = (s32[8]{0:T(128)S(1)}, s32[8]{0:T(128)}, u32[]{:S(2)}) copy-start(s32[8]{0:T(128)} %vertical.3) | copy-start | bytes 100
  71.8 28.2 %collective-permute-start.8 = (bf16[2,2048,128]{2,1,0:T(8,128)(2,1)}, bf16[2,2048,128]{2,1,0:T(8,128)(2,1)S(1)}, u32[]{:S(2)}, u32[]{:S(2)}) collective-permute-start(bf16[2,2048,128]{2,1,0:T(8,128)(2,1)} %collective-permute-done.6.kv_back), channel_id=1, source_target_pairs={{4,0},{12,8},{20,16},{28,24},{5,1},{13,9},{21,17},{29,25},{6,2},{1... | collective-permute-start | bytes 3145736 | tf_op jit(solution)/shard_map/ppermute | solution.py:235
  79.4 54.3 %collective-permute-start.2 = (bf16[2,2048,128]{2,1,0:T(8,128)(2,1)}, bf16[2,2048,128]{2,1,0:T(8,128)(2,1)S(1)}, u32[]{:S(2)}, u32[]{:S(2)}) collective-permute-start(bf16[2,2048,128]{2,1,0:T(8,128)(2,1)} %collective-permute-done.kv_back), channel_id=1, source_target_pairs={{4,0},{12,8},{20,16},{28,24},{5,1},{13,9},{21,17},{29,25},{6,2},{1... | collective-permute-start | bytes 3145736 | tf_op jit(solution)/shard_map/ppermute | solution.py:235
  100.0 1.0 copy-start.18
  133.4 40.6 %collective-permute-start.25 = (bf16[2,640,128]{2,1,0:T(8,128)(2,1)S(1)}, bf16[2,640,128]{2,1,0:T(8,128)(2,1)S(1)}, u32[]{:S(2)}, u32[]{:S(2)}) collective-permute-start(bf16[2,640,128]{2,1,0:T(8,128)(2,1)S(1)} %pad_maximum_fusion.7), channel_id=1, source_target_pairs={{0,16},{4,20},{8,24},{12,28},{16,0},{20,4},{24,8},{28,12},{1,17},{... | collective-permute-start | bytes 983048 | tf_op jit(solution)/shard_map/ppermute | solution.py:235
  133.5 54.4 %collective-permute-start.23 = (bf16[2,2048,128]{2,1,0:T(8,128)(2,1)S(1)}, bf16[2,2048,128]{2,1,0:T(8,128)(2,1)S(1)}, u32[]{:S(2)}, u32[]{:S(2)}) collective-permute-start(bf16[2,2048,128]{2,1,0:T(8,128)(2,1)S(1)} %get-tuple-element.45), channel_id=1, source_target_pairs={{0,4},{4,0},{8,12},{12,8},{16,20},{20,16},{24,28},{28,24},{1,5},{5... | collective-permute-start | bytes 3145736 | tf_op jit(solution)/shard_map/ppermute | solution.py:235
  133.6 1.0 copy-start.16
  134.6 1.0 copy-start.17
  168.0 5.1 %copy-start.5 = (bf16[2048,512]{1,0:T(8,128)(2,1)S(1)}, bf16[2048,512]{1,0:T(8,128)(2,1)}, u32[]{:S(2)}) copy-start(bf16[2048,512]{1,0:T(8,128)(2,1)} %get-tuple-element.38) | copy-start | bytes 6291460
  168.1 13.6 %collective-permute-start.20 = (bf16[2,640,128]{2,1,0:T(8,128)(2,1)S(1)}, bf16[2,640,128]{2,1,0:T(8,128)(2,1)S(1)}, u32[]{:S(2)}, u32[]{:S(2)}) collective-permute-start(bf16[2,640,128]{2,1,0:T(8,128)(2,1)S(1)} %pad_maximum_fusion.6), channel_id=1, source_target_pairs={{0,16},{4,20},{8,24},{12,28},{16,0},{20,4},{24,8},{28,12},{1,17},{... | collective-permute-start | bytes 983048 | tf_op jit(solution)/shard_map/ppermute | solution.py:235
  171.0 24.1 %collective-permute-start.18 = (bf16[2,2048,128]{2,1,0:T(8,128)(2,1)S(1)}, bf16[2,2048,128]{2,1,0:T(8,128)(2,1)S(1)}, u32[]{:S(2)}, u32[]{:S(2)}) collective-permute-start(bf16[2,2048,128]{2,1,0:T(8,128)(2,1)S(1)} %get-tuple-element.41), channel_id=1, source_target_pairs={{0,4},{4,0},{8,12},{12,8},{16,20},{20,16},{24,28},{28,24},{1,5},{5... | collective-permute-start | bytes 3145736 | tf_op jit(solution)/shard_map/ppermute | solution.py:235
  174.0 69.8 %collective-permute-start.13 = (bf16[512,512]{1,0:T(8,128)(2,1)S(1)}, bf16[512,512]{1,0:T(8,128)(2,1)S(1)}, u32[]{:S(2)}, u32[]{:S(2)}) collective-permute-start(bf16[512,512]{1,0:T(8,128)(2,1)S(1)} %get-tuple-element.49), channel_id=1, source_target_pairs={{0,1},{1,0},{2,3},{3,2},{4,5},{5,4},{6,7},{7,6},{8,9},{9,8},{10,11... | collective-permute-start | bytes 1572872 | tf_op jit(solution)/shard_map/ppermute | solution.py:278
  174.2 9.7 %collective-permute-start.26 = (bf16[2,384,128]{2,1,0:T(8,128)(2,1)S(1)}, bf16[2,384,128]{2,1,0:T(8,128)(2,1)S(1)}, u32[]{:S(2)}, u32[]{:S(2)}) collective-permute-start(bf16[2,384,128]{2,1,0:T(8,128)(2,1)S(1)} %pad_maximum_fusion.11), channel_id=1, source_target_pairs={{0,8},{4,12},{8,0},{12,4},{16,24},{20,28},{24,16},{28,20},{1,9},{5... | collective-permute-start | bytes 589832 | tf_op jit(solution)/shard_map/ppermute | solution.py:235
  181.9 5.8 %collective-permute-start.21 = (bf16[2,384,128]{2,1,0:T(8,128)(2,1)S(1)}, bf16[2,384,128]{2,1,0:T(8,128)(2,1)S(1)}, u32[]{:S(2)}, u32[]{:S(2)}) collective-permute-start(bf16[2,384,128]{2,1,0:T(8,128)(2,1)S(1)} %pad_maximum_fusion.10), channel_id=1, source_target_pairs={{0,8},{4,12},{8,0},{12,4},{16,24},{20,28},{24,16},{28,20},{1,9},{5... | collective-permute-start | bytes 589832 | tf_op jit(solution)/shard_map/ppermute | solution.py:235
  184.1 9.6 %collective-permute-start.27 = (bf16[2,256,128]{2,1,0:T(8,128)(2,1)S(1)}, bf16[2,256,128]{2,1,0:T(8,128)(2,1)S(1)}, u32[]{:S(2)}, u32[]{:S(2)}) collective-permute-start(bf16[2,256,128]{2,1,0:T(8,128)(2,1)S(1)} %pad_maximum_fusion.17), channel_id=1, source_target_pairs={{0,4},{4,0},{8,12},{12,8},{16,20},{20,16},{24,28},{28,24},{1,5},{5... | collective-permute-start | bytes 393224 | tf_op jit(solution)/shard_map/ppermute | solution.py:235
  187.9 2.8 copy-start.4
  188.2 28.1 %collective-permute-start.24 = (bf16[2,2048,128]{2,1,0:T(8,128)(2,1)S(1)}, bf16[2,2048,128]{2,1,0:T(8,128)(2,1)S(1)}, u32[]{:S(2)}, u32[]{:S(2)}) collective-permute-start(bf16[2,2048,128]{2,1,0:T(8,128)(2,1)S(1)} %fusion.3), channel_id=1, source_target_pairs={{8,0},{12,4},{16,8},{20,12},{24,16},{28,20},{9,1},{13,5},{17,9},{2... | collective-permute-start | bytes 3145736 | tf_op jit(solution)/shard_map/ppermute | solution.py:235
  189.7 5.3 %collective-permute-start.22 = (bf16[2,256,128]{2,1,0:T(8,128)(2,1)S(1)}, bf16[2,256,128]{2,1,0:T(8,128)(2,1)S(1)}, u32[]{:S(2)}, u32[]{:S(2)}) collective-permute-start(bf16[2,256,128]{2,1,0:T(8,128)(2,1)S(1)} %pad_maximum_fusion.16), channel_id=1, source_target_pairs={{0,4},{4,0},{8,12},{12,8},{16,20},{20,16},{24,28},{28,24},{1,5},{5... | collective-permute-start | bytes 393224 | tf_op jit(solution)/shard_map/ppermute | solution.py:235
  191.6 24.8 %copy-start.3 = (f32[2,2048,128]{2,1,0:T(8,128)S(1)}, f32[2,2048,128]{2,1,0:T(8,128)}, u32[]{:S(2)}) copy-start(f32[2,2048,128]{2,1,0:T(8,128)} %get-tuple-element.43) | copy-start | bytes 6291460
  195.5 40.4 %collective-permute-start.19 = (bf16[2,2048,128]{2,1,0:T(8,128)(2,1)S(1)}, bf16[2,2048,128]{2,1,0:T(8,128)(2,1)S(1)}, u32[]{:S(2)}, u32[]{:S(2)}) collective-permute-start(bf16[2,2048,128]{2,1,0:T(8,128)(2,1)S(1)} %fusion.2), channel_id=1, source_target_pairs={{8,0},{12,4},{16,8},{20,12},{24,16},{28,20},{9,1},{13,5},{17,9},{2... | collective-permute-start | bytes 3145736 | tf_op jit(solution)/shard_map/ppermute | solution.py:235
  216.8 19.0 %copy-start.2 = (f32[2,2048,128]{2,1,0:T(8,128)S(1)}, f32[2,2048,128]{2,1,0:T(8,128)}, u32[]{:S(2)}) copy-start(f32[2,2048,128]{2,1,0:T(8,128)} %get-tuple-element.39) | copy-start | bytes 6291460
  217.0 22.5 %collective-permute-start.33 = (bf16[2,512,128]{2,1,0:T(8,128)(2,1)S(1)}, bf16[2,512,128]{2,1,0:T(8,128)(2,1)S(1)}, u32[]{:S(2)}, u32[]{:S(2)}) collective-permute-start(bf16[2,512,128]{2,1,0:T(8,128)(2,1)S(1)} %get-tuple-element.59), channel_id=1, source_target_pairs={{0,3},{1,2},{2,1},{3,0},{4,7},{5,6},{6,5},{7,4},{8,11},{9,10},{10,... | collective-permute-start | bytes 786440 | tf_op jit(solution)/shard_map/ppermute | solution.py:278
  217.1 23.7 %collective-permute-start.31 = (bf16[2,512,128]{2,1,0:T(8,128)(2,1)S(1)}, bf16[2,512,128]{2,1,0:T(8,128)(2,1)S(1)}, u32[]{:S(2)}, u32[]{:S(2)}) collective-permute-start(bf16[2,512,128]{2,1,0:T(8,128)(2,1)S(1)} %get-tuple-element.60), channel_id=1, source_target_pairs={{0,2},{1,3},{2,0},{3,1},{4,6},{5,7},{6,4},{7,5},{8,10},{9,11},{10,... | collective-permute-start | bytes 786440 | tf_op jit(solution)/shard_map/ppermute | solution.py:278
  238.0 3.6 %collective-permute-start.29 = (bf16[2,512,128]{2,1,0:T(8,128)(2,1)S(1)}, bf16[2,512,128]{2,1,0:T(8,128)(2,1)S(1)}, u32[]{:S(2)}, u32[]{:S(2)}) collective-permute-start(bf16[2,512,128]{2,1,0:T(8,128)(2,1)S(1)} %get-tuple-element.61), channel_id=1, source_target_pairs={{0,1},{1,0},{2,3},{3,2},{4,5},{5,4},{6,7},{7,6},{8,9},{9,8},{10,11... | collective-permute-start | bytes 786440 | tf_op jit(solution)/shard_map/ppermute | solution.py:278
  238.0 8.2 %collective-permute-start.32 = (bf16[2,512,128]{2,1,0:T(8,128)(2,1)S(1)}, bf16[2,512,128]{2,1,0:T(8,128)(2,1)S(1)}, u32[]{:S(2)}, u32[]{:S(2)}) collective-permute-start(bf16[2,512,128]{2,1,0:T(8,128)(2,1)S(1)} %get-tuple-element.62), channel_id=1, source_target_pairs={{0,3},{1,2},{2,1},{3,0},{4,7},{5,6},{6,5},{7,4},{8,11},{9,10},{10,... | collective-permute-start | bytes 786440 | tf_op jit(solution)/shard_map/ppermute | solution.py:278
  239.5 13.3 %collective-permute-start.30 = (bf16[2,512,128]{2,1,0:T(8,128)(2,1)S(1)}, bf16[2,512,128]{2,1,0:T(8,128)(2,1)S(1)}, u32[]{:S(2)}, u32[]{:S(2)}) collective-permute-start(bf16[2,512,128]{2,1,0:T(8,128)(2,1)S(1)} %get-tuple-element.63), channel_id=1, source_target_pairs={{0,2},{1,3},{2,0},{3,1},{4,6},{5,7},{6,4},{7,5},{8,10},{9,11},{10,... | collective-permute-start | bytes 786440 | tf_op jit(solution)/shard_map/ppermute | solution.py:278
  240.8 13.4 %collective-permute-start.28 = (bf16[2,512,128]{2,1,0:T(8,128)(2,1)S(1)}, bf16[2,512,128]{2,1,0:T(8,128)(2,1)S(1)}, u32[]{:S(2)}, u32[]{:S(2)}) collective-permute-start(bf16[2,512,128]{2,1,0:T(8,128)(2,1)S(1)} %get-tuple-element.64), channel_id=1, source_target_pairs={{0,1},{1,0},{2,3},{3,2},{4,5},{5,4},{6,7},{7,6},{8,9},{9,8},{10,11... | collective-permute-start | bytes 786440 | tf_op jit(solution)/shard_map/ppermute | solution.py:278
  241.6 22.5 %collective-permute-start.15 = (bf16[512,512]{1,0:T(8,128)(2,1)S(1)}, bf16[512,512]{1,0:T(8,128)(2,1)S(1)}, u32[]{:S(2)}, u32[]{:S(2)}) collective-permute-start(bf16[512,512]{1,0:T(8,128)(2,1)S(1)} %get-tuple-element.48), channel_id=1, source_target_pairs={{0,2},{1,3},{2,0},{3,1},{4,6},{5,7},{6,4},{7,5},{8,10},{9,11},{10,... | collective-permute-start | bytes 1572872 | tf_op jit(solution)/shard_map/ppermute | solution.py:278
  243.7 52.8 %copy-start.8 = (bf16[512,512]{1,0:T(8,128)(2,1)}, bf16[512,512]{1,0:T(8,128)(2,1)S(1)}, u32[]{:S(2)}) copy-start(bf16[512,512]{1,0:T(8,128)(2,1)S(1)} %collective-permute-done.13.refs_3_) | copy-start | bytes 1572868
  243.7 30.5 %collective-permute-start.17 = (bf16[512,512]{1,0:T(8,128)(2,1)S(1)}, bf16[512,512]{1,0:T(8,128)(2,1)S(1)}, u32[]{:S(2)}, u32[]{:S(2)}) collective-permute-start(bf16[512,512]{1,0:T(8,128)(2,1)S(1)} %get-tuple-element.47), channel_id=1, source_target_pairs={{0,3},{1,2},{2,1},{3,0},{4,7},{5,6},{6,5},{7,4},{8,11},{9,10},{10,... | collective-permute-start | bytes 1572872 | tf_op jit(solution)/shard_map/ppermute | solution.py:278
  246.2 28.1 %collective-permute-start.12 = (bf16[512,512]{1,0:T(8,128)(2,1)S(1)}, bf16[512,512]{1,0:T(8,128)(2,1)S(1)}, u32[]{:S(2)}, u32[]{:S(2)}) collective-permute-start(bf16[512,512]{1,0:T(8,128)(2,1)S(1)} %get-tuple-element.53), channel_id=1, source_target_pairs={{0,1},{1,0},{2,3},{3,2},{4,5},{5,4},{6,7},{7,6},{8,9},{9,8},{10,11... | collective-permute-start | bytes 1572872 | tf_op jit(solution)/shard_map/ppermute | solution.py:278
  252.8 33.7 %collective-permute-start.14 = (bf16[512,512]{1,0:T(8,128)(2,1)S(1)}, bf16[512,512]{1,0:T(8,128)(2,1)S(1)}, u32[]{:S(2)}, u32[]{:S(2)}) collective-permute-start(bf16[512,512]{1,0:T(8,128)(2,1)S(1)} %get-tuple-element.52), channel_id=1, source_target_pairs={{0,2},{1,3},{2,0},{3,1},{4,6},{5,7},{6,4},{7,5},{8,10},{9,11},{10,... | collective-permute-start | bytes 1572872 | tf_op jit(solution)/shard_map/ppermute | solution.py:278
  254.3 42.2 %collective-permute-start.16 = (bf16[512,512]{1,0:T(8,128)(2,1)S(1)}, bf16[512,512]{1,0:T(8,128)(2,1)S(1)}, u32[]{:S(2)}, u32[]{:S(2)}) collective-permute-start(bf16[512,512]{1,0:T(8,128)(2,1)S(1)} %get-tuple-element.51), channel_id=1, source_target_pairs={{0,3},{1,2},{2,1},{3,0},{4,7},{5,6},{6,5},{7,4},{8,11},{9,10},{10,... | collective-permute-start | bytes 1572872 | tf_op jit(solution)/shard_map/ppermute | solution.py:278
  264.1 32.4 %copy-start.9 = (bf16[512,512]{1,0:T(8,128)(2,1)}, bf16[512,512]{1,0:T(8,128)(2,1)S(1)}, u32[]{:S(2)}) copy-start(bf16[512,512]{1,0:T(8,128)(2,1)S(1)} %collective-permute-done.15.refs_5_) | copy-start | bytes 1572868
  274.3 22.2 %copy-start.10 = (bf16[512,512]{1,0:T(8,128)(2,1)}, bf16[512,512]{1,0:T(8,128)(2,1)S(1)}, u32[]{:S(2)}) copy-start(bf16[512,512]{1,0:T(8,128)(2,1)S(1)} %collective-permute-done.17.refs_7_) | copy-start | bytes 1572868
  274.3 22.2 %copy-start.11 = (bf16[512,512]{1,0:T(8,128)(2,1)}, bf16[512,512]{1,0:T(8,128)(2,1)S(1)}, u32[]{:S(2)}) copy-start(bf16[512,512]{1,0:T(8,128)(2,1)S(1)} %collective-permute-done.12.refs_2_) | copy-start | bytes 1572868
  286.5 10.0 %copy-start.12 = (bf16[512,512]{1,0:T(8,128)(2,1)}, bf16[512,512]{1,0:T(8,128)(2,1)S(1)}, u32[]{:S(2)}) copy-start(bf16[512,512]{1,0:T(8,128)(2,1)S(1)} %collective-permute-done.14.refs_4_) | copy-start | bytes 1572868
  296.5 0.8 copy-start.13

commit v2 on v1

v2 whole, which is shorter than its diff:
```python
import functools
import math

import jax
import jax.numpy as jnp
from jax import lax
from jax.experimental import pallas as pl
from jax.experimental.pallas import tpu as pltpu
from jax.sharding import PartitionSpec as P

HD = 128
BLK = 128
VERT_DEV = 1
FAR = 1e30


def attention_kernel(dims, place, vertical, columns, offsets, *refs):
    local_blocks, group, vert_total, heads, cuts, parts, counts = dims
    refs = list(refs)

    def take(count):
        taken = refs[:count]
        del refs[:count]
        return taken

    q_ref, do_ref, kv_own, kv_column, kv_other = take(5)
    kv_back, kv_even, kv_odd = take(counts[0]), take(counts[1]), take(counts[2])
    dq_refs, (own_ref,), prev_refs, back_refs = take(heads), take(1), take(cuts), take(cuts)
    far_refs = take(2)
    pool_k, pool_v, acc_k, acc_v, sems = refs
    turn_number = pl.program_id(0)
    seq_index, head_index = place[0], place[1]
    share = local_blocks // heads
    step = (turn_number // share ^ head_index) * share + lax.rem(turn_number, share)
    rows = local_blocks * BLK
    scale = 1.0 / math.sqrt(HD)

    @pl.when(turn_number == 0)
    def _():
        def copies(prev, parity):
            parts = [(kv_own, 0)]
            parts += [(ref, 2 * rows + at * ref.shape[1]) for at, ref in enumerate(kv_back)]
            parts += [(ref, rows + at * ref.shape[1]) for at, ref in enumerate(prev)]
            made = []
            for side, pool in enumerate((pool_k, pool_v)):
                for ref, start in parts:
                    made.append((ref.at[side], pool.at[pl.ds(start, ref.shape[1])]))
                for ref, number in ((kv_column, parity), (kv_other, 1 - parity)):
                    for plane in range(vert_total // 2):
                        into = pool.at[pl.ds(3 * rows + (2 * plane + number) * BLK, BLK)]
                        made.append((ref.at[plane, side], into))
                source = kv_other if parity else kv_column
                made.append((source.at[vert_total // 2, side], pool.at[pl.ds(3 * rows + vert_total * BLK, BLK)]))
            return [pltpu.make_async_copy(*ends, sems.at[at]) for at, ends in enumerate(made)]

        odd = lax.rem(seq_index, 2) == 1
        ways = ((odd, kv_even, 1), (jnp.logical_not(odd), kv_odd, 0))
        for way, prev, parity in ways:

            @pl.when(way)
            def _():
                for copy in copies(prev, parity):
                    copy.start()

        acc_k[...] = jnp.zeros_like(acc_k)
        acc_v[...] = jnp.zeros_like(acc_v)
        for way, prev, parity in ways:

            @pl.when(way)
            def _():
                for copy in copies(prev, parity):
                    copy.wait()

    block = seq_index * local_blocks + step

    def column_block(column):
        return column // VERT_DEV * local_blocks + vertical[column]

    def near(offset):
        at = step - offset
        return jnp.where(at >= 0, at, jnp.where(at >= -local_blocks, at + 2 * local_blocks, at + 4 * local_blocks))

    first, second = offsets[step, 0], offsets[step, 1]
    left, right = columns[step, 0], columns[step, 1]
    b2, b3 = block - first, block - second
    b4, b5 = column_block(left), column_block(right)
    far = 3 * local_blocks
    slots = [far + vert_total, step, near(first), near(second), far + left, far + right]
    live = [
        block > 0,
        None,
        b2 > 0,
        (b3 > 0) & (b3 != b2),
        (b4 > 0) & (b4 < block) & (b4 != b2) & (b4 != b3),
        (b5 > 0) & (b5 < block) & (b5 != b2) & (b5 != b3) & (b5 != b4),
    ]
    spots = [pl.ds(pl.multiple_of(slot * BLK, BLK), BLK) for slot in slots]
    queries = jnp.concatenate([q_ref[:, g * HD : (g + 1) * HD] for g in range(group)], axis=0)
    grads = jnp.concatenate([do_ref[:, g * HD : (g + 1) * HD] for g in range(group)], axis=0)
    width = group * BLK
    keys = [pool_k[spot, :] for spot in spots]
    values = [pool_v[spot, :] for spot in spots]
    contract_last = (((1,), (1,)), ((), ()))
    contract_first = (((0,), (0,)), ((), ()))
    key_at = lax.broadcasted_iota(jnp.int32, (BLK, width), 0)
    query_at = lax.broadcasted_iota(jnp.int32, (BLK, width), 1) % BLK
    seen = key_at <= query_at
    turn = scale * math.log2(math.e)
    scores, tops = [], []
    for number in range(6):
        part = lax.dot_general(keys[number], queries, contract_last, preferred_element_type=jnp.float32)
        part = part * turn
        if number == 1:
            part = jnp.where(seen, part, -FAR)
        scores.append(part)
        top = jnp.max(part, axis=0, keepdims=True)
        if number != 1:
            top = jnp.where(live[number], top, -FAR)
        tops.append(top)
    top = functools.reduce(jnp.maximum, tops)
    weights, products = [], []
    total = jnp.zeros((1, width), jnp.float32)
    delta = jnp.zeros((1, width), jnp.float32)
    for number in range(6):
        base = top if number == 1 else jnp.where(live[number], top, FAR)
        weight = jnp.exp2(scores[number] - base)
        product = lax.dot_general(values[number], grads, contract_last, preferred_element_type=jnp.float32)
        total = total + jnp.sum(weight, axis=0, keepdims=True)
        delta = delta + jnp.sum(weight * product, axis=0, keepdims=True)
        weights.append(weight)
        products.append(product)
    inverse = 1.0 / total
    delta = delta * inverse
    dq = jnp.zeros((width, HD), jnp.float32)
    for number in range(6):
        prob = weights[number] * inverse
        dscore = (prob * (products[number] - delta)).astype(jnp.bfloat16)
        prob = prob.astype(jnp.bfloat16)
        acc_v[spots[number], :] += jnp.dot(prob, grads, preferred_element_type=jnp.float32)
        acc_k[spots[number], :] += jnp.dot(dscore, queries, preferred_element_type=jnp.float32)
        dq = dq + lax.dot_general(dscore, keys[number], contract_first, preferred_element_type=jnp.float32)
    dq = (dq * scale).astype(jnp.bfloat16)
    for k, dq_ref in enumerate(dq_refs):

        @pl.when(turn_number // share == k)
        def _():
            for g in range(group):
                dq_ref[:, g * HD : (g + 1) * HD] = dq[g * BLK : (g + 1) * BLK]

    @pl.when(turn_number == local_blocks - 1)
    def _():
        size = rows // cuts // parts
        for side, (acc, factor) in enumerate(((acc_k, scale), (acc_v, 1.0))):
            for cut in range(cuts):
                for part in range(parts):
                    start = (part * cuts + cut) * size
                    into = pl.ds(part * size, size)
                    prev_refs[cut][side, into, :] = (acc[pl.ds(rows + start, size), :] * factor).astype(jnp.bfloat16)
                    back_refs[cut][side, into, :] = (acc[pl.ds(2 * rows + start, size), :] * factor).astype(jnp.bfloat16)
            own_ref[side] = acc[:rows, :] * factor

            def far_block(number):
                start = pl.multiple_of((3 * local_blocks + number) * BLK, BLK)
                return (acc[pl.ds(start, BLK), :] * factor).astype(jnp.bfloat16)

            for ref, parity in ((far_refs[0], seq_index % 2), (far_refs[1], 1 - seq_index % 2)):
                for plane in range(vert_total // 2):
                    ref[plane, side] = far_block(2 * plane + parity)
                ref[vert_total // 2, side] = far_block(vert_total)


def attention(
    head, kv_local, heads, cuts, parts, place, vertical, columns, offsets, queries, grad_out, kv_own, kv_column, kv_other,
    kv_back, kv_even, kv_odd
):
    seq_len = queries.shape[0]
    local_blocks = seq_len // BLK
    width = queries.shape[1] // kv_local
    group = width // HD
    vert_total = vertical.shape[0]
    total_rows = 3 * seq_len + (vert_total + 1) * BLK
    anywhere = pl.BlockSpec(memory_space=pl.ANY)
    share = local_blocks // heads
    by_block = pl.BlockSpec((BLK, width), lambda i, place, *_: ((i // share ^ place[1]) * share + i % share, head))

    def whole(*shape):
        return pl.BlockSpec(shape, lambda i, *_: (0,) * len(shape))

    def share_spec(k):
        return pl.BlockSpec((BLK, width), lambda i, *_: (jnp.clip(i - k * share, 0, share - 1), 0))

    near_shape = (2, seq_len, HD)
    cut_shape = (2, seq_len // cuts, HD)
    block_shape = (2, BLK, HD)
    far_shapes = [(vert_total // 2 + 1, *block_shape)] * 2
    flops = 2 * 5 * seq_len * group * 6 * BLK * HD
    pools = [*kv_back, *kv_even, *kv_odd]
    counts = (len(kv_back), len(kv_even), len(kv_odd))
    outs = pl.pallas_call(
        functools.partial(attention_kernel, (local_blocks, group, vert_total, heads, cuts, parts, counts)),
        grid_spec=pltpu.PrefetchScalarGridSpec(
            num_scalar_prefetch=4,
            grid=(local_blocks,),
            in_specs=[by_block, by_block] + [anywhere] * (3 + len(pools)),
            out_specs=[share_spec(k) for k in range(heads)]
            + [whole(*near_shape)]
            + [whole(*cut_shape)] * (2 * cuts)
            + [whole(*shape) for shape in far_shapes],
            scratch_shapes=[
                pltpu.VMEM((total_rows, HD), jnp.bfloat16),
                pltpu.VMEM((total_rows, HD), jnp.bfloat16),
                pltpu.VMEM((total_rows, HD), jnp.float32),
                pltpu.VMEM((total_rows, HD), jnp.float32),
                pltpu.SemaphoreType.DMA((2 * (2 + len(pools) + vert_total),)),
            ],
        ),
        out_shape=[jax.ShapeDtypeStruct((seq_len // heads, width), jnp.bfloat16)] * heads
        + [jax.ShapeDtypeStruct(near_shape, jnp.float32)]
        + [jax.ShapeDtypeStruct(cut_shape, jnp.bfloat16)] * (2 * cuts)
        + [jax.ShapeDtypeStruct(shape, jnp.bfloat16) for shape in far_shapes],
        compiler_params=pltpu.CompilerParams(vmem_limit_bytes=50 * 1024 * 1024),
        cost_estimate=pl.CostEstimate(
            flops=4 * flops, bytes_accessed=20 * 1024 * 1024, transcendentals=seq_len * group * 6 * BLK
        ),
        name="attention",
    )(place, vertical, columns, offsets, queries, grad_out, kv_own, kv_column, kv_other, *pools)
    at = heads + 1
    return outs[:heads], outs[heads], outs[at : at + cuts], outs[at + cuts : at + 2 * cuts], *outs[at + 2 * cuts :]


def queries_kernel(heads, kv_local, place, *refs):
    for k in range(heads):
        for head in range(kv_local):
            piece = refs[k * kv_local + head]
            width = piece.shape[1]
            column = (place[1] ^ k) * kv_local + head
            refs[-1][:, pl.ds(pl.multiple_of(column * width, width), width)] = piece[...]


def assemble_queries(place, heads, kv_local, pieces):
    rows, width = pieces[0, 0].shape
    tile = min(rows, 128)
    count = heads * kv_local
    return pl.pallas_call(
        functools.partial(queries_kernel, heads, kv_local),
        grid_spec=pltpu.PrefetchScalarGridSpec(
            num_scalar_prefetch=1,
            grid=(rows // tile,),
            in_specs=[pl.BlockSpec((tile, width), lambda i, *_: (i, 0))] * count,
            out_specs=pl.BlockSpec((tile, width * count), lambda i, *_: (i, 0)),
        ),
        out_shape=jax.ShapeDtypeStruct((rows, width * count), jnp.bfloat16),
        name="assemble_queries",
    )(place, *(pieces[k, head] for k in range(heads) for head in range(kv_local)))


def pairs_kernel(heads, kv_local, cuts, place, *refs):
    k_out, v_out = refs[-2:]
    refs = list(refs[:-2])
    for k in range(heads):
        for head in range(kv_local):
            column = (place[1] ^ k) * kv_local + head
            spot = pl.ds(pl.multiple_of(column * HD, HD), HD)
            for cut in range(cuts[head]):
                both = refs.pop(0)
                size = both.shape[1]
                k_out[pl.ds(cut * size, size), spot] = both[0]
                v_out[pl.ds(cut * size, size), spot] = both[1]


def assemble_pairs(place, heads, kv_local, cuts, pieces):
    arrays = [pieces[k, head, cut] for k in range(heads) for head in range(kv_local) for cut in range(cuts[head])]
    rows = pieces[0, 0, 0].shape[1] * cuts[0]
    out_shape = jax.ShapeDtypeStruct((rows, HD * heads * kv_local), jnp.bfloat16)
    return pl.pallas_call(
        functools.partial(pairs_kernel, heads, kv_local, cuts),
        grid_spec=pltpu.PrefetchScalarGridSpec(
            num_scalar_prefetch=1,
            grid=(1,),
            in_specs=[pl.BlockSpec(array.shape, lambda i, *_: (0, 0, 0)) for array in arrays],
            out_specs=[pl.BlockSpec(out_shape.shape, lambda i, *_: (0, 0))] * 2,
        ),
        out_shape=[out_shape] * 2,
        name="assemble_pairs",
    )(place, *arrays)


def after(value, *others):
    return lax.optimization_barrier((value, others))[0]


def shards(queries, keys, values, grad_out, vertical, columns, offsets):
    seq_len = queries.shape[0]
    seq_size = lax.axis_size("seq")
    heads = lax.axis_size("head")
    kv_local = keys.shape[1] // HD
    local_blocks = seq_len // BLK
    cuts = 2
    half = seq_len // 2
    seq_index = lax.axis_index("seq")
    head_index = lax.axis_index("head")
    place = jnp.stack([seq_index, head_index]).astype(jnp.int32)
    odd = seq_index % 2 == 1
    levels = [1 << level for level in range(int(math.log2(seq_size)))]

    def along(array, pairs, name):
        with jax.named_scope(name):
            return lax.ppermute(array, "seq", pairs)

    def across(array, k, name):
        with jax.named_scope(name):
            return lax.ppermute(array, "head", [(i, i ^ k) for i in range(heads)]) if k else array

    def shift(by, only=None):
        return [(i, i + by) for i in range(seq_size) if 0 <= i + by < seq_size and only in (None, i % 2)]

    exchange = [(i, i ^ 1) for i in range(seq_size)]
    own_vertical = lax.dynamic_slice_in_dim(vertical, seq_index * VERT_DEV, VERT_DEV)[0]
    kvs = [
        jnp.stack([keys[:, head * HD : (head + 1) * HD], values[:, head * HD : (head + 1) * HD]])
        for head in range(kv_local)
    ]
    mine = jnp.stack([lax.dynamic_slice_in_dim(kv, own_vertical * BLK, BLK, axis=1) for kv in kvs])
    sink = jnp.stack([kv[:, :BLK] for kv in kvs])
    groups = [list(range(0, seq_size, 2)), list(range(1, seq_size, 2))]

    def column_of(block, name):
        with jax.named_scope(name):
            wide = jnp.broadcast_to(block, (seq_size // 2, *block.shape))
            return lax.all_to_all(wide, "seq", split_axis=0, concat_axis=0, axis_index_groups=groups)

    first = sink
    for hop in reversed(levels[1:]):
        got = along(first, [(i, i + hop) for i in range(0, seq_size, 2 * hop)], f"in_first{hop}")
        first = jnp.where(seq_index % (2 * hop) == hop, got, first)

    fetched = []
    for head, kv in enumerate(kvs):
        block = mine[head]
        if head:
            kv, block = after((kv, block), fetched[0][1][1])
        backs = [along(kv[:, :half], shift(2), f"in_back{head}_a")]
        kv_column = jnp.concatenate([column_of(block, f"in_column{head}"), first[None, head]])
        kv_other = along(kv_column, exchange, f"in_column_pair{head}")
        if head:
            backs.append(along(after(kv[:, half:], backs[0]), shift(2), f"in_back{head}_b"))
            odds = [along(backs[0], shift(-1, 1), f"in_odd{head}_a"), along(after(kv[:, half:], backs[0]), shift(1, 1), f"in_odd{head}_b")]
        else:
            backs.append(along(after(kv[:, half:], backs[0]), shift(2), f"in_back{head}_b"))
            odds = [along(backs[0], shift(-1, 1), f"in_odd{head}_a"), along(after(backs[1], kv_other), shift(-1, 1), f"in_odd{head}_b")]
        evens = [along(kv, shift(1, 0), f"in_even{head}")]
        fetched.append((kv, backs, evens, odds, kv_column, kv_other))
    if kv_local > 1:
        place = after(place, fetched[1][1][0], fetched[1][4])

    query_pieces, pair_pieces, results, far_pairs = {}, {}, [], []
    planes = seq_size // 2
    cut_counts = [cuts if head + 1 == kv_local else 1 for head in range(kv_local)]
    for head, (kv, backs, evens, odds, kv_column, kv_other) in enumerate(fetched):
        last = head + 1 == kv_local
        dqs, own, prevs, backs, *fars = attention(
            head, kv_local, heads, cut_counts[head], heads if last else 1,
            place, vertical, columns, offsets, queries, grad_out, kv, kv_column, kv_other, backs, evens, odds,
        )
        if not last:
            far_pairs.append((fars[0], along(fars[1], exchange, f"out_far_pair{head}")))
            for k in range(heads):
                query_pieces[k, head] = across(dqs[k], k, f"out_query{head}_{k}")
            sides = [along(prev, exchange, f"out_pair{head}") for prev in prevs]
            results.append((own, sides, backs))
            continue
        if head:
            results = after(results, dqs[0])
            before = [query_pieces[k, head - 1] for k in range(heads)]
            prevs, fars, dqs = after((prevs, fars, dqs), before, far_pairs, results)
        first_k = heads // 2
        sides = [along(prevs[0], exchange, f"out_pair{head}_0")]
        far_pairs.append((fars[0], along(fars[1], exchange, f"out_far_pair{head}")))
        query_pieces[first_k, head] = across(dqs[first_k], first_k, f"out_query{head}_{first_k}")

        def onward(back, side, name):
            total = back.astype(jnp.float32) + jnp.where(odd, side.astype(jnp.float32), 0.0)
            return along(total.astype(jnp.bfloat16), shift(-2), name)

        for at, (own_before, sides_before, backs_before) in enumerate(results):
            returned = [onward(back, side, f"out_onward{at}") for back, side in zip(backs_before, sides_before)]
            results[at] = (own_before, sides_before, returned)
        far_sum = jnp.stack([keep.astype(jnp.float32) + pair.astype(jnp.float32) for keep, pair in far_pairs], axis=1)
        first = far_sum[planes]
        with jax.named_scope("out_far"):
            far = lax.all_to_all(
                far_sum[:planes].astype(jnp.bfloat16), "seq", split_axis=0, concat_axis=0, axis_index_groups=groups
            )
        far = jnp.sum(far.astype(jnp.float32), axis=0)
        prevs, dqs = after((prevs, dqs), far_sum, query_pieces[first_k, head])
        sides += [along(prev, exchange, f"out_pair{head}_{cut + 1}") for cut, prev in enumerate(prevs[1:])]
        for hop in levels[1:]:
            pairs = [(i + hop, i) for i in range(0, seq_size, 2 * hop)]
            first = first + along(first.astype(jnp.bfloat16), pairs, f"out_first{hop}").astype(jnp.float32)
        for k in range(heads):
            if k != first_k:
                query_pieces[k, head] = across(dqs[k], k, f"out_query{head}_{k}")
        sides[1] = after(sides[1], [query_pieces[k, head] for k in range(heads)])
        returned = [onward(back, side, f"out_onward{head}_{cut}") for cut, (back, side) in enumerate(zip(backs, sides))]
        results.append((own, sides, returned))

    def token_blocks(array, parts):
        return array.reshape(2, heads, parts, -1, BLK, HD).astype(jnp.float32)

    for head, (own, sides, returned) in enumerate(results):
        count = cut_counts[head]
        if head + 1 == kv_local:
            returned = after(returned, list(pair_pieces.values()))
            query_out = assemble_queries(place, heads, kv_local, query_pieces)
        block_ids = jnp.arange(local_blocks).reshape(1, heads, count, -1, 1, 1)
        for cut in range(count):
            if cut:
                returned = after(returned, query_out, [pair_pieces[k, head, cut - 1] for k in range(heads)])
            total = token_blocks(own, count)[:, :, cut : cut + 1]
            side = token_blocks(sides[cut], 1)
            total = total + jnp.where(odd, 0.0, side) + token_blocks(returned[cut], 1)
            block = block_ids[:, :, cut : cut + 1]
            total = total + jnp.where(block == own_vertical, far[head][:, None, None, None], 0.0)
            total = total + jnp.where((block == 0) & (seq_index == 0), first[head][:, None, None, None], 0.0)
            total = total.astype(jnp.bfloat16).reshape(2, heads, -1, HD)
            for k in range(heads):
                piece = lax.dynamic_index_in_dim(total, head_index ^ k, 1, keepdims=False)
                pair_pieces[k, head, cut] = across(piece, k, f"out_pairs{head}_{cut}_{k}")
    return (query_out, *assemble_pairs(place, heads, kv_local, cut_counts, pair_pieces))


def solution(mesh):
    return jax.shard_map(
        shards,
        mesh=mesh,
        in_specs=(
            P("seq", "head"),
            P("seq", "head"),
            P("seq", "head"),
            P("seq", "head"),
            P(),
            P("seq", None),
            P("seq", None),
        ),
        out_specs=(P(("seq", "head"), None), P(("seq", "head"), None), P(("seq", "head"), None)),
        check_vma=False,
    )
```

time: 305 us -> 256 us (0.84)
  waiting for transfers between devices: 164 us -> 69.6 us
  starting transfers between devices: 42.6 us -> 76 us
  other arithmetic: 7.87 us -> 17 us
  Pallas kernels: 71.2 us -> 78.2 us
  local copies, waits for them, and re-layouts: 16.3 us -> 11.7 us
    ppermute x22 -> x24, waiting for transfers between devices: 116 us -> 56.9 us  [along(): return lax.ppermute(array, 'seq', pairs)]
    ppermute x12 -> x15, waiting for transfers between devices: 47.9 us -> 12.7 us  [across(): lax.ppermute(array, 'head', [(i, i ^ k) for i in range(heads)])]
    ppermute x22 -> x24, starting transfers between devices: 34.7 us -> 51.4 us  [along(): return lax.ppermute(array, 'seq', pairs)]
    all_to_all x0 -> x3, starting transfers between devices: none -> 14.1 us  [the longest x2 8.15 us: column_of(): lax.all_to_all(wide, 'seq', split_axis=0, concat_axis=0, axis_index_group...]
    convert_element_type x12 -> x7, other arithmetic: 1.28 us -> 7.28 us  [the longest x2 3.71 us: onward(): return along(total.astype(jnp.bfloat16), shift(-2), name)]
    pallas_call x2, Pallas kernels: 64.6 us -> 68.5 us  [attention(): pl.pallas_call(functools.partial(attention_kernel, (local_blocks, group,...]
    squeeze x8 -> x3, local copies, waits for them, and re-layouts: 5.76 us -> 2.28 us  [shards(): piece = lax.dynamic_index_in_dim(total, head_index ^ k, 1, keepdims=False)]
    pallas_call x1 -> x2, Pallas kernels: 6.6 us -> 9.7 us  [the longest x1 5.56 us: assemble_queries(): pl.pallas_call(functools.partial(queries_kernel, heads, kv_local), grid_s...]
  transfers between devices with their start and end apart: 34 -> 42, of which waited for: 18 -> 13; matrix products, arithmetic and copies ran while one was open for 6% -> 7% of each run, Pallas kernels for 21% -> 29%
where the time goes in v2:
time: 256 us; the launch traced here: 255 us
  Pallas kernels  78.2 us (31%)
  starting transfers between devices  76 us (30%)
  waiting for transfers between devices  69.6 us (27%)
  other arithmetic  17 us (7%)
  local copies, waits for them, and re-layouts  11.7 us (5%)
    pallas_call x2, Pallas kernels, attention(): pl.pallas_call(functools.partial(attention_kernel, (local_blocks, group,...  68.5 us
    ppermute x24, waiting for transfers between devices, along(): return lax.ppermute(array, 'seq', pairs)  56.9 us
    ppermute x24, starting transfers between devices, along(): return lax.ppermute(array, 'seq', pairs)  51.4 us
    ppermute x15, waiting for transfers between devices, across(): lax.ppermute(array, 'head', [(i, i ^ k) for i in range(heads)])  12.7 us
    ppermute x15, starting transfers between devices, across(): lax.ppermute(array, 'head', [(i, i ^ k) for i in range(heads)])  10.4 us
    all_to_all x2, starting transfers between devices, column_of(): lax.all_to_all(wide, 'seq', split_axis=0, concat_axis=0, axis_index_group...  8.15 us
    all_to_all x1, starting transfers between devices, shards(): lax.all_to_all(far_sum[:planes].astype(jnp.bfloat16), 'seq', split_axis=0...  5.99 us
    pallas_call x1, Pallas kernels, assemble_queries(): pl.pallas_call(functools.partial(queries_kernel, heads, kv_local), grid_s...  5.56 us
  transfers between devices with their start and end apart: 42, of which 13 were waited for; matrix products, arithmetic and copies ran while one was open for 7% of the time, Pallas kernels for 29%

profile of v2, /device:TPU:0, one launch (start us, length us, event | category | flops | bytes accessed | tf_op | source)
XLA Modules:
  0.0 254.6 jit_solution(2276300056878499055)
XLA Ops:
  0.6 1.3 dynamic_slice.47
  2.6 1.7 slice_bitcast_fusion.2
  4.3 5.9 %collective-permute-start.3 = (bf16[2,2,128,128]{3,2,1,0:T(8,128)(2,1)S(1)}, bf16[2,2,128,128]{3,2,1,0:T(8,128)(2,1)S(1)}, u32[]{:S(2)}, u32[]{:S(2)}) collective-permute-start(bf16[2,2,128,128]{3,2,1,0:T(8,128)(2,1)S(1)} %pad_maximum_fusion.5), channel_id=1, source_target_pairs={{0,16},{1,17},{2,18},{3,19}} | collective-permute-start | bytes 393224 | tf_op jit(solution)/shard_map/in_first4/ppermute | solution.py:308
  10.2 1.1 fusion.23
  11.3 1.3 collective-permute-start
  12.6 0.7 broadcast_in_dim.133
  13.4 3.4 %all-to-all-start.1 = ((bf16[4,2,128,128]{3,2,1,0:T(8,128)(2,1)}), bf16[4,2,128,128]{3,2,1,0:T(8,128)(2,1)S(1)}, u32[]{:S(2)}, u32[]{:S(2)}) async-start(bf16[4,2,128,128]{3,2,1,0:T(8,128)(2,1)} %broadcast_in_dim.133), calls=%async_computation.1 | async-start | bytes 524288 | tf_op jit(solution)/shard_map/in_column0/all_to_all | solution.py:330
  16.8 1.1 pad_maximum_fusion.1.refs_2_
  17.9 3.1 %collective-permute-start.6 = (bf16[2,2048,128]{2,1,0:T(8,128)(2,1)}, bf16[2,2048,128]{2,1,0:T(8,128)(2,1)}, u32[]{:S(2)}, u32[]{:S(2)}) collective-permute-start(bf16[2,2048,128]{2,1,0:T(8,128)(2,1)} %pad_maximum_fusion.1.refs_2_), channel_id=1, source_target_pairs={{0,4},{8,12},{16,20},{24,28},{1,5},{9,13},{17,21},{25,29},{2,6},{1... | collective-permute-start | bytes 3145736 | tf_op jit(solution)/shard_map/in_even0/ppermute | solution.py:308
  21.0 1.1 pad_maximum_fusion.2.refs_2_
  22.1 4.1 %collective-permute-start.4 = (bf16[2,2,128,128]{3,2,1,0:T(8,128)(2,1)S(1)}, bf16[2,2,128,128]{3,2,1,0:T(8,128)(2,1)S(1)}, u32[]{:S(2)}, u32[]{:S(2)}) collective-permute-start(bf16[2,2,128,128]{3,2,1,0:T(8,128)(2,1)S(1)} %broadcast_select_fusion), channel_id=1, source_target_pairs={{0,8},{16,24},{1,9},{17,25},{2,10},{18,26},{3,11},{19,27}} | collective-permute-start | bytes 393224 | tf_op jit(solution)/shard_map/in_first2/ppermute | solution.py:308
  27.0 3.3 %collective-permute-start.1 = (bf16[2,1024,128]{2,1,0:T(8,128)(2,1)}, bf16[2,1024,128]{2,1,0:T(8,128)(2,1)}, u32[]{:S(2)}, u32[]{:S(2)}) collective-permute-start(bf16[2,1024,128]{2,1,0:T(8,128)(2,1)} %get-tuple-element.50), channel_id=1, source_target_pairs={{0,8},{4,12},{8,16},{12,20},{16,24},{20,28},{1,9},{5,13},{9,17},{1... | collective-permute-start | bytes 1572872 | tf_op jit(solution)/shard_map/in_back0_b/ppermute | solution.py:308
  30.3 1.9 collective-permute-done.4
  32.4 1.3 collective-permute-start.7
  33.7 8.9 %collective-permute-done.1.refs_6_ = bf16[2,1024,128]{2,1,0:T(8,128)(2,1)} collective-permute-done((bf16[2,1024,128]{2,1,0:T(8,128)(2,1)}, bf16[2,1024,128]{2,1,0:T(8,128)(2,1)}, u32[]{:S(2)}, u32[]{:S(2)}) %collective-permute-start.1) | collective-permute-done | bytes 524320 | tf_op jit(solution)/shard_map/in_back0_b/ppermute | solution.py:308
  43.4 4.7 %all-to-all-start = ((bf16[4,2,128,128]{3,2,1,0:T(8,128)(2,1)}), bf16[4,2,128,128]{3,2,1,0:T(8,128)(2,1)S(1)}, u32[]{:S(2)}, u32[]{:S(2)}) async-start(bf16[4,2,128,128]{3,2,1,0:T(8,128)(2,1)} %broadcast_in_dim.132), calls=%async_computation | async-start | bytes 524288 | tf_op jit(solution)/shard_map/in_column1/all_to_all | solution.py:330
  48.1 0.9 fusion.38
  49.0 4.7 %collective-permute-start.2 = (bf16[2,1024,128]{2,1,0:T(8,128)(2,1)S(1)}, bf16[2,1024,128]{2,1,0:T(8,128)(2,1)}, u32[]{:S(2)}, u32[]{:S(2)}) collective-permute-start(bf16[2,1024,128]{2,1,0:T(8,128)(2,1)S(1)} %get-tuple-element.104), channel_id=1, source_target_pairs={{0,8},{4,12},{8,16},{12,20},{16,24},{20,28},{1,9},{5,13},{9,17},{1... | collective-permute-start | bytes 1572872 | tf_op jit(solution)/shard_map/in_back1_a/ppermute | solution.py:308
  53.7 1.3 collective-permute-start.8
  55.1 6.3 %collective-permute-start.11 = (bf16[2,2048,128]{2,1,0:T(8,128)(2,1)S(1)}, bf16[2,2048,128]{2,1,0:T(8,128)(2,1)}, u32[]{:S(2)}, u32[]{:S(2)}) collective-permute-start(bf16[2,2048,128]{2,1,0:T(8,128)(2,1)S(1)} %copy-done.7), channel_id=1, source_target_pairs={{0,4},{8,12},{16,20},{24,28},{1,5},{9,13},{17,21},{25,29},{2,6},{1... | collective-permute-start | bytes 3145736 | tf_op jit(solution)/shard_map/in_even1/ppermute | solution.py:308
  61.5 1.3 collective-permute-done.2.refs_5_
  62.8 5.0 %collective-permute-start.10 = (bf16[2,1024,128]{2,1,0:T(8,128)(2,1)}, bf16[2,1024,128]{2,1,0:T(8,128)(2,1)S(1)}, u32[]{:S(2)}, u32[]{:S(2)}) collective-permute-start(bf16[2,1024,128]{2,1,0:T(8,128)(2,1)} %get-tuple-element.56), channel_id=1, source_target_pairs={{0,8},{4,12},{8,16},{12,20},{16,24},{20,28},{1,9},{5,13},{9,17},{1... | collective-permute-start | bytes 1572872 | tf_op jit(solution)/shard_map/in_back1_b/ppermute | solution.py:308
  68.5 2.2 collective-permute-done.8.refs_9_
  70.8 1.3 collective-permute-start.12
  72.1 34.3 %attention.2 = (bf16[512,512]{1,0:T(8,128)(2,1)S(1)}, bf16[512,512]{1,0:T(8,128)(2,1)S(1)}, bf16[512,512]{1,0:T(8,128)(2,1)S(1)}, bf16[512,512]{1,0:T(8,128)(2,1...) custom-call(s32[2]{0:T(128)S(1)} %pad_add_fusion.place, ...), custom_call_target="tpu_custom_call" | custom-call | flops 32212254720 | bytes 20971520 | tf_op jit(solution)/shard_map/attention/pallas_call | solution.py:199
  106.4 0.8 copy-done
  107.2 3.1 %collective-permute-start.18 = (bf16[2,2048,128]{2,1,0:T(8,128)(2,1)}, bf16[2,2048,128]{2,1,0:T(8,128)(2,1)S(1)}, u32[]{:S(2)}, u32[]{:S(2)}) collective-permute-start(bf16[2,2048,128]{2,1,0:T(8,128)(2,1)} %get-tuple-element.71), channel_id=1, source_target_pairs={{0,4},{4,0},{8,12},{12,8},{16,20},{20,16},{24,28},{28,24},{1,5},{5... | collective-permute-start | bytes 3145736 | tf_op jit(solution)/shard_map/out_pair0/ppermute | solution.py:308
  110.3 1.6 collective-permute-start.15
  112.7 34.2 %attention.3 = (bf16[512,512]{1,0:T(8,128)(2,1)S(1)}, bf16[512,512]{1,0:T(8,128)(2,1)S(1)}, bf16[512,512]{1,0:T(8,128)(2,1)S(1)}, bf16[512,512]{1,0:T(8,128)(2,1...) custom-call(s32[2]{0:T(128)S(1)} %pad_add_fusion.place, ...), custom_call_target="tpu_custom_call" | custom-call | flops 32212254720 | bytes 20971520 | tf_op jit(solution)/shard_map/attention/pallas_call | solution.py:199
  147.0 0.8 copy-done.1
  147.8 1.7 collective-permute-start.19
  149.7 1.6 collective-permute-start.20
  151.2 1.3 collective-permute-start.26
  152.5 6.0 %collective-permute-done.19 = bf16[5,2,128,128]{3,2,1,0:T(8,128)(2,1)} collective-permute-done((bf16[5,2,128,128]{3,2,1,0:T(8,128)(2,1)S(1)}, bf16[5,2,128,128]{3,2,1,0:T(8,128)(2,1)}, u32[]{:S(2)}, u32[]{:S(2)}) %collective-permute-start.19) | collective-permute-done | bytes 327712 | tf_op jit(solution)/shard_map/out_far_pair1/ppermute | solution.py:308
  158.6 1.0 add_bitcast_fusion
  159.6 1.3 collective-permute-start.24
  161.0 1.3 fusion.3
  162.3 1.4 collective-permute-start.23
  163.8 0.9 copy.23
  164.6 6.0 %all-to-all-start.2 = ((bf16[4,2,2,128,128]{4,3,2,1,0:T(8,128)(2,1)}), bf16[4,2,2,128,128]{4,3,2,1,0:T(8,128)(2,1)}, u32[]{:S(2)}, u32[]{:S(2)}) async-start(bf16[4,2,2,128,128]{4,3,2,1,0:T(8,128)(2,1)} %copy.23), calls=%async_computation.2 | async-start | bytes 1048576 | tf_op jit(solution)/shard_map/out_far/all_to_all | solution.py:391
  170.7 1.4 collective-permute-start.25
  172.2 1.2 collective-permute-start.22
  173.4 2.4 fusion.7
  175.8 28.2 %collective-permute-done.25 = bf16[2,2,128,128]{3,2,1,0:T(8,128)(2,1)S(1)} collective-permute-done((bf16[2,2,128,128]{3,2,1,0:T(8,128)(2,1)S(1)}, bf16[2,2,128,128]{3,2,1,0:T(8,128)(2,1)S(1)}, u32[]{:S(2)}, u32[]{:S(2)}) %collective-permute-start.25) | collective-permute-done | bytes 131104 | tf_op jit(solution)/shard_map/out_first4/ppermute | solution.py:308
  204.0 1.3 collective-permute-start.27
  205.5 1.1 convert_select_fusion.2
  206.6 1.5 collective-permute-start.29
  208.1 1.6 fusion.1
  209.7 1.1 convert_reduce_fusion
  211.7 0.8 dynamic-slice_bitcast_fusion
  212.5 1.3 collective-permute-start.31
  215.0 6.1 %collective-permute-done.27 = bf16[2,1024,128]{2,1,0:T(8,128)(2,1)} collective-permute-done((bf16[2,1024,128]{2,1,0:T(8,128)(2,1)}, bf16[2,1024,128]{2,1,0:T(8,128)(2,1)}, u32[]{:S(2)}, u32[]{:S(2)}) %collective-permute-start.27) | collective-permute-done | bytes 524320 | tf_op jit(solution)/shard_map/out_onward1_0/ppermute | solution.py:308
  221.6 4.8 %collective-permute-done.32.refs_9_ = bf16[2,512,128]{2,1,0:T(8,128)(2,1)S(1)} collective-permute-done((bf16[2,512,128]{2,1,0:T(8,128)(2,1)S(1)}, bf16[2,512,128]{2,1,0:T(8,128)(2,1)S(1)}, u32[]{:S(2)}, u32[]{:S(2)}) %collective-permute-start.32) | collective-permute-done | bytes 262176 | tf_op jit(solution)/shard_map/out_pairs0_0_3/ppermute | solution.py:312
  226.4 2.2 collective-permute-done.29
  228.7 1.4 fusion.21
  230.1 0.8 dynamic-slice_bitcast_fusion.8
  230.9 1.8 collective-permute-start.34
  232.8 5.6 %assemble_queries.1 = bf16[512,4096]{1,0:T(8,128)(2,1)} custom-call(s32[2]{0:T(128)} %copy-done.2, bf16[512,512]{1,0:T(8,128)(2,1)} %copy-done, bf16[512,512]{1,0:T(8,128)(2,1)} %copy-done.1, bf16[512,512]{1,0:T(8,128)(2,1)} %copy-done.13, bf16[512,512]{1,0:T(8,128)(2,1)} %copy-done.16, bf16[512,512]{1,0:T(8,128)(2,1)} %copy-done.14, ...), custom_call_target="tpu_custom_call" | custom-call | tf_op jit(solution)/shard_map/assemble_queries/pallas_call | solution.py:244
  238.4 1.2 collective-permute-done.35.refs_10_
  239.6 1.4 fusion.16
  241.9 1.7 collective-permute-start.37
  243.7 4.6 %collective-permute-done.37.refs_8_ = bf16[2,256,128]{2,1,0:T(8,128)(2,1)S(1)} collective-permute-done((bf16[2,256,128]{2,1,0:T(8,128)(2,1)S(1)}, bf16[2,256,128]{2,1,0:T(8,128)(2,1)S(1)}, u32[]{:S(2)}, u32[]{:S(2)}) %collective-permute-start.37) | collective-permute-done | bytes 131104 | tf_op jit(solution)/shard_map/out_pairs1_1_2/ppermute | solution.py:312
  248.3 1.6 collective-permute-done.38.refs_11_
  250.5 4.1 %assemble_pairs.1 = (bf16[512,1024]{1,0:T(8,128)(2,1)}, bf16[512,1024]{1,0:T(8,128)(2,1)}) custom-call(s32[2]{0:T(128)} %copy-done.2, bf16[2,512,128]{2,1,0:T(8,128)(2,1)} %get-tuple-element.102.refs_0_, bf16[2,256,128]{2,1,0:T(8,128)(2,1)} %get-tuple-element.122.refs_1_, bf16[2,256,128]{2,1,0:T(8,128)(2,1)} %get-tuple-element.118.refs_2_, ...), custom_call_target="tpu_custom_call" | custom-call | tf_op jit(solution)/shard_map/assemble_pairs/pallas_call | solution.py:275
  (138 shorter events, 8.3 us)
Async XLA Ops:
  4.3 17.8 %collective-permute-start.3 = (bf16[2,2,128,128]{3,2,1,0:T(8,128)(2,1)S(1)}, bf16[2,2,128,128]{3,2,1,0:T(8,128)(2,1)S(1)}, u32[]{:S(2)}, u32[]{:S(2)}) collective-permute-start(bf16[2,2,128,128]{3,2,1,0:T(8,128)(2,1)S(1)} %pad_maximum_fusion.5), channel_id=1, source_target_pairs={{0,16},{1,17},{2,18},{3,19}} | collective-permute-start | bytes 393224 | tf_op jit(solution)/shard_map/in_first4/ppermute | solution.py:308
  11.3 15.7 %collective-permute-start = (bf16[2,1024,128]{2,1,0:T(8,128)(2,1)}, bf16[2,1024,128]{2,1,0:T(8,128)(2,1)S(1)}, u32[]{:S(2)}, u32[]{:S(2)}) collective-permute-start(bf16[2,1024,128]{2,1,0:T(8,128)(2,1)} %get-tuple-element.109), channel_id=1, source_target_pairs={{0,8},{4,12},{8,16},{12,20},{16,24},{20,28},{1,9},{5,13},{9,17},{1... | collective-permute-start | bytes 1572872 | tf_op jit(solution)/shard_map/in_back0_a/ppermute | solution.py:308
  13.4 18.9 %all-to-all-start.1 = ((bf16[4,2,128,128]{3,2,1,0:T(8,128)(2,1)}), bf16[4,2,128,128]{3,2,1,0:T(8,128)(2,1)S(1)}, u32[]{:S(2)}, u32[]{:S(2)}) async-start(bf16[4,2,128,128]{3,2,1,0:T(8,128)(2,1)} %broadcast_in_dim.133), calls=%async_computation.1 | async-start | bytes 524288 | tf_op jit(solution)/shard_map/in_column0/all_to_all | solution.py:330
  16.8 10.1 %copy-start.27 = (s32[16,2]{0,1:T(2,128)S(1)}, s32[16,2]{0,1:T(2,128)}, u32[]{:S(2)}) copy-start(s32[16,2]{0,1:T(2,128)} %param.12) | copy-start | bytes 388
  16.8 10.2 %copy-start.28 = (s32[16,2]{0,1:T(2,128)S(1)}, s32[16,2]{0,1:T(2,128)}, u32[]{:S(2)}) copy-start(s32[16,2]{0,1:T(2,128)} %param.13) | copy-start | bytes 388
  17.9 49.9 %collective-permute-start.6 = (bf16[2,2048,128]{2,1,0:T(8,128)(2,1)}, bf16[2,2048,128]{2,1,0:T(8,128)(2,1)}, u32[]{:S(2)}, u32[]{:S(2)}) collective-permute-start(bf16[2,2048,128]{2,1,0:T(8,128)(2,1)} %pad_maximum_fusion.1.refs_2_), channel_id=1, source_target_pairs={{0,4},{8,12},{16,20},{24,28},{1,5},{9,13},{17,21},{25,29},{2,6},{1... | collective-permute-start | bytes 3145736 | tf_op jit(solution)/shard_map/in_even0/ppermute | solution.py:308
  22.1 26.0 %copy-start.7 = (bf16[2,2048,128]{2,1,0:T(8,128)(2,1)S(1)}, bf16[2,2048,128]{2,1,0:T(8,128)(2,1)}, u32[]{:S(2)}) copy-start(bf16[2,2048,128]{2,1,0:T(8,128)(2,1)} %pad_maximum_fusion.2.refs_2_) | copy-start | bytes 3145732
  22.1 10.1 %collective-permute-start.4 = (bf16[2,2,128,128]{3,2,1,0:T(8,128)(2,1)S(1)}, bf16[2,2,128,128]{3,2,1,0:T(8,128)(2,1)S(1)}, u32[]{:S(2)}, u32[]{:S(2)}) collective-permute-start(bf16[2,2,128,128]{3,2,1,0:T(8,128)(2,1)S(1)} %broadcast_select_fusion), channel_id=1, source_target_pairs={{0,8},{16,24},{1,9},{17,25},{2,10},{18,26},{3,11},{19,27}} | collective-permute-start | bytes 393224 | tf_op jit(solution)/shard_map/in_first2/ppermute | solution.py:308
  27.0 15.6 %collective-permute-start.1 = (bf16[2,1024,128]{2,1,0:T(8,128)(2,1)}, bf16[2,1024,128]{2,1,0:T(8,128)(2,1)}, u32[]{:S(2)}, u32[]{:S(2)}) collective-permute-start(bf16[2,1024,128]{2,1,0:T(8,128)(2,1)} %get-tuple-element.50), channel_id=1, source_target_pairs={{0,8},{4,12},{8,16},{12,20},{16,24},{20,28},{1,9},{5,13},{9,17},{1... | collective-permute-start | bytes 1572872 | tf_op jit(solution)/shard_map/in_back0_b/ppermute | solution.py:308
  32.2 39.8 %copy-start.3 = (s32[8]{0:T(128)S(1)}, s32[8]{0:T(128)}, u32[]{:S(2)}) copy-start(s32[8]{0:T(128)} %vertical.3) | copy-start | bytes 100
  32.3 21.4 %collective-permute-start.5 = (bf16[5,2,128,128]{3,2,1,0:T(8,128)(2,1)S(1)}, bf16[5,2,128,128]{3,2,1,0:T(8,128)(2,1)S(1)}, u32[]{:S(2)}, u32[]{:S(2)}) collective-permute-start(bf16[5,2,128,128]{3,2,1,0:T(8,128)(2,1)S(1)} %pad_maximum_fusion.4.refs_3_), channel_id=1, source_target_pairs={{0,4},{4,0},{8,12},{12,8},{16,20},{20,16},{24,28},{28,24},{1,5},{5... | collective-permute-start | bytes 983048 | tf_op jit(solution)/shard_map/in_column_pair0/ppermute | solution.py:308
  32.4 79.9 %copy-start.2 = (s32[2]{0:T(128)}, s32[2]{0:T(128)S(1)}, u32[]{:S(2)}) copy-start(s32[2]{0:T(128)S(1)} %pad_add_fusion.place) | copy-start | bytes 28
  32.4 30.3 %collective-permute-start.7 = (bf16[2,1024,128]{2,1,0:T(8,128)(2,1)S(1)}, bf16[2,1024,128]{2,1,0:T(8,128)(2,1)}, u32[]{:S(2)}, u32[]{:S(2)}) collective-permute-start(bf16[2,1024,128]{2,1,0:T(8,128)(2,1)S(1)} %collective-permute-done.refs_5_), channel_id=1, source_target_pairs={{4,0},{12,8},{20,16},{28,24},{5,1},{13,9},{21,17},{29,25},{6,2},{1... | collective-permute-start | bytes 1572872 | tf_op jit(solution)/shard_map/in_odd0_a/ppermute | solution.py:308
  43.4 18.1 %all-to-all-start = ((bf16[4,2,128,128]{3,2,1,0:T(8,128)(2,1)}), bf16[4,2,128,128]{3,2,1,0:T(8,128)(2,1)S(1)}, u32[]{:S(2)}, u32[]{:S(2)}) async-start(bf16[4,2,128,128]{3,2,1,0:T(8,128)(2,1)} %broadcast_in_dim.132), calls=%async_computation | async-start | bytes 524288 | tf_op jit(solution)/shard_map/in_column1/all_to_all | solution.py:330
  49.0 13.8 %collective-permute-start.2 = (bf16[2,1024,128]{2,1,0:T(8,128)(2,1)S(1)}, bf16[2,1024,128]{2,1,0:T(8,128)(2,1)}, u32[]{:S(2)}, u32[]{:S(2)}) collective-permute-start(bf16[2,1024,128]{2,1,0:T(8,128)(2,1)S(1)} %get-tuple-element.104), channel_id=1, source_target_pairs={{0,8},{4,12},{8,16},{12,20},{16,24},{20,28},{1,9},{5,13},{9,17},{1... | collective-permute-start | bytes 1572872 | tf_op jit(solution)/shard_map/in_back1_a/ppermute | solution.py:308
  53.7 17.1 %collective-permute-start.8 = (bf16[2,1024,128]{2,1,0:T(8,128)(2,1)}, bf16[2,1024,128]{2,1,0:T(8,128)(2,1)}, u32[]{:S(2)}, u32[]{:S(2)}) collective-permute-start(bf16[2,1024,128]{2,1,0:T(8,128)(2,1)} %collective-permute-done.1.refs_6_), channel_id=1, source_target_pairs={{4,0},{12,8},{20,16},{28,24},{5,1},{13,9},{21,17},{29,25},{6,2},{1... | collective-permute-start | bytes 1572872 | tf_op jit(solution)/shard_map/in_odd0_b/ppermute | solution.py:308
  55.1 57.1 %collective-permute-start.11 = (bf16[2,2048,128]{2,1,0:T(8,128)(2,1)S(1)}, bf16[2,2048,128]{2,1,0:T(8,128)(2,1)}, u32[]{:S(2)}, u32[]{:S(2)}) collective-permute-start(bf16[2,2048,128]{2,1,0:T(8,128)(2,1)S(1)} %copy-done.7), channel_id=1, source_target_pairs={{0,4},{8,12},{16,20},{24,28},{1,5},{9,13},{17,21},{25,29},{2,6},{1... | collective-permute-start | bytes 3145736 | tf_op jit(solution)/shard_map/in_even1/ppermute | solution.py:308
  62.8 44.4 %collective-permute-start.9 = (bf16[5,2,128,128]{3,2,1,0:T(8,128)(2,1)S(1)}, bf16[5,2,128,128]{3,2,1,0:T(8,128)(2,1)S(1)}, u32[]{:S(2)}, u32[]{:S(2)}) collective-permute-start(bf16[5,2,128,128]{3,2,1,0:T(8,128)(2,1)S(1)} %pad_maximum_fusion.3.refs_3_), channel_id=1, source_target_pairs={{0,4},{4,0},{8,12},{12,8},{16,20},{20,16},{24,28},{28,24},{1,5},{5... | collective-permute-start | bytes 983048 | tf_op jit(solution)/shard_map/in_column_pair1/ppermute | solution.py:308
  62.8 47.5 %collective-permute-start.10 = (bf16[2,1024,128]{2,1,0:T(8,128)(2,1)}, bf16[2,1024,128]{2,1,0:T(8,128)(2,1)S(1)}, u32[]{:S(2)}, u32[]{:S(2)}) collective-permute-start(bf16[2,1024,128]{2,1,0:T(8,128)(2,1)} %get-tuple-element.56), channel_id=1, source_target_pairs={{0,8},{4,12},{8,16},{12,20},{16,24},{20,28},{1,9},{5,13},{9,17},{1... | collective-permute-start | bytes 1572872 | tf_op jit(solution)/shard_map/in_back1_b/ppermute | solution.py:308
  67.8 42.5 %collective-permute-start.13 = (bf16[2,1024,128]{2,1,0:T(8,128)(2,1)}, bf16[2,1024,128]{2,1,0:T(8,128)(2,1)S(1)}, u32[]{:S(2)}, u32[]{:S(2)}) collective-permute-start(bf16[2,1024,128]{2,1,0:T(8,128)(2,1)} %get-tuple-element.56), channel_id=1, source_target_pairs={{4,8},{12,16},{20,24},{5,9},{13,17},{21,25},{6,10},{14,18},{22,26}... | collective-permute-start | bytes 1572872 | tf_op jit(solution)/shard_map/in_odd1_b/ppermute | solution.py:308
  70.8 41.1 %collective-permute-start.12 = (bf16[2,1024,128]{2,1,0:T(8,128)(2,1)}, bf16[2,1024,128]{2,1,0:T(8,128)(2,1)S(1)}, u32[]{:S(2)}, u32[]{:S(2)}) collective-permute-start(bf16[2,1024,128]{2,1,0:T(8,128)(2,1)} %collective-permute-done.2.refs_5_), channel_id=1, source_target_pairs={{4,0},{12,8},{20,16},{28,24},{5,1},{13,9},{21,17},{29,25},{6,2},{1... | collective-permute-start | bytes 1572872 | tf_op jit(solution)/shard_map/in_odd1_a/ppermute | solution.py:308
  107.2 40.6 %collective-permute-start.18 = (bf16[2,2048,128]{2,1,0:T(8,128)(2,1)}, bf16[2,2048,128]{2,1,0:T(8,128)(2,1)S(1)}, u32[]{:S(2)}, u32[]{:S(2)}) collective-permute-start(bf16[2,2048,128]{2,1,0:T(8,128)(2,1)} %get-tuple-element.71), channel_id=1, source_target_pairs={{0,4},{4,0},{8,12},{12,8},{16,20},{20,16},{24,28},{28,24},{1,5},{5... | collective-permute-start | bytes 3145736 | tf_op jit(solution)/shard_map/out_pair0/ppermute | solution.py:308
  110.3 2.0 copy-start.29
  110.3 37.5 %collective-permute-start.14 = (bf16[512,512]{1,0:T(8,128)(2,1)S(1)}, bf16[512,512]{1,0:T(8,128)(2,1)S(1)}, u32[]{:S(2)}, u32[]{:S(2)}) collective-permute-start(bf16[512,512]{1,0:T(8,128)(2,1)S(1)} %get-tuple-element.65), channel_id=1, source_target_pairs={{0,1},{1,0},{2,3},{3,2},{4,5},{5,4},{6,7},{7,6},{8,9},{9,8},{10,11... | collective-permute-start | bytes 1572872 | tf_op jit(solution)/shard_map/out_query0_1/ppermute | solution.py:312
  110.3 37.4 %collective-permute-start.15 = (bf16[512,512]{1,0:T(8,128)(2,1)S(1)}, bf16[512,512]{1,0:T(8,128)(2,1)S(1)}, u32[]{:S(2)}, u32[]{:S(2)}) collective-permute-start(bf16[512,512]{1,0:T(8,128)(2,1)S(1)} %get-tuple-element.66), channel_id=1, source_target_pairs={{0,2},{1,3},{2,0},{3,1},{4,6},{5,7},{6,4},{7,5},{8,10},{9,11},{10,... | collective-permute-start | bytes 1572872 | tf_op jit(solution)/shard_map/out_query0_2/ppermute | solution.py:312
  111.9 35.9 %collective-permute-start.16 = (bf16[512,512]{1,0:T(8,128)(2,1)S(1)}, bf16[512,512]{1,0:T(8,128)(2,1)S(1)}, u32[]{:S(2)}, u32[]{:S(2)}) collective-permute-start(bf16[512,512]{1,0:T(8,128)(2,1)S(1)} %get-tuple-element.67), channel_id=1, source_target_pairs={{0,3},{1,2},{2,1},{3,0},{4,7},{5,6},{6,5},{7,4},{8,11},{9,10},{10,... | collective-permute-start | bytes 1572872 | tf_op jit(solution)/shard_map/out_query0_3/ppermute | solution.py:312
  112.2 35.6 %collective-permute-start.17 = (bf16[5,2,128,128]{3,2,1,0:T(8,128)(2,1)S(1)}, bf16[5,2,128,128]{3,2,1,0:T(8,128)(2,1)S(1)}, u32[]{:S(2)}, u32[]{:S(2)}) collective-permute-start(bf16[5,2,128,128]{3,2,1,0:T(8,128)(2,1)S(1)} %get-tuple-element.69), channel_id=1, source_target_pairs={{0,4},{4,0},{8,12},{12,8},{16,20},{20,16},{24,28},{28,24},{1,5},{5... | collective-permute-start | bytes 983048 | tf_op jit(solution)/shard_map/out_far_pair0/ppermute | solution.py:308
  147.8 10.7 %collective-permute-start.19 = (bf16[5,2,128,128]{3,2,1,0:T(8,128)(2,1)S(1)}, bf16[5,2,128,128]{3,2,1,0:T(8,128)(2,1)}, u32[]{:S(2)}, u32[]{:S(2)}) collective-permute-start(bf16[5,2,128,128]{3,2,1,0:T(8,128)(2,1)S(1)} %get-tuple-element.83), channel_id=1, source_target_pairs={{0,4},{4,0},{8,12},{12,8},{16,20},{20,16},{24,28},{28,24},{1,5},{5... | collective-permute-start | bytes 983048 | tf_op jit(solution)/shard_map/out_far_pair1/ppermute | solution.py:308
  149.5 11.4 %copy-start.5 = (bf16[2,2048,128]{2,1,0:T(8,128)(2,1)S(1)}, bf16[2,2048,128]{2,1,0:T(8,128)(2,1)}, u32[]{:S(2)}) copy-start(bf16[2,2048,128]{2,1,0:T(8,128)(2,1)} %copy-done.4) | copy-start | bytes 3145732
  149.6 11.4 %copy-start.12 = (bf16[2,2048,128]{2,1,0:T(8,128)(2,1)S(1)}, bf16[2,2048,128]{2,1,0:T(8,128)(2,1)}, u32[]{:S(2)}) copy-start(bf16[2,2048,128]{2,1,0:T(8,128)(2,1)} %get-tuple-element.75) | copy-start | bytes 3145732
  149.7 22.5 %collective-permute-start.20 = (bf16[512,512]{1,0:T(8,128)(2,1)S(1)}, bf16[512,512]{1,0:T(8,128)(2,1)}, u32[]{:S(2)}, u32[]{:S(2)}) collective-permute-start(bf16[512,512]{1,0:T(8,128)(2,1)S(1)} %get-tuple-element.80), channel_id=1, source_target_pairs={{0,2},{1,3},{2,0},{3,1},{4,6},{5,7},{6,4},{7,5},{8,10},{9,11},{10,... | collective-permute-start | bytes 1572872 | tf_op jit(solution)/shard_map/out_query1_2/ppermute | solution.py:312
  151.2 22.2 %collective-permute-start.26 = (bf16[2,1024,128]{2,1,0:T(8,128)(2,1)S(1)}, bf16[2,1024,128]{2,1,0:T(8,128)(2,1)}, u32[]{:S(2)}, u32[]{:S(2)}) collective-permute-start(bf16[2,1024,128]{2,1,0:T(8,128)(2,1)S(1)} %get-tuple-element.76), channel_id=1, source_target_pairs={{0,4},{4,0},{8,12},{12,8},{16,20},{20,16},{24,28},{28,24},{1,5},{5... | collective-permute-start | bytes 1572872 | tf_op jit(solution)/shard_map/out_pair1_0/ppermute | solution.py:308
  159.6 11.0 %collective-permute-start.24 = (bf16[2,2,128,128]{3,2,1,0:T(8,128)(2,1)S(1)}, bf16[2,2,128,128]{3,2,1,0:T(8,128)(2,1)S(1)}, u32[]{:S(2)}, u32[]{:S(2)}) collective-permute-start(bf16[2,2,128,128]{3,2,1,0:T(8,128)(2,1)S(1)} %get-tuple-element.97), channel_id=1, source_target_pairs={{8,0},{24,16},{9,1},{25,17},{10,2},{26,18},{11,3},{27,19}} | collective-permute-start | bytes 393224 | tf_op jit(solution)/shard_map/out_first2/ppermute | solution.py:308
  162.3 11.1 %copy-start.19 = (bf16[2,1024,128]{2,1,0:T(8,128)(2,1)S(1)}, bf16[2,1024,128]{2,1,0:T(8,128)(2,1)}, u32[]{:S(2)}) copy-start(bf16[2,1024,128]{2,1,0:T(8,128)(2,1)} %get-tuple-element.88) | copy-start | bytes 1572868
  162.3 45.8 %collective-permute-start.23 = (bf16[2,2048,128]{2,1,0:T(8,128)(2,1)}, bf16[2,2048,128]{2,1,0:T(8,128)(2,1)}, u32[]{:S(2)}, u32[]{:S(2)}) collective-permute-start(bf16[2,2048,128]{2,1,0:T(8,128)(2,1)} %fusion.3), channel_id=1, source_target_pairs={{8,0},{12,4},{16,8},{20,12},{24,16},{28,20},{9,1},{13,5},{17,9},{2... | collective-permute-start | bytes 3145736 | tf_op jit(solution)/shard_map/out_onward0/ppermute | solution.py:308
  164.6 45.0 %all-to-all-start.2 = ((bf16[4,2,2,128,128]{4,3,2,1,0:T(8,128)(2,1)}), bf16[4,2,2,128,128]{4,3,2,1,0:T(8,128)(2,1)}, u32[]{:S(2)}, u32[]{:S(2)}) async-start(bf16[4,2,2,128,128]{4,3,2,1,0:T(8,128)(2,1)} %copy.23), calls=%async_computation.2 | async-start | bytes 1048576 | tf_op jit(solution)/shard_map/out_far/all_to_all | solution.py:391
  170.7 34.8 %copy-start.18 = (bf16[2,1024,128]{2,1,0:T(8,128)(2,1)S(1)}, bf16[2,1024,128]{2,1,0:T(8,128)(2,1)}, u32[]{:S(2)}) copy-start(bf16[2,1024,128]{2,1,0:T(8,128)(2,1)} %get-tuple-element.89) | copy-start | bytes 1572868
  170.7 33.4 %collective-permute-start.25 = (bf16[2,2,128,128]{3,2,1,0:T(8,128)(2,1)S(1)}, bf16[2,2,128,128]{3,2,1,0:T(8,128)(2,1)S(1)}, u32[]{:S(2)}, u32[]{:S(2)}) collective-permute-start(bf16[2,2,128,128]{3,2,1,0:T(8,128)(2,1)S(1)} %fusion.26), channel_id=1, source_target_pairs={{16,0},{17,1},{18,2},{19,3}} | collective-permute-start | bytes 393224 | tf_op jit(solution)/shard_map/out_first4/ppermute | solution.py:308
  172.1 33.3 %collective-permute-start.21 = (bf16[512,512]{1,0:T(8,128)(2,1)S(1)}, bf16[512,512]{1,0:T(8,128)(2,1)S(1)}, u32[]{:S(2)}, u32[]{:S(2)}) collective-permute-start(bf16[512,512]{1,0:T(8,128)(2,1)S(1)} %get-tuple-element.85), channel_id=1, source_target_pairs={{0,1},{1,0},{2,3},{3,2},{4,5},{5,4},{6,7},{7,6},{8,9},{9,8},{10,11... | collective-permute-start | bytes 1572872 | tf_op jit(solution)/shard_map/out_query1_1/ppermute | solution.py:312
  172.2 33.2 %collective-permute-start.22 = (bf16[512,512]{1,0:T(8,128)(2,1)S(1)}, bf16[512,512]{1,0:T(8,128)(2,1)S(1)}, u32[]{:S(2)}, u32[]{:S(2)}) collective-permute-start(bf16[512,512]{1,0:T(8,128)(2,1)S(1)} %get-tuple-element.86), channel_id=1, source_target_pairs={{0,3},{1,2},{2,1},{3,0},{4,7},{5,6},{6,5},{7,4},{8,11},{9,10},{10,... | collective-permute-start | bytes 1572872 | tf_op jit(solution)/shard_map/out_query1_3/ppermute | solution.py:312
  173.4 32.0 %collective-permute-start.28 = (bf16[2,1024,128]{2,1,0:T(8,128)(2,1)}, bf16[2,1024,128]{2,1,0:T(8,128)(2,1)S(1)}, u32[]{:S(2)}, u32[]{:S(2)}) collective-permute-start(bf16[2,1024,128]{2,1,0:T(8,128)(2,1)} %get-tuple-element.90), channel_id=1, source_target_pairs={{0,4},{4,0},{8,12},{12,8},{16,20},{20,16},{24,28},{28,24},{1,5},{5... | collective-permute-start | bytes 1572872 | tf_op jit(solution)/shard_map/out_pair1_1/ppermute | solution.py:308
  175.8 32.3 %copy-start.6 = (bf16[2,2048,128]{2,1,0:T(8,128)(2,1)S(1)}, bf16[2,2048,128]{2,1,0:T(8,128)(2,1)}, u32[]{:S(2)}) copy-start(bf16[2,2048,128]{2,1,0:T(8,128)(2,1)} %copy-done.4) | copy-start | bytes 3145732
  175.8 32.3 %copy-start.9 = (f32[2,2048,128]{2,1,0:T(8,128)S(1)}, f32[2,2048,128]{2,1,0:T(8,128)}, u32[]{:S(2)}) copy-start(f32[2,2048,128]{2,1,0:T(8,128)} %get-tuple-element.73) | copy-start | bytes 6291460
  204.0 17.1 %collective-permute-start.27 = (bf16[2,1024,128]{2,1,0:T(8,128)(2,1)}, bf16[2,1024,128]{2,1,0:T(8,128)(2,1)}, u32[]{:S(2)}, u32[]{:S(2)}) collective-permute-start(bf16[2,1024,128]{2,1,0:T(8,128)(2,1)} %get-tuple-element.125), channel_id=1, source_target_pairs={{8,0},{12,4},{16,8},{20,12},{24,16},{28,20},{9,1},{13,5},{17,9},{2... | collective-permute-start | bytes 1572872 | tf_op jit(solution)/shard_map/out_onward1_0/ppermute | solution.py:308
  205.4 2.6 %copy-start.16 = (bf16[512,512]{1,0:T(8,128)(2,1)}, bf16[512,512]{1,0:T(8,128)(2,1)S(1)}, u32[]{:S(2)}) copy-start(bf16[512,512]{1,0:T(8,128)(2,1)S(1)} %collective-permute-done.21.refs_3_) | copy-start | bytes 1572868
  205.4 2.6 %copy-start.17 = (bf16[512,512]{1,0:T(8,128)(2,1)}, bf16[512,512]{1,0:T(8,128)(2,1)S(1)}, u32[]{:S(2)}) copy-start(bf16[512,512]{1,0:T(8,128)(2,1)S(1)} %collective-permute-done.22.refs_7_) | copy-start | bytes 1572868
  206.6 22.1 %collective-permute-start.29 = (bf16[2,1024,128]{2,1,0:T(8,128)(2,1)}, bf16[2,1024,128]{2,1,0:T(8,128)(2,1)}, u32[]{:S(2)}, u32[]{:S(2)}) collective-permute-start(bf16[2,1024,128]{2,1,0:T(8,128)(2,1)} %get-tuple-element.124), channel_id=1, source_target_pairs={{8,0},{12,4},{16,8},{20,12},{24,16},{28,20},{9,1},{13,5},{17,9},{2... | collective-permute-start | bytes 1572872 | tf_op jit(solution)/shard_map/out_onward1_1/ppermute | solution.py:308
  210.9 17.7 %copy-start.10 = (f32[2,2048,128]{2,1,0:T(8,128)S(1)}, f32[2,2048,128]{2,1,0:T(8,128)}, u32[]{:S(2)}) copy-start(f32[2,2048,128]{2,1,0:T(8,128)} %get-tuple-element.87) | copy-start | bytes 6291460
  211.7 17.0 %copy-start.8 = (f32[2,1024,128]{2,1,0:T(8,128)S(1)}, f32[2,1024,128]{2,1,0:T(8,128)}, u32[]{:S(2)}) copy-start(f32[2,1024,128]{2,1,0:T(8,128)} %get-tuple-element.126) | copy-start | bytes 3145732
  212.5 8.6 %collective-permute-start.30 = (bf16[2,512,128]{2,1,0:T(8,128)(2,1)S(1)}, bf16[2,512,128]{2,1,0:T(8,128)(2,1)S(1)}, u32[]{:S(2)}, u32[]{:S(2)}) collective-permute-start(bf16[2,512,128]{2,1,0:T(8,128)(2,1)S(1)} %get-tuple-element.101), channel_id=1, source_target_pairs={{0,1},{1,0},{2,3},{3,2},{4,5},{5,4},{6,7},{7,6},{8,9},{9,8},{10,11... | collective-permute-start | bytes 786440 | tf_op jit(solution)/shard_map/out_pairs0_0_1/ppermute | solution.py:312
  212.5 9.1 %collective-permute-start.31 = (bf16[2,512,128]{2,1,0:T(8,128)(2,1)S(1)}, bf16[2,512,128]{2,1,0:T(8,128)(2,1)S(1)}, u32[]{:S(2)}, u32[]{:S(2)}) collective-permute-start(bf16[2,512,128]{2,1,0:T(8,128)(2,1)S(1)} %get-tuple-element.100), channel_id=1, source_target_pairs={{0,2},{1,3},{2,0},{3,1},{4,6},{5,7},{6,4},{7,5},{8,10},{9,11},{10,... | collective-permute-start | bytes 786440 | tf_op jit(solution)/shard_map/out_pairs0_0_2/ppermute | solution.py:312
  213.8 12.6 %collective-permute-start.32 = (bf16[2,512,128]{2,1,0:T(8,128)(2,1)S(1)}, bf16[2,512,128]{2,1,0:T(8,128)(2,1)S(1)}, u32[]{:S(2)}, u32[]{:S(2)}) collective-permute-start(bf16[2,512,128]{2,1,0:T(8,128)(2,1)S(1)} %get-tuple-element.99), channel_id=1, source_target_pairs={{0,3},{1,2},{2,1},{3,0},{4,7},{5,6},{6,5},{7,4},{8,11},{9,10},{10,... | collective-permute-start | bytes 786440 | tf_op jit(solution)/shard_map/out_pairs0_0_3/ppermute | solution.py:312
  221.1 7.6 %copy-start.20 = (bf16[2,512,128]{2,1,0:T(8,128)(2,1)}, bf16[2,512,128]{2,1,0:T(8,128)(2,1)S(1)}, u32[]{:S(2)}) copy-start(bf16[2,512,128]{2,1,0:T(8,128)(2,1)S(1)} %collective-permute-done.30.refs_3_) | copy-start | bytes 786436
  221.6 7.1 %copy-start.21 = (bf16[2,512,128]{2,1,0:T(8,128)(2,1)}, bf16[2,512,128]{2,1,0:T(8,128)(2,1)S(1)}, u32[]{:S(2)}) copy-start(bf16[2,512,128]{2,1,0:T(8,128)(2,1)S(1)} %collective-permute-done.31.refs_6_) | copy-start | bytes 786436
  226.4 2.2 copy-start.22
  230.9 7.5 %collective-permute-start.33 = (bf16[2,256,128]{2,1,0:T(8,128)(2,1)}, bf16[2,256,128]{2,1,0:T(8,128)(2,1)S(1)}, u32[]{:S(2)}, u32[]{:S(2)}) collective-permute-start(bf16[2,256,128]{2,1,0:T(8,128)(2,1)} %get-tuple-element.121), channel_id=1, source_target_pairs={{0,1},{1,0},{2,3},{3,2},{4,5},{5,4},{6,7},{7,6},{8,9},{9,8},{10,11... | collective-permute-start | bytes 393224 | tf_op jit(solution)/shard_map/out_pairs1_0_1/ppermute | solution.py:312
  230.9 7.5 %collective-permute-start.34 = (bf16[2,256,128]{2,1,0:T(8,128)(2,1)}, bf16[2,256,128]{2,1,0:T(8,128)(2,1)}, u32[]{:S(2)}, u32[]{:S(2)}) collective-permute-start(bf16[2,256,128]{2,1,0:T(8,128)(2,1)} %get-tuple-element.120), channel_id=1, source_target_pairs={{0,2},{1,3},{2,0},{3,1},{4,6},{5,7},{6,4},{7,5},{8,10},{9,11},{10,... | collective-permute-start | bytes 393224 | tf_op jit(solution)/shard_map/out_pairs1_0_2/ppermute | solution.py:312
  232.7 6.9 %copy-start.11 = (f32[2,2048,128]{2,1,0:T(8,128)S(1)}, f32[2,2048,128]{2,1,0:T(8,128)}, u32[]{:S(2)}) copy-start(f32[2,2048,128]{2,1,0:T(8,128)} %get-tuple-element.87) | copy-start | bytes 6291460
  232.7 6.9 %collective-permute-start.35 = (bf16[2,256,128]{2,1,0:T(8,128)(2,1)}, bf16[2,256,128]{2,1,0:T(8,128)(2,1)}, u32[]{:S(2)}, u32[]{:S(2)}) collective-permute-start(bf16[2,256,128]{2,1,0:T(8,128)(2,1)} %get-tuple-element.119), channel_id=1, source_target_pairs={{0,3},{1,2},{2,1},{3,0},{4,7},{5,6},{6,5},{7,4},{8,11},{9,10},{10,... | collective-permute-start | bytes 393224 | tf_op jit(solution)/shard_map/out_pairs1_0_3/ppermute | solution.py:312
  238.4 2.6 %copy-start.23 = (bf16[2,256,128]{2,1,0:T(8,128)(2,1)}, bf16[2,256,128]{2,1,0:T(8,128)(2,1)S(1)}, u32[]{:S(2)}) copy-start(bf16[2,256,128]{2,1,0:T(8,128)(2,1)S(1)} %collective-permute-done.33.refs_4_) | copy-start | bytes 393220
  241.7 1.9 collective-permute-start.36
  241.9 6.3 %collective-permute-start.37 = (bf16[2,256,128]{2,1,0:T(8,128)(2,1)S(1)}, bf16[2,256,128]{2,1,0:T(8,128)(2,1)S(1)}, u32[]{:S(2)}, u32[]{:S(2)}) collective-permute-start(bf16[2,256,128]{2,1,0:T(8,128)(2,1)S(1)} %get-tuple-element.116), channel_id=1, source_target_pairs={{0,2},{1,3},{2,0},{3,1},{4,6},{5,7},{6,4},{7,5},{8,10},{9,11},{10,... | collective-permute-start | bytes 393224 | tf_op jit(solution)/shard_map/out_pairs1_1_2/ppermute | solution.py:312
  243.7 6.2 %collective-permute-start.38 = (bf16[2,256,128]{2,1,0:T(8,128)(2,1)S(1)}, bf16[2,256,128]{2,1,0:T(8,128)(2,1)S(1)}, u32[]{:S(2)}, u32[]{:S(2)}) collective-permute-start(bf16[2,256,128]{2,1,0:T(8,128)(2,1)S(1)} %get-tuple-element.115), channel_id=1, source_target_pairs={{0,3},{1,2},{2,1},{3,0},{4,7},{5,6},{6,5},{7,4},{8,11},{9,10},{10,... | collective-permute-start | bytes 393224 | tf_op jit(solution)/shard_map/out_pairs1_1_3/ppermute | solution.py:312
  243.7 6.2 %copy-start.24 = (bf16[2,256,128]{2,1,0:T(8,128)(2,1)}, bf16[2,256,128]{2,1,0:T(8,128)(2,1)S(1)}, u32[]{:S(2)}) copy-start(bf16[2,256,128]{2,1,0:T(8,128)(2,1)S(1)} %collective-permute-done.36.refs_5_) | copy-start | bytes 393220
  (10 other events, 13.5 us)

commit v3 on v2

v3 whole, which is shorter than its diff:
```python
import functools
import math

import jax
import jax.numpy as jnp
from jax import lax
from jax.experimental import pallas as pl
from jax.experimental.pallas import tpu as pltpu
from jax.sharding import PartitionSpec as P

HD = 128
BLK = 128
VERT_DEV = 1
FAR = 1e30


def attention_kernel(dims, place, vertical, columns, offsets, *refs):
    local_blocks, group, vert_total, heads, last = dims
    refs = list(refs)

    def take(count):
        taken = refs[:count]
        del refs[:count]
        return taken

    q_ref, do_ref, kv_own, kv_column, kv_other = take(5)
    kv_back, kv_even, kv_odd = take(3)
    dq_refs, (own_ref, prev_ref, back_ref), far_refs = take(heads), take(3), take(2 if last else 1)
    pool_k, pool_v, acc_k, acc_v, dq_out, sems = refs
    turn_number = pl.program_id(0)
    seq_index, head_index = place[0], place[1]
    share = local_blocks // heads
    together = min(4, share)
    turns = share // together
    step_base = ((turn_number // turns ^ head_index) * turns + lax.rem(turn_number, turns)) * together
    rows = local_blocks * BLK
    scale = 1.0 / math.sqrt(HD)

    @pl.when(turn_number == 0)
    def _():
        def copies(prev, parity):
            parts = [(kv_own, 0), (prev, rows), (kv_back, 2 * rows)]
            made = []
            for side, pool in enumerate((pool_k, pool_v)):
                for ref, start in parts:
                    made.append((ref.at[side], pool.at[pl.ds(start, ref.shape[1])]))
                for ref, number in ((kv_column, parity), (kv_other, 1 - parity)):
                    for plane in range(vert_total // 2):
                        into = pool.at[pl.ds(3 * rows + (2 * plane + number) * BLK, BLK)]
                        made.append((ref.at[plane, side], into))
                source = kv_other if parity else kv_column
                made.append((source.at[vert_total // 2, side], pool.at[pl.ds(3 * rows + vert_total * BLK, BLK)]))
            return [pltpu.make_async_copy(*ends, sems.at[at]) for at, ends in enumerate(made)]

        odd = lax.rem(seq_index, 2) == 1
        ways = ((odd, kv_even, 1), (jnp.logical_not(odd), kv_odd, 0))
        for way, prev, parity in ways:

            @pl.when(way)
            def _():
                for copy in copies(prev, parity):
                    copy.start()

        acc_k[...] = jnp.zeros_like(acc_k)
        acc_v[...] = jnp.zeros_like(acc_v)
        for way, prev, parity in ways:

            @pl.when(way)
            def _():
                for copy in copies(prev, parity):
                    copy.wait()

    scale_two = scale * math.log2(math.e)
    contract_last = (((1,), (1,)), ((), ()))
    contract_first = (((0,), (0,)), ((), ()))
    width = group * BLK
    seen = lax.broadcasted_iota(jnp.int32, (BLK, width), 0) <= lax.broadcasted_iota(jnp.int32, (BLK, width), 1) % BLK

    def column_block(column):
        return column // VERT_DEV * local_blocks + vertical[column]

    def stacked(ref, here):
        return jnp.concatenate([ref[here, g * HD : (g + 1) * HD] for g in range(group)], axis=0)

    def begin(sub):
        step = step_base + sub
        block = seq_index * local_blocks + step
        here = slice(sub * BLK, (sub + 1) * BLK)

        def near(offset):
            at = step - offset
            return jnp.where(at >= 0, at, jnp.where(at >= -local_blocks, at + 2 * local_blocks, at + 4 * local_blocks))

        first, second = offsets[step, 0], offsets[step, 1]
        left, right = columns[step, 0], columns[step, 1]
        b2, b3 = block - first, block - second
        b4, b5 = column_block(left), column_block(right)
        far = 3 * local_blocks
        slots = [far + vert_total, step, near(first), near(second), far + left, far + right]
        live = [
            block > 0,
            None,
            b2 > 0,
            (b3 > 0) & (b3 != b2),
            (b4 > 0) & (b4 < block) & (b4 != b2) & (b4 != b3),
            (b5 > 0) & (b5 < block) & (b5 != b2) & (b5 != b3) & (b5 != b4),
        ]
        spots = [pl.ds(pl.multiple_of(slot * BLK, BLK), BLK) for slot in slots]
        queries, grads = stacked(q_ref, here), stacked(do_ref, here)
        keys = jnp.concatenate([pool_k[spot, :] for spot in spots], axis=0)
        values = jnp.concatenate([pool_v[spot, :] for spot in spots], axis=0)
        score = lax.dot_general(keys, queries, contract_last, preferred_element_type=jnp.float32)
        product = lax.dot_general(values, grads, contract_last, preferred_element_type=jnp.float32)
        return live, spots, queries, grads, keys, score, product

    def weigh(live, score, product):
        scores, tops, weights, probs, dscores = [], [], [], [], []
        for number in range(6):
            part = score[number * BLK : (number + 1) * BLK] * scale_two
            if number == 1:
                part = jnp.where(seen, part, -FAR)
            scores.append(part)
            top = jnp.max(part, axis=0, keepdims=True)
            tops.append(top if number == 1 else jnp.where(live[number], top, -FAR))
        top = functools.reduce(jnp.maximum, tops)
        total, delta = 0.0, 0.0
        for number in range(6):
            weight = jnp.exp2(scores[number] - (top if number == 1 else jnp.where(live[number], top, FAR)))
            total = total + jnp.sum(weight, axis=0, keepdims=True)
            delta = delta + jnp.sum(weight * product[number * BLK : (number + 1) * BLK], axis=0, keepdims=True)
            weights.append(weight)
        inverse = 1.0 / total
        delta = delta * inverse
        for number in range(6):
            prob = weights[number] * inverse
            dscores.append((prob * (product[number * BLK : (number + 1) * BLK] - delta)).astype(jnp.bfloat16))
            probs.append(prob.astype(jnp.bfloat16))
        return jnp.concatenate(probs, axis=0), jnp.concatenate(dscores, axis=0)

    def finish(sub, spots, queries, grads, keys, prob, dscore):
        value_terms = jnp.dot(prob, grads, preferred_element_type=jnp.float32)
        key_terms = jnp.dot(dscore, queries, preferred_element_type=jnp.float32)
        dq = lax.dot_general(dscore, keys, contract_first, preferred_element_type=jnp.float32)
        dq = (dq * scale).astype(jnp.bfloat16)
        for number, spot in enumerate(spots):
            acc_v[spot, :] += value_terms[number * BLK : (number + 1) * BLK]
            acc_k[spot, :] += key_terms[number * BLK : (number + 1) * BLK]
        for g in range(group):
            dq_out[sub * BLK : (sub + 1) * BLK, g * HD : (g + 1) * HD] = dq[g * BLK : (g + 1) * BLK]

    begun = begin(0)
    for sub in range(together):
        live, spots, queries, grads, keys, score, product = begun
        if sub + 1 < together:
            begun = begin(sub + 1)
        prob, dscore = weigh(live, score, product)
        finish(sub, spots, queries, grads, keys, prob, dscore)

    for k, dq_ref in enumerate(dq_refs):

        @pl.when(turn_number // (share // together) == k)
        def _():
            dq_ref[...] = dq_out[...]

    @pl.when(turn_number == local_blocks // together - 1)
    def _():
        for side, (acc, factor) in enumerate(((acc_k, scale), (acc_v, 1.0))):
            prev_ref[side] = (acc[rows : 2 * rows, :] * factor).astype(jnp.bfloat16)
            back_ref[side] = (acc[2 * rows : 3 * rows, :] * factor).astype(jnp.bfloat16)
            own_ref[side] = acc[:rows, :] * factor

            def far_block(number):
                start = pl.multiple_of((3 * local_blocks + number) * BLK, BLK)
                return (acc[pl.ds(start, BLK), :] * factor).astype(jnp.bfloat16)

            if last:
                for ref, parity in ((far_refs[0], seq_index % 2), (far_refs[1], 1 - seq_index % 2)):
                    for plane in range(vert_total // 2):
                        ref[plane, side] = far_block(2 * plane + parity)
                    ref[vert_total // 2, side] = far_block(vert_total)
            else:
                sink = far_block(vert_total)
                for number in range(vert_total):
                    far_refs[0][number, 0, side] = far_block(number)
                    far_refs[0][number, 1, side] = sink


def attention(
    head, kv_local, heads, place, vertical, columns, offsets, queries, grad_out, kv_own, kv_column, kv_other,
    kv_back, kv_even, kv_odd
):
    seq_len = queries.shape[0]
    local_blocks = seq_len // BLK
    width = queries.shape[1] // kv_local
    group = width // HD
    vert_total = vertical.shape[0]
    total_rows = 3 * seq_len + (vert_total + 1) * BLK
    anywhere = pl.BlockSpec(memory_space=pl.ANY)
    share = local_blocks // heads
    together = min(4, share)
    turns = share // together
    by_block = pl.BlockSpec((together * BLK, width), lambda i, place, *_: ((i // turns ^ place[1]) * turns + i % turns, head))

    def whole(*shape):
        return pl.BlockSpec(shape, lambda i, *_: (0,) * len(shape))

    def share_spec(k):
        return pl.BlockSpec((together * BLK, width), lambda i, *_: (jnp.clip(i - k * turns, 0, turns - 1), 0))

    near_shape = (2, seq_len, HD)
    block_shape = (2, BLK, HD)
    last = head + 1 == kv_local
    far_shapes = [(vert_total // 2 + 1, *block_shape)] * 2 if last else [(vert_total, 2, *block_shape)]
    flops = 2 * 5 * seq_len * group * 6 * BLK * HD
    outs = pl.pallas_call(
        functools.partial(attention_kernel, (local_blocks, group, vert_total, heads, last)),
        grid_spec=pltpu.PrefetchScalarGridSpec(
            num_scalar_prefetch=4,
            grid=(local_blocks // together,),
            in_specs=[by_block, by_block] + [anywhere] * 6,
            out_specs=[share_spec(k) for k in range(heads)]
            + [whole(*near_shape)] * 3
            + [whole(*shape) for shape in far_shapes],
            scratch_shapes=[
                pltpu.VMEM((total_rows, HD), jnp.bfloat16),
                pltpu.VMEM((total_rows, HD), jnp.bfloat16),
                pltpu.VMEM((total_rows, HD), jnp.float32),
                pltpu.VMEM((total_rows, HD), jnp.float32),
                pltpu.VMEM((together * BLK, width), jnp.bfloat16),
                pltpu.SemaphoreType.DMA((2 * (4 + vert_total),)),
            ],
        ),
        out_shape=[jax.ShapeDtypeStruct((seq_len // heads, width), jnp.bfloat16)] * heads
        + [jax.ShapeDtypeStruct(near_shape, jnp.float32)]
        + [jax.ShapeDtypeStruct(near_shape, jnp.bfloat16)] * 2
        + [jax.ShapeDtypeStruct(shape, jnp.bfloat16) for shape in far_shapes],
        compiler_params=pltpu.CompilerParams(vmem_limit_bytes=50 * 1024 * 1024),
        cost_estimate=pl.CostEstimate(
            flops=4 * flops, bytes_accessed=20 * 1024 * 1024, transcendentals=seq_len * group * 6 * BLK
        ),
        name="attention",
    )(place, vertical, columns, offsets, queries, grad_out, kv_own, kv_column, kv_other, kv_back, kv_even, kv_odd)
    return outs[:heads], *outs[heads:]


def queries_kernel(heads, kv_local, place, *refs):
    for k in range(heads):
        for head in range(kv_local):
            piece = refs[k * kv_local + head]
            width = piece.shape[1]
            column = (place[1] ^ k) * kv_local + head
            refs[-1][:, pl.ds(pl.multiple_of(column * width, width), width)] = piece[...]


def assemble_queries(place, heads, kv_local, pieces):
    rows, width = pieces[0, 0].shape
    tile = min(rows, 128)
    count = heads * kv_local
    return pl.pallas_call(
        functools.partial(queries_kernel, heads, kv_local),
        grid_spec=pltpu.PrefetchScalarGridSpec(
            num_scalar_prefetch=1,
            grid=(rows // tile,),
            in_specs=[pl.BlockSpec((tile, width), lambda i, *_: (i, 0))] * count,
            out_specs=pl.BlockSpec((tile, width * count), lambda i, *_: (i, 0)),
        ),
        out_shape=jax.ShapeDtypeStruct((rows, width * count), jnp.bfloat16),
        name="assemble_queries",
    )(place, *(pieces[k, head] for k in range(heads) for head in range(kv_local)))


def pairs_kernel(heads, kv_local, place, *refs):
    k_out, v_out = refs[-2:]
    for k in range(heads):
        for head in range(kv_local):
            column = (place[1] ^ k) * kv_local + head
            spot = pl.ds(pl.multiple_of(column * HD, HD), HD)
            both = refs[k * kv_local + head]
            k_out[:, spot] = both[0]
            v_out[:, spot] = both[1]


def assemble_pairs(place, heads, kv_local, pieces):
    arrays = [pieces[k, head] for k in range(heads) for head in range(kv_local)]
    rows = arrays[0].shape[1]
    tile = min(rows, 256)
    out_shape = jax.ShapeDtypeStruct((rows, HD * heads * kv_local), jnp.bfloat16)
    return pl.pallas_call(
        functools.partial(pairs_kernel, heads, kv_local),
        grid_spec=pltpu.PrefetchScalarGridSpec(
            num_scalar_prefetch=1,
            grid=(rows // tile,),
            in_specs=[pl.BlockSpec((2, tile, HD), lambda i, *_: (0, i, 0))] * len(arrays),
            out_specs=[pl.BlockSpec((tile, out_shape.shape[1]), lambda i, *_: (i, 0))] * 2,
        ),
        out_shape=[out_shape] * 2,
        name="assemble_pairs",
    )(place, *arrays)


def after(value, *others):
    return lax.optimization_barrier((value, others))[0]


def shards(queries, keys, values, grad_out, vertical, columns, offsets):
    seq_len = queries.shape[0]
    seq_size = lax.axis_size("seq")
    heads = lax.axis_size("head")
    kv_local = keys.shape[1] // HD
    local_blocks = seq_len // BLK
    seq_index = lax.axis_index("seq")
    head_index = lax.axis_index("head")
    place = jnp.stack([seq_index, head_index]).astype(jnp.int32)
    odd = seq_index % 2 == 1
    levels = [1 << level for level in range(int(math.log2(seq_size)))]

    def along(array, pairs, name):
        with jax.named_scope(name):
            return lax.ppermute(array, "seq", pairs)

    def across(array, k, name):
        with jax.named_scope(name):
            return lax.ppermute(array, "head", [(i, i ^ k) for i in range(heads)]) if k else array

    def shift(by, only=None):
        return [(i, i + by) for i in range(seq_size) if 0 <= i + by < seq_size and only in (None, i % 2)]

    exchange = [(i, i ^ 1) for i in range(seq_size)]
    own_vertical = lax.dynamic_slice_in_dim(vertical, seq_index * VERT_DEV, VERT_DEV)[0]
    kvs = [
        jnp.stack([keys[:, head * HD : (head + 1) * HD], values[:, head * HD : (head + 1) * HD]])
        for head in range(kv_local)
    ]
    mine = jnp.stack([lax.dynamic_slice_in_dim(kv, own_vertical * BLK, BLK, axis=1) for kv in kvs])
    sink = jnp.stack([kv[:, :BLK] for kv in kvs])
    groups = [list(range(0, seq_size, 2)), list(range(1, seq_size, 2))]

    def column_of(block, name):
        with jax.named_scope(name):
            wide = jnp.broadcast_to(block, (seq_size // 2, *block.shape))
            return lax.all_to_all(wide, "seq", split_axis=0, concat_axis=0, axis_index_groups=groups)

    first = sink
    for hop in reversed(levels[1:]):
        got = along(first, [(i, i + hop) for i in range(0, seq_size, 2 * hop)], f"in_first{hop}")
        first = jnp.where(seq_index % (2 * hop) == hop, got, first)

    column = column_of(mine, "in_column")
    kv_columns = [jnp.concatenate([column[:, head], first[None, head]]) for head in range(kv_local)]

    fetched = []
    for head, kv in enumerate(kvs):
        kv_column = kv_columns[head]
        if head:
            kv, kv_column = after((kv, kv_column), fetched[-1][1], fetched[-1][5])
        kv_other = along(kv_column, exchange, f"in_column_pair{head}")
        if head:
            back, even = along(kv, shift(2), f"in_back{head}"), along(kv, shift(1), f"in_prev{head}")
            odd_prev = even
        else:
            back, even = along(kv, shift(2), f"in_back{head}"), along(kv, shift(1, 0), f"in_even{head}")
            odd_prev = along(after(back, kv_other), shift(-1, 1), f"in_odd{head}")
        fetched.append((kv, back, even, odd_prev, kv_column, kv_other))

    planes = seq_size // 2
    query_pieces, pair_pieces, results, fars = {}, {}, [], []

    def onward(back, side):
        return (back.astype(jnp.float32) + jnp.where(odd, side.astype(jnp.float32), 0.0)).astype(jnp.bfloat16)

    for head, (kv, back, even, odd_prev, kv_column, kv_other) in enumerate(fetched):
        last = head + 1 == kv_local
        dqs, own, prev, back, *table = attention(
            head, kv_local, heads, place, vertical, columns, offsets, queries, grad_out, kv, kv_column, kv_other, back, even, odd_prev
        )
        if not last:
            with jax.named_scope(f"out_far{head}"):
                fars.append(lax.all_to_all(table[0], "seq", split_axis=0, concat_axis=0))
            for k in range(heads):
                query_pieces[k, head] = across(dqs[k], k, f"out_query{head}_{k}")
            results.append((own, along(prev, exchange, f"out_pair{head}"), back))
            continue
        keep, give = table
        if head:
            before = [query_pieces[k, head - 1] for k in range(heads)]
            fars, results = after((fars, results), dqs[0])
            prev, give, dqs = after((prev, give, dqs), before, fars, results)
        got = along(give, exchange, f"out_far_pair{head}")
        for k in range(2, heads):
            query_pieces[k, head] = across(dqs[k], k, f"out_query{head}_{k}")
        sent = [onward(back_before, side_before) for _, side_before, back_before in results]
        side = along(after(prev, sent), exchange, f"out_pair{head}")
        results = [
            (own_before, side_before, along(piece, shift(-2), f"out_onward{at}"))
            for at, ((own_before, side_before, _), piece) in enumerate(zip(results, sent))
        ]
        far_sum = (keep.astype(jnp.float32) + got.astype(jnp.float32)).astype(jnp.bfloat16)
        far_sum = jnp.stack([far_sum[:planes], jnp.broadcast_to(far_sum[planes], far_sum[:planes].shape)], axis=1)
        with jax.named_scope("out_far"):
            fars.append(lax.all_to_all(far_sum, "seq", split_axis=0, concat_axis=0, axis_index_groups=groups))
        fars = [jnp.sum(terms.astype(jnp.float32), axis=0) for terms in fars]
        if heads > 1:
            query_pieces[1, head] = across(after(dqs[1], far_sum), 1, f"out_query{head}_1")
        query_pieces[0, head] = dqs[0]
        results.append((own, side, along(onward(back, side), shift(-2), f"out_onward{head}")))

    block_ids = jnp.arange(local_blocks)[None, :, None, None]
    for head, (own, side, returned) in enumerate(results):
        if head and head + 1 == kv_local:
            query_out = assemble_queries(place, heads, kv_local, query_pieces)
            returned = after(returned, query_out, list(pair_pieces.values()))
        elif kv_local == 1:
            query_out = assemble_queries(place, heads, kv_local, query_pieces)

        def blocked(array):
            return array.reshape(2, local_blocks, BLK, HD).astype(jnp.float32)

        total = blocked(own) + (jnp.where(odd, 0.0, blocked(side)) + blocked(returned))
        total = total + jnp.where(block_ids == own_vertical, fars[head][0][:, None], 0.0)
        total = total + jnp.where((block_ids == 0) & (seq_index == 0), fars[head][1][:, None], 0.0)
        total = total.astype(jnp.bfloat16).reshape(2, heads, -1, HD)
        for k in range(heads):
            piece = lax.dynamic_index_in_dim(total, head_index ^ k, 1, keepdims=False)
            pair_pieces[k, head] = across(piece, k, f"out_pairs{head}_{k}")
    return (query_out, *assemble_pairs(place, heads, kv_local, pair_pieces))


def solution(mesh):
    return jax.shard_map(
        shards,
        mesh=mesh,
        in_specs=(
            P("seq", "head"),
            P("seq", "head"),
            P("seq", "head"),
            P("seq", "head"),
            P(),
            P("seq", None),
            P("seq", None),
        ),
        out_specs=(P(("seq", "head"), None), P(("seq", "head"), None), P(("seq", "head"), None)),
        check_vma=False,
    )
```

time: 256 us -> 238 us (0.930)
  starting transfers between devices: 76 us -> 58.1 us
  waiting for transfers between devices: 69.6 us -> 81.3 us
  Pallas kernels: 78.2 us -> 68.1 us
    ppermute x24 -> x14, starting transfers between devices: 51.4 us -> 37.1 us  [along(): return lax.ppermute(array, 'seq', pairs)]
    ppermute x15 -> x12, waiting for transfers between devices: 12.7 us -> 24.5 us  [across(): lax.ppermute(array, 'head', [(i, i ^ k) for i in range(heads)])]
    pallas_call x2, Pallas kernels: 68.5 us -> 59 us  [attention(): pl.pallas_call(functools.partial(attention_kernel, (local_blocks, group,...]
    ppermute x24 -> x14, waiting for transfers between devices: 56.9 us -> 51.1 us  [along(): return lax.ppermute(array, 'seq', pairs)]
    all_to_all x1 -> x2, starting transfers between devices: 5.99 us -> 11.3 us  [the longest x1 5.77 us: shards(): fars.append(lax.all_to_all(table[0], 'seq', split_axis=0, concat_axis=0))]
    all_to_all x2 -> x1, starting transfers between devices: 8.15 us -> 3.47 us  [column_of(): lax.all_to_all(wide, 'seq', split_axis=0, concat_axis=0, axis_index_group...]
    ppermute x15 -> x12, starting transfers between devices: 10.4 us -> 6.22 us  [across(): lax.ppermute(array, 'head', [(i, i ^ k) for i in range(heads)])]
    all_to_all x1 -> x2, waiting for transfers between devices: 0.01 us -> 3.8 us  [the longest x1 3.79 us: shards(): lax.all_to_all(far_sum, 'seq', split_axis=0, concat_axis=0, axis_index_gr...]
  transfers between devices with their start and end apart: 42 -> 29, of which waited for: 13 -> 14; matrix products, arithmetic and copies ran while one was open for 7% -> 7% of each run, Pallas kernels for 29% -> 27%
where the time goes in v3:
time: 238 us; the launch traced here: 236 us
  waiting for transfers between devices  81.3 us (34%)
  Pallas kernels  68.1 us (29%)
  starting transfers between devices  58.1 us (24%)
  other arithmetic  15.1 us (6%)
  local copies, waits for them, and re-layouts  11.8 us (5%)
    pallas_call x2, Pallas kernels, attention(): pl.pallas_call(functools.partial(attention_kernel, (local_blocks, group,...  59 us
    ppermute x14, waiting for transfers between devices, along(): return lax.ppermute(array, 'seq', pairs)  51.1 us
    ppermute x14, starting transfers between devices, along(): return lax.ppermute(array, 'seq', pairs)  37.1 us
    ppermute x12, waiting for transfers between devices, across(): lax.ppermute(array, 'head', [(i, i ^ k) for i in range(heads)])  24.5 us
    ppermute x12, starting transfers between devices, across(): lax.ppermute(array, 'head', [(i, i ^ k) for i in range(heads)])  6.22 us
    all_to_all x1, starting transfers between devices, shards(): fars.append(lax.all_to_all(table[0], 'seq', split_axis=0, concat_axis=0))  5.77 us
    all_to_all x1, starting transfers between devices, shards(): lax.all_to_all(far_sum, 'seq', split_axis=0, concat_axis=0, axis_index_gr...  5.57 us
    pallas_call x1, Pallas kernels, assemble_queries(): pl.pallas_call(functools.partial(queries_kernel, heads, kv_local), grid_s...  5.56 us
  transfers between devices with their start and end apart: 29, of which 14 were waited for; matrix products, arithmetic and copies ran while one was open for 7% of the time, Pallas kernels for 27%

profile of v3, /device:TPU:0, one launch (start us, length us, event | category | flops | bytes accessed | tf_op | source)
XLA Modules:
  0.0 236.2 jit_solution(10014735847579211837)
XLA Ops:
  0.7 1.4 slice_bitcast_fusion
  2.3 0.6 dynamic_slice.34
  3.5 5.9 %collective-permute-start = (bf16[2,2,128,128]{3,2,1,0:T(8,128)(2,1)S(1)}, bf16[2,2,128,128]{3,2,1,0:T(8,128)(2,1)S(1)}, u32[]{:S(2)}, u32[]{:S(2)}) collective-permute-start(bf16[2,2,128,128]{3,2,1,0:T(8,128)(2,1)S(1)} %pad_maximum_fusion.6), channel_id=1, source_target_pairs={{0,16},{1,17},{2,18},{3,19}} | collective-permute-start | bytes 393224 | tf_op jit(solution)/shard_map/in_first4/ppermute | solution.py:319
  9.5 0.9 broadcast_in_dim.85
  10.4 3.5 %all-to-all-start = ((bf16[4,2,2,128,128]{4,3,2,1,0:T(8,128)(2,1)}), bf16[4,2,2,128,128]{4,3,2,1,0:T(8,128)(2,1)S(1)}, u32[]{:S(2)}, u32[]{:S(2)}) async-start(bf16[4,2,2,128,128]{4,3,2,1,0:T(8,128)(2,1)} %broadcast_in_dim.85), calls=%async_computation | async-start | bytes 1048576 | tf_op jit(solution)/shard_map/in_column/all_to_all | solution.py:341
  14.0 3.9 %collective-permute-start.1 = (bf16[2,2,128,128]{3,2,1,0:T(8,128)(2,1)S(1)}, bf16[2,2,128,128]{3,2,1,0:T(8,128)(2,1)S(1)}, u32[]{:S(2)}, u32[]{:S(2)}) collective-permute-start(bf16[2,2,128,128]{3,2,1,0:T(8,128)(2,1)S(1)} %broadcast_select_fusion), channel_id=1, source_target_pairs={{0,8},{16,24},{1,9},{17,25},{2,10},{18,26},{3,11},{19,27}} | collective-permute-start | bytes 393224 | tf_op jit(solution)/shard_map/in_first2/ppermute | solution.py:319
  17.8 1.1 pad_maximum_fusion.refs_2_
  18.9 2.3 collective-permute-start.3
  21.2 5.2 %collective-permute-done.1 = bf16[2,2,128,128]{3,2,1,0:T(8,128)(2,1)S(1)} collective-permute-done((bf16[2,2,128,128]{3,2,1,0:T(8,128)(2,1)S(1)}, bf16[2,2,128,128]{3,2,1,0:T(8,128)(2,1)S(1)}, u32[]{:S(2)}, u32[]{:S(2)}) %collective-permute-start.1) | collective-permute-done | bytes 131104 | tf_op jit(solution)/shard_map/in_first2/ppermute | solution.py:319
  26.5 1.8 all-to-all-done
  28.5 4.9 %collective-permute-start.4 = (bf16[2,2048,128]{2,1,0:T(8,128)(2,1)}, bf16[2,2048,128]{2,1,0:T(8,128)(2,1)}, u32[]{:S(2)}, u32[]{:S(2)}) collective-permute-start(bf16[2,2048,128]{2,1,0:T(8,128)(2,1)} %pad_maximum_fusion.refs_2_), channel_id=1, source_target_pairs={{0,4},{8,12},{16,20},{24,28},{1,5},{9,13},{17,21},{25,29},{2,6},{1... | collective-permute-start | bytes 3145736 | tf_op jit(solution)/shard_map/in_even0/ppermute | solution.py:319
  33.4 14.5 %collective-permute-done.3.refs_5_ = bf16[2,2048,128]{2,1,0:T(8,128)(2,1)} collective-permute-done((bf16[2,2048,128]{2,1,0:T(8,128)(2,1)}, bf16[2,2048,128]{2,1,0:T(8,128)(2,1)}, u32[]{:S(2)}, u32[]{:S(2)}) %collective-permute-start.3) | collective-permute-done | bytes 1048608 | tf_op jit(solution)/shard_map/in_back0/ppermute | solution.py:319
  47.9 1.3 collective-permute-start.5
  49.2 0.6 fusion.23
  50.3 1.1 pad_maximum_fusion.1.refs_2_
  51.4 5.4 %collective-permute-start.7 = (bf16[2,2048,128]{2,1,0:T(8,128)(2,1)}, bf16[2,2048,128]{2,1,0:T(8,128)(2,1)}, u32[]{:S(2)}, u32[]{:S(2)}) collective-permute-start(bf16[2,2048,128]{2,1,0:T(8,128)(2,1)} %pad_maximum_fusion.1.refs_2_), channel_id=1, source_target_pairs={{0,8},{4,12},{8,16},{12,20},{16,24},{20,28},{1,9},{5,13},{9,17},{1... | collective-permute-start | bytes 3145736 | tf_op jit(solution)/shard_map/in_back1/ppermute | solution.py:319
  56.8 6.5 %collective-permute-start.8 = (bf16[2,2048,128]{2,1,0:T(8,128)(2,1)}, bf16[2,2048,128]{2,1,0:T(8,128)(2,1)}, u32[]{:S(2)}, u32[]{:S(2)}) collective-permute-start(bf16[2,2048,128]{2,1,0:T(8,128)(2,1)} %pad_maximum_fusion.1.refs_2_), channel_id=1, source_target_pairs={{0,4},{4,8},{8,12},{12,16},{16,20},{20,24},{24,28},{1,5},{5,9},{9,... | collective-permute-start | bytes 3145736 | tf_op jit(solution)/shard_map/in_prev1/ppermute | solution.py:319
  63.3 12.9 %collective-permute-done.5.refs_7_ = bf16[2,2048,128]{2,1,0:T(8,128)(2,1)} collective-permute-done((bf16[2,2048,128]{2,1,0:T(8,128)(2,1)}, bf16[2,2048,128]{2,1,0:T(8,128)(2,1)}, u32[]{:S(2)}, u32[]{:S(2)}) %collective-permute-start.5) | collective-permute-done | bytes 1048608 | tf_op jit(solution)/shard_map/in_odd0/ppermute | solution.py:319
  76.2 29.8 %attention.2 = (bf16[512,512]{1,0:T(8,128)(2,1)S(1)}, bf16[512,512]{1,0:T(8,128)(2,1)}, bf16[512,512]{1,0:T(8,128)(2,1)}, bf16[512,512]{1,0:T(8,128)(2,1)}, f32[...) custom-call(s32[2]{0:T(128)S(1)} %pad_add_fusion.place, ...), custom_call_target="tpu_custom_call" | custom-call | flops 32212254720 | bytes 20971520 | tf_op jit(solution)/shard_map/attention/pallas_call | solution.py:215
  106.0 0.8 copy-done
  106.8 1.5 collective-permute-start.10
  108.3 5.8 %all-to-all-start.1 = ((bf16[8,2,2,128,128]{4,3,2,1,0:T(8,128)(2,1)}), bf16[8,2,2,128,128]{4,3,2,1,0:T(8,128)(2,1)}, u32[]{:S(2)}, u32[]{:S(2)}) async-start(bf16[8,2,2,128,128]{4,3,2,1,0:T(8,128)(2,1)} %get-tuple-element.51), calls=%async_computation.1 | async-start | bytes 2097152 | tf_op jit(solution)/shard_map/out_far0/all_to_all | solution.py:378
  114.0 0.7 copy-done.3
  114.9 1.9 collective-permute-start.12
  116.8 1.0 copy-done.4
  117.8 29.2 %attention.3 = (bf16[512,512]{1,0:T(8,128)(2,1)S(1)}, bf16[512,512]{1,0:T(8,128)(2,1)S(1)}, bf16[512,512]{1,0:T(8,128)(2,1)S(1)}, bf16[512,512]{1,0:T(8,128)(2,1...) custom-call(s32[2]{0:T(128)S(1)} %pad_add_fusion.place, ...), custom_call_target="tpu_custom_call" | custom-call | flops 32212254720 | bytes 20971520 | tf_op jit(solution)/shard_map/attention/pallas_call | solution.py:215
  147.0 0.8 copy-done.1
  147.8 0.7 copy-done.5
  148.5 2.1 collective-permute-done.12
  150.6 0.4 collective-permute-start.13
  151.0 0.5 collective-permute-start.15
  151.5 2.9 %fusion.3 = bf16[2,2048,128]{2,1,0:T(8,128)(2,1)} fusion(bf16[2,2048,128]{2,1,0:T(8,128)(2,1)} %collective-permute-done.12, bf16[2,2048,128]{2,1,0:T(8,128)(2,1)} %get-tuple-element.58, pred[]{:T(512)S(6)} %eq.41), kind=kLoop, calls=%fused_computation.7 | loop fusion | flops 2621440 | bytes 3145729 | tf_op jit(solution)/shard_map/convert_element_type | solution.py:369
  154.4 1.3 collective-permute-start.17
  155.6 1.8 collective-permute-start.18
  157.4 2.1 collective-permute-done.13
  159.9 1.4 convert_reduce_fusion
  161.3 0.8 copy.26
  162.2 5.6 %all-to-all-start.2 = ((bf16[4,2,2,128,128]{4,3,2,1,0:T(8,128)(2,1)}), bf16[4,2,2,128,128]{4,3,2,1,0:T(8,128)(2,1)}, u32[]{:S(2)}, u32[]{:S(2)}) async-start(bf16[4,2,2,128,128]{4,3,2,1,0:T(8,128)(2,1)} %copy.26), calls=%async_computation.2 | async-start | bytes 1048576 | tf_op jit(solution)/shard_map/out_far/all_to_all | solution.py:400
  167.8 5.6 %collective-permute-done.16.refs_7_ = bf16[512,512]{1,0:T(8,128)(2,1)} collective-permute-done((bf16[512,512]{1,0:T(8,128)(2,1)S(1)}, bf16[512,512]{1,0:T(8,128)(2,1)}, u32[]{:S(2)}, u32[]{:S(2)}) %collective-permute-start.16) | collective-permute-done | bytes 524320 | tf_op jit(solution)/shard_map/out_query1_3/ppermute | solution.py:323
  173.4 5.6 %assemble_queries.1 = bf16[512,4096]{1,0:T(8,128)(2,1)} custom-call(s32[2]{0:T(128)} %copy-done.2, bf16[512,512]{1,0:T(8,128)(2,1)} %copy-done, bf16[512,512]{1,0:T(8,128)(2,1)} %copy-done.1, bf16[512,512]{1,0:T(8,128)(2,1)} %collective-permute-done.9.refs_2_, bf16[512,512]{1,0:T(8,128)(2,1)} %collective-permute-done.14.refs_3_, ...), custom_call_target="tpu_custom_call" | custom-call | tf_op jit(solution)/shard_map/assemble_queries/pallas_call | solution.py:259
  178.9 2.5 %collective-permute-done.18 = bf16[2,2048,128]{2,1,0:T(8,128)(2,1)S(1)} collective-permute-done((bf16[2,2048,128]{2,1,0:T(8,128)(2,1)}, bf16[2,2048,128]{2,1,0:T(8,128)(2,1)S(1)}, u32[]{:S(2)}, u32[]{:S(2)}) %collective-permute-start.18) | collective-permute-done | bytes 1048608 | tf_op jit(solution)/shard_map/out_pair1/ppermute | solution.py:319
  181.5 1.3 fusion.7
  182.8 1.5 collective-permute-start.19
  184.3 1.9 fusion.1
  186.7 0.8 fusion.12
  187.6 1.0 dynamic-slice_bitcast_fusion.4
  188.6 0.8 collective-permute-start.20
  189.4 0.8 collective-permute-start.21
  190.2 0.5 collective-permute-start.22
  190.7 3.8 %all-to-all-done.2 = bf16[4,2,2,128,128]{4,3,2,1,0:T(8,128)(2,1)} async-done(((bf16[4,2,2,128,128]{4,3,2,1,0:T(8,128)(2,1)}), bf16[4,2,2,128,128]{4,3,2,1,0:T(8,128)(2,1)}, u32[]{:S(2)}, u32[]{:S(2)}) %all-to-all-start.2) | async-done | bytes 524320 | tf_op jit(solution)/shard_map/out_far/all_to_all | solution.py:400
  194.5 1.1 convert_reduce_fusion.1
  195.7 3.2 %collective-permute-done.21.refs_4_ = bf16[2,512,128]{2,1,0:T(8,128)(2,1)} collective-permute-done((bf16[2,512,128]{2,1,0:T(8,128)(2,1)}, bf16[2,512,128]{2,1,0:T(8,128)(2,1)}, u32[]{:S(2)}, u32[]{:S(2)}) %collective-permute-start.21) | collective-permute-done | bytes 262176 | tf_op jit(solution)/shard_map/out_pairs0_2/ppermute | solution.py:323
  198.9 3.7 %collective-permute-done.22.refs_6_ = bf16[2,512,128]{2,1,0:T(8,128)(2,1)} collective-permute-done((bf16[2,512,128]{2,1,0:T(8,128)(2,1)}, bf16[2,512,128]{2,1,0:T(8,128)(2,1)}, u32[]{:S(2)}, u32[]{:S(2)}) %collective-permute-start.22) | collective-permute-done | bytes 262176 | tf_op jit(solution)/shard_map/out_pairs0_3/ppermute | solution.py:323
  202.6 11.7 %collective-permute-done.19 = bf16[2,2048,128]{2,1,0:T(8,128)(2,1)} collective-permute-done((bf16[2,2048,128]{2,1,0:T(8,128)(2,1)}, bf16[2,2048,128]{2,1,0:T(8,128)(2,1)}, u32[]{:S(2)}, u32[]{:S(2)}) %collective-permute-start.19) | collective-permute-done | bytes 1048608 | tf_op jit(solution)/shard_map/out_onward1/ppermute | solution.py:319
  214.3 1.6 fusion.5
  216.1 0.2 broadcast_in_dim.101
  216.3 0.8 fusion.9
  217.2 0.8 dynamic-slice_bitcast_fusion
  218.0 0.5 collective-permute-start.24
  218.5 1.3 collective-permute-start.25
  219.8 7.2 %collective-permute-done.24.refs_5_ = bf16[2,512,128]{2,1,0:T(8,128)(2,1)S(1)} collective-permute-done((bf16[2,512,128]{2,1,0:T(8,128)(2,1)S(1)}, bf16[2,512,128]{2,1,0:T(8,128)(2,1)S(1)}, u32[]{:S(2)}, u32[]{:S(2)}) %collective-permute-start.24) | collective-permute-done | bytes 262176 | tf_op jit(solution)/shard_map/out_pairs1_2/ppermute | solution.py:323
  227.1 4.8 %collective-permute-done.25.refs_7_ = bf16[2,512,128]{2,1,0:T(8,128)(2,1)S(1)} collective-permute-done((bf16[2,512,128]{2,1,0:T(8,128)(2,1)S(1)}, bf16[2,512,128]{2,1,0:T(8,128)(2,1)S(1)}, u32[]{:S(2)}, u32[]{:S(2)}) %collective-permute-start.25) | collective-permute-done | bytes 262176 | tf_op jit(solution)/shard_map/out_pairs1_3/ppermute | solution.py:323
  231.9 0.7 copy-done.14
  232.6 3.6 %assemble_pairs.1 = (bf16[512,1024]{1,0:T(8,128)(2,1)}, bf16[512,1024]{1,0:T(8,128)(2,1)}) custom-call(s32[2]{0:T(128)} %copy-done.2, bf16[2,512,128]{2,1,0:T(8,128)(2,1)} %get-tuple-element.80.refs_0_, bf16[2,512,128]{2,1,0:T(8,128)(2,1)} %get-tuple-element.76.refs_1_, bf16[2,512,128]{2,1,0:T(8,128)(2,1)} %copy-done.11, bf16[2,512,128]{2,1,0:T(8,128)(2,1)} %copy-done.12, ...), custom_call_target="tpu_custom_call" | custom-call | tf_op jit(solution)/shard_map/assemble_pairs/pallas_call | solution.py:288
  (77 shorter events, 2.1 us)
Async XLA Ops:
  0.6 1.5 copy-start.9
  0.6 1.6 copy-start.6
  3.5 10.4 %collective-permute-start = (bf16[2,2,128,128]{3,2,1,0:T(8,128)(2,1)S(1)}, bf16[2,2,128,128]{3,2,1,0:T(8,128)(2,1)S(1)}, u32[]{:S(2)}, u32[]{:S(2)}) collective-permute-start(bf16[2,2,128,128]{3,2,1,0:T(8,128)(2,1)S(1)} %pad_maximum_fusion.6), channel_id=1, source_target_pairs={{0,16},{1,17},{2,18},{3,19}} | collective-permute-start | bytes 393224 | tf_op jit(solution)/shard_map/in_first4/ppermute | solution.py:319
  10.4 17.9 %all-to-all-start = ((bf16[4,2,2,128,128]{4,3,2,1,0:T(8,128)(2,1)}), bf16[4,2,2,128,128]{4,3,2,1,0:T(8,128)(2,1)S(1)}, u32[]{:S(2)}, u32[]{:S(2)}) async-start(bf16[4,2,2,128,128]{4,3,2,1,0:T(8,128)(2,1)} %broadcast_in_dim.85), calls=%async_computation | async-start | bytes 1048576 | tf_op jit(solution)/shard_map/in_column/all_to_all | solution.py:341
  13.9 35.9 %copy-start.15 = (s32[16,2]{0,1:T(2,128)S(1)}, s32[16,2]{0,1:T(2,128)}, u32[]{:S(2)}) copy-start(s32[16,2]{0,1:T(2,128)} %param.12) | copy-start | bytes 388
  14.0 36.0 %copy-start.16 = (s32[16,2]{0,1:T(2,128)S(1)}, s32[16,2]{0,1:T(2,128)}, u32[]{:S(2)}) copy-start(s32[16,2]{0,1:T(2,128)} %param.13) | copy-start | bytes 388
  14.0 12.5 %collective-permute-start.1 = (bf16[2,2,128,128]{3,2,1,0:T(8,128)(2,1)S(1)}, bf16[2,2,128,128]{3,2,1,0:T(8,128)(2,1)S(1)}, u32[]{:S(2)}, u32[]{:S(2)}) collective-permute-start(bf16[2,2,128,128]{3,2,1,0:T(8,128)(2,1)S(1)} %broadcast_select_fusion), channel_id=1, source_target_pairs={{0,8},{16,24},{1,9},{17,25},{2,10},{18,26},{3,11},{19,27}} | collective-permute-start | bytes 393224 | tf_op jit(solution)/shard_map/in_first2/ppermute | solution.py:319
  18.9 29.0 %collective-permute-start.3 = (bf16[2,2048,128]{2,1,0:T(8,128)(2,1)}, bf16[2,2048,128]{2,1,0:T(8,128)(2,1)}, u32[]{:S(2)}, u32[]{:S(2)}) collective-permute-start(bf16[2,2048,128]{2,1,0:T(8,128)(2,1)} %pad_maximum_fusion.refs_2_), channel_id=1, source_target_pairs={{0,8},{4,12},{8,16},{12,20},{16,24},{20,28},{1,9},{5,13},{9,17},{1... | collective-permute-start | bytes 3145736 | tf_op jit(solution)/shard_map/in_back0/ppermute | solution.py:319
  28.4 19.4 %collective-permute-start.2 = (bf16[5,2,128,128]{3,2,1,0:T(8,128)(2,1)S(1)}, bf16[5,2,128,128]{3,2,1,0:T(8,128)(2,1)S(1)}, u32[]{:S(2)}, u32[]{:S(2)}) collective-permute-start(bf16[5,2,128,128]{3,2,1,0:T(8,128)(2,1)S(1)} %pad_maximum_fusion.3.refs_3_), channel_id=1, source_target_pairs={{0,4},{4,0},{8,12},{12,8},{16,20},{20,16},{24,28},{28,24},{1,5},{5... | collective-permute-start | bytes 983048 | tf_op jit(solution)/shard_map/in_column_pair0/ppermute | solution.py:319
  28.5 34.8 %collective-permute-start.4 = (bf16[2,2048,128]{2,1,0:T(8,128)(2,1)}, bf16[2,2048,128]{2,1,0:T(8,128)(2,1)}, u32[]{:S(2)}, u32[]{:S(2)}) collective-permute-start(bf16[2,2048,128]{2,1,0:T(8,128)(2,1)} %pad_maximum_fusion.refs_2_), channel_id=1, source_target_pairs={{0,4},{8,12},{16,20},{24,28},{1,5},{9,13},{17,21},{25,29},{2,6},{1... | collective-permute-start | bytes 3145736 | tf_op jit(solution)/shard_map/in_even0/ppermute | solution.py:319
  47.9 28.3 %collective-permute-start.5 = (bf16[2,2048,128]{2,1,0:T(8,128)(2,1)}, bf16[2,2048,128]{2,1,0:T(8,128)(2,1)}, u32[]{:S(2)}, u32[]{:S(2)}) collective-permute-start(bf16[2,2048,128]{2,1,0:T(8,128)(2,1)} %collective-permute-done.3.refs_5_), channel_id=1, source_target_pairs={{4,0},{12,8},{20,16},{28,24},{5,1},{13,9},{21,17},{29,25},{6,2},{1... | collective-permute-start | bytes 3145736 | tf_op jit(solution)/shard_map/in_odd0/ppermute | solution.py:319
  50.1 66.7 %copy-start.2 = (s32[2]{0:T(128)}, s32[2]{0:T(128)S(1)}, u32[]{:S(2)}) copy-start(s32[2]{0:T(128)S(1)} %pad_add_fusion.place) | copy-start | bytes 28
  51.4 63.4 %collective-permute-start.7 = (bf16[2,2048,128]{2,1,0:T(8,128)(2,1)}, bf16[2,2048,128]{2,1,0:T(8,128)(2,1)}, u32[]{:S(2)}, u32[]{:S(2)}) collective-permute-start(bf16[2,2048,128]{2,1,0:T(8,128)(2,1)} %pad_maximum_fusion.1.refs_2_), channel_id=1, source_target_pairs={{0,8},{4,12},{8,16},{12,20},{16,24},{20,28},{1,9},{5,13},{9,17},{1... | collective-permute-start | bytes 3145736 | tf_op jit(solution)/shard_map/in_back1/ppermute | solution.py:319
  56.8 60.0 %collective-permute-start.8 = (bf16[2,2048,128]{2,1,0:T(8,128)(2,1)}, bf16[2,2048,128]{2,1,0:T(8,128)(2,1)}, u32[]{:S(2)}, u32[]{:S(2)}) collective-permute-start(bf16[2,2048,128]{2,1,0:T(8,128)(2,1)} %pad_maximum_fusion.1.refs_2_), channel_id=1, source_target_pairs={{0,4},{4,8},{8,12},{12,16},{16,20},{20,24},{24,28},{1,5},{5,9},{9,... | collective-permute-start | bytes 3145736 | tf_op jit(solution)/shard_map/in_prev1/ppermute | solution.py:319
  63.3 50.7 %collective-permute-start.6 = (bf16[5,2,128,128]{3,2,1,0:T(8,128)(2,1)S(1)}, bf16[5,2,128,128]{3,2,1,0:T(8,128)(2,1)S(1)}, u32[]{:S(2)}, u32[]{:S(2)}) collective-permute-start(bf16[5,2,128,128]{3,2,1,0:T(8,128)(2,1)S(1)} %pad_maximum_fusion.4.refs_3_), channel_id=1, source_target_pairs={{0,4},{4,0},{8,12},{12,8},{16,20},{20,16},{24,28},{28,24},{1,5},{5... | collective-permute-start | bytes 983048 | tf_op jit(solution)/shard_map/in_column_pair1/ppermute | solution.py:319
  106.0 0.8 copy-start
  106.8 43.8 %collective-permute-start.9 = (bf16[512,512]{1,0:T(8,128)(2,1)}, bf16[512,512]{1,0:T(8,128)(2,1)}, u32[]{:S(2)}, u32[]{:S(2)}) collective-permute-start(bf16[512,512]{1,0:T(8,128)(2,1)} %get-tuple-element.48), channel_id=1, source_target_pairs={{0,1},{1,0},{2,3},{3,2},{4,5},{5,4},{6,7},{7,6},{8,9},{9,8},{10,11... | collective-permute-start | bytes 1572872 | tf_op jit(solution)/shard_map/out_query0_1/ppermute | solution.py:323
  106.8 43.8 %collective-permute-start.10 = (bf16[512,512]{1,0:T(8,128)(2,1)}, bf16[512,512]{1,0:T(8,128)(2,1)}, u32[]{:S(2)}, u32[]{:S(2)}) collective-permute-start(bf16[512,512]{1,0:T(8,128)(2,1)} %get-tuple-element.49), channel_id=1, source_target_pairs={{0,2},{1,3},{2,0},{3,1},{4,6},{5,7},{6,4},{7,5},{8,10},{9,11},{10,... | collective-permute-start | bytes 1572872 | tf_op jit(solution)/shard_map/out_query0_2/ppermute | solution.py:323
  108.3 42.3 %all-to-all-start.1 = ((bf16[8,2,2,128,128]{4,3,2,1,0:T(8,128)(2,1)}), bf16[8,2,2,128,128]{4,3,2,1,0:T(8,128)(2,1)}, u32[]{:S(2)}, u32[]{:S(2)}) async-start(bf16[8,2,2,128,128]{4,3,2,1,0:T(8,128)(2,1)} %get-tuple-element.51), calls=%async_computation.1 | async-start | bytes 2097152 | tf_op jit(solution)/shard_map/out_far0/all_to_all | solution.py:378
  114.0 0.7 copy-start.3
  114.8 35.8 %collective-permute-start.11 = (bf16[512,512]{1,0:T(8,128)(2,1)}, bf16[512,512]{1,0:T(8,128)(2,1)}, u32[]{:S(2)}, u32[]{:S(2)}) collective-permute-start(bf16[512,512]{1,0:T(8,128)(2,1)} %get-tuple-element.50), channel_id=1, source_target_pairs={{0,3},{1,2},{2,1},{3,0},{4,7},{5,6},{6,5},{7,4},{8,11},{9,10},{10,... | collective-permute-start | bytes 1572872 | tf_op jit(solution)/shard_map/out_query0_3/ppermute | solution.py:323
  114.9 35.7 %collective-permute-start.12 = (bf16[2,2048,128]{2,1,0:T(8,128)(2,1)S(1)}, bf16[2,2048,128]{2,1,0:T(8,128)(2,1)}, u32[]{:S(2)}, u32[]{:S(2)}) collective-permute-start(bf16[2,2048,128]{2,1,0:T(8,128)(2,1)S(1)} %get-tuple-element.53), channel_id=1, source_target_pairs={{0,4},{4,0},{8,12},{12,8},{16,20},{20,16},{24,28},{28,24},{1,5},{5... | collective-permute-start | bytes 3145736 | tf_op jit(solution)/shard_map/out_pair0/ppermute | solution.py:319
  116.8 1.0 copy-start.4
  147.0 0.8 copy-start.1
  147.8 0.7 copy-start.5
  150.6 9.0 %collective-permute-start.13 = (bf16[5,2,128,128]{3,2,1,0:T(8,128)(2,1)}, bf16[5,2,128,128]{3,2,1,0:T(8,128)(2,1)S(1)}, u32[]{:S(2)}, u32[]{:S(2)}) collective-permute-start(bf16[5,2,128,128]{3,2,1,0:T(8,128)(2,1)} %copy-done.5), channel_id=1, source_target_pairs={{0,4},{4,0},{8,12},{12,8},{16,20},{20,16},{24,28},{28,24},{1,5},{5... | collective-permute-start | bytes 983048 | tf_op jit(solution)/shard_map/out_far_pair1/ppermute | solution.py:319
  151.0 16.8 %collective-permute-start.15 = (bf16[512,512]{1,0:T(8,128)(2,1)S(1)}, bf16[512,512]{1,0:T(8,128)(2,1)}, u32[]{:S(2)}, u32[]{:S(2)}) collective-permute-start(bf16[512,512]{1,0:T(8,128)(2,1)S(1)} %get-tuple-element.64), channel_id=1, source_target_pairs={{0,2},{1,3},{2,0},{3,1},{4,6},{5,7},{6,4},{7,5},{8,10},{9,11},{10,... | collective-permute-start | bytes 1572872 | tf_op jit(solution)/shard_map/out_query1_2/ppermute | solution.py:323
  151.5 21.9 %collective-permute-start.16 = (bf16[512,512]{1,0:T(8,128)(2,1)S(1)}, bf16[512,512]{1,0:T(8,128)(2,1)}, u32[]{:S(2)}, u32[]{:S(2)}) collective-permute-start(bf16[512,512]{1,0:T(8,128)(2,1)S(1)} %get-tuple-element.65), channel_id=1, source_target_pairs={{0,3},{1,2},{2,1},{3,0},{4,7},{5,6},{6,5},{7,4},{8,11},{9,10},{10,... | collective-permute-start | bytes 1572872 | tf_op jit(solution)/shard_map/out_query1_3/ppermute | solution.py:323
  154.4 29.9 %collective-permute-start.17 = (bf16[2,2048,128]{2,1,0:T(8,128)(2,1)}, bf16[2,2048,128]{2,1,0:T(8,128)(2,1)}, u32[]{:S(2)}, u32[]{:S(2)}) collective-permute-start(bf16[2,2048,128]{2,1,0:T(8,128)(2,1)} %fusion.3), channel_id=1, source_target_pairs={{8,0},{12,4},{16,8},{20,12},{24,16},{28,20},{9,1},{13,5},{17,9},{2... | collective-permute-start | bytes 3145736 | tf_op jit(solution)/shard_map/out_onward0/ppermute | solution.py:319
  155.6 25.8 %collective-permute-start.18 = (bf16[2,2048,128]{2,1,0:T(8,128)(2,1)}, bf16[2,2048,128]{2,1,0:T(8,128)(2,1)S(1)}, u32[]{:S(2)}, u32[]{:S(2)}) collective-permute-start(bf16[2,2048,128]{2,1,0:T(8,128)(2,1)} %get-tuple-element.68), channel_id=1, source_target_pairs={{0,4},{4,0},{8,12},{12,8},{16,20},{20,16},{24,28},{28,24},{1,5},{5... | collective-permute-start | bytes 3145736 | tf_op jit(solution)/shard_map/out_pair1/ppermute | solution.py:319
  159.8 13.5 %collective-permute-start.14 = (bf16[512,512]{1,0:T(8,128)(2,1)S(1)}, bf16[512,512]{1,0:T(8,128)(2,1)}, u32[]{:S(2)}, u32[]{:S(2)}) collective-permute-start(bf16[512,512]{1,0:T(8,128)(2,1)S(1)} %get-tuple-element.63), channel_id=1, source_target_pairs={{0,1},{1,0},{2,3},{3,2},{4,5},{5,4},{6,7},{7,6},{8,9},{9,8},{10,11... | collective-permute-start | bytes 1572872 | tf_op jit(solution)/shard_map/out_query1_1/ppermute | solution.py:323
  162.2 32.3 %all-to-all-start.2 = ((bf16[4,2,2,128,128]{4,3,2,1,0:T(8,128)(2,1)}), bf16[4,2,2,128,128]{4,3,2,1,0:T(8,128)(2,1)}, u32[]{:S(2)}, u32[]{:S(2)}) async-start(bf16[4,2,2,128,128]{4,3,2,1,0:T(8,128)(2,1)} %copy.26), calls=%async_computation.2 | async-start | bytes 1048576 | tf_op jit(solution)/shard_map/out_far/all_to_all | solution.py:400
  173.3 8.1 %copy-start.10 = (bf16[2,2048,128]{2,1,0:T(8,128)(2,1)S(1)}, bf16[2,2048,128]{2,1,0:T(8,128)(2,1)}, u32[]{:S(2)}) copy-start(bf16[2,2048,128]{2,1,0:T(8,128)(2,1)} %get-tuple-element.69) | copy-start | bytes 3145732
  178.9 5.4 %copy-start.8 = (f32[2,2048,128]{2,1,0:T(8,128)S(1)}, f32[2,2048,128]{2,1,0:T(8,128)}, u32[]{:S(2)}) copy-start(f32[2,2048,128]{2,1,0:T(8,128)} %get-tuple-element.56) | copy-start | bytes 6291460
  182.8 31.5 %collective-permute-start.19 = (bf16[2,2048,128]{2,1,0:T(8,128)(2,1)}, bf16[2,2048,128]{2,1,0:T(8,128)(2,1)}, u32[]{:S(2)}, u32[]{:S(2)}) collective-permute-start(bf16[2,2048,128]{2,1,0:T(8,128)(2,1)} %fusion.7), channel_id=1, source_target_pairs={{8,0},{12,4},{16,8},{20,12},{24,16},{28,20},{9,1},{13,5},{17,9},{2... | collective-permute-start | bytes 3145736 | tf_op jit(solution)/shard_map/out_onward1/ppermute | solution.py:319
  187.5 26.7 %copy-start.7 = (f32[2,2048,128]{2,1,0:T(8,128)S(1)}, f32[2,2048,128]{2,1,0:T(8,128)}, u32[]{:S(2)}) copy-start(f32[2,2048,128]{2,1,0:T(8,128)} %get-tuple-element.66) | copy-start | bytes 6291460
  188.6 7.1 %collective-permute-start.20 = (bf16[2,512,128]{2,1,0:T(8,128)(2,1)}, bf16[2,512,128]{2,1,0:T(8,128)(2,1)S(1)}, u32[]{:S(2)}, u32[]{:S(2)}) collective-permute-start(bf16[2,512,128]{2,1,0:T(8,128)(2,1)} %get-tuple-element.79), channel_id=1, source_target_pairs={{0,1},{1,0},{2,3},{3,2},{4,5},{5,4},{6,7},{7,6},{8,9},{9,8},{10,11... | collective-permute-start | bytes 786440 | tf_op jit(solution)/shard_map/out_pairs0_1/ppermute | solution.py:323
  189.4 9.5 %collective-permute-start.21 = (bf16[2,512,128]{2,1,0:T(8,128)(2,1)}, bf16[2,512,128]{2,1,0:T(8,128)(2,1)}, u32[]{:S(2)}, u32[]{:S(2)}) collective-permute-start(bf16[2,512,128]{2,1,0:T(8,128)(2,1)} %get-tuple-element.78), channel_id=1, source_target_pairs={{0,2},{1,3},{2,0},{3,1},{4,6},{5,7},{6,4},{7,5},{8,10},{9,11},{10,... | collective-permute-start | bytes 786440 | tf_op jit(solution)/shard_map/out_pairs0_2/ppermute | solution.py:323
  190.2 12.3 %collective-permute-start.22 = (bf16[2,512,128]{2,1,0:T(8,128)(2,1)}, bf16[2,512,128]{2,1,0:T(8,128)(2,1)}, u32[]{:S(2)}, u32[]{:S(2)}) collective-permute-start(bf16[2,512,128]{2,1,0:T(8,128)(2,1)} %get-tuple-element.77), channel_id=1, source_target_pairs={{0,3},{1,2},{2,1},{3,0},{4,7},{5,6},{6,5},{7,4},{8,11},{9,10},{10,... | collective-permute-start | bytes 786440 | tf_op jit(solution)/shard_map/out_pairs0_3/ppermute | solution.py:323
  195.7 20.2 %copy-start.11 = (bf16[2,512,128]{2,1,0:T(8,128)(2,1)}, bf16[2,512,128]{2,1,0:T(8,128)(2,1)S(1)}, u32[]{:S(2)}) copy-start(bf16[2,512,128]{2,1,0:T(8,128)(2,1)S(1)} %collective-permute-done.20.refs_2_) | copy-start | bytes 786436
  217.9 1.9 collective-permute-start.23
  218.0 9.1 %collective-permute-start.24 = (bf16[2,512,128]{2,1,0:T(8,128)(2,1)S(1)}, bf16[2,512,128]{2,1,0:T(8,128)(2,1)S(1)}, u32[]{:S(2)}, u32[]{:S(2)}) collective-permute-start(bf16[2,512,128]{2,1,0:T(8,128)(2,1)S(1)} %get-tuple-element.74), channel_id=1, source_target_pairs={{0,2},{1,3},{2,0},{3,1},{4,6},{5,7},{6,4},{7,5},{8,10},{9,11},{10,... | collective-permute-start | bytes 786440 | tf_op jit(solution)/shard_map/out_pairs1_2/ppermute | solution.py:323
  218.5 13.4 %collective-permute-start.25 = (bf16[2,512,128]{2,1,0:T(8,128)(2,1)S(1)}, bf16[2,512,128]{2,1,0:T(8,128)(2,1)S(1)}, u32[]{:S(2)}, u32[]{:S(2)}) collective-permute-start(bf16[2,512,128]{2,1,0:T(8,128)(2,1)S(1)} %get-tuple-element.73), channel_id=1, source_target_pairs={{0,3},{1,2},{2,1},{3,0},{4,7},{5,6},{6,5},{7,4},{8,11},{9,10},{10,... | collective-permute-start | bytes 786440 | tf_op jit(solution)/shard_map/out_pairs1_3/ppermute | solution.py:323
  219.8 12.1 %copy-start.12 = (bf16[2,512,128]{2,1,0:T(8,128)(2,1)}, bf16[2,512,128]{2,1,0:T(8,128)(2,1)S(1)}, u32[]{:S(2)}) copy-start(bf16[2,512,128]{2,1,0:T(8,128)(2,1)S(1)} %collective-permute-done.23.refs_3_) | copy-start | bytes 786436
  227.1 4.8 %copy-start.13 = (bf16[2,512,128]{2,1,0:T(8,128)(2,1)}, bf16[2,512,128]{2,1,0:T(8,128)(2,1)S(1)}, u32[]{:S(2)}) copy-start(bf16[2,512,128]{2,1,0:T(8,128)(2,1)S(1)} %collective-permute-done.24.refs_5_) | copy-start | bytes 786436
  231.9 0.7 copy-start.14

commit v4 on v3

--- a/solution.py
+++ b/solution.py
@@ -15,7 +15,7 @@
 
 
 def attention_kernel(dims, place, vertical, columns, offsets, *refs):
-    local_blocks, group, vert_total, heads, last = dims
+    local_blocks, group, vert_total, heads, head, last = dims
     refs = list(refs)
 
     def take(count):
@@ -23,7 +23,7 @@
         del refs[:count]
         return taken
 
-    q_ref, do_ref, kv_own, kv_column, kv_other = take(5)
+    q_ref, do_ref, kv_own, kv_column, kv_other, first_even, first_odd = take(7)
     kv_back, kv_even, kv_odd = take(3)
     dq_refs, (own_ref, prev_ref, back_ref), far_refs = take(heads), take(3), take(2 if last else 1)
     pool_k, pool_v, acc_k, acc_v, dq_out, sems = refs
@@ -48,8 +48,8 @@
                     for plane in range(vert_total // 2):
                         into = pool.at[pl.ds(3 * rows + (2 * plane + number) * BLK, BLK)]
                         made.append((ref.at[plane, side], into))
-                source = kv_other if parity else kv_column
-                made.append((source.at[vert_total // 2, side], pool.at[pl.ds(3 * rows + vert_total * BLK, BLK)]))
+                source = first_odd if parity else first_even
+                made.append((source.at[head, side], pool.at[pl.ds(3 * rows + vert_total * BLK, BLK)]))
             return [pltpu.make_async_copy(*ends, sems.at[at]) for at, ends in enumerate(made)]
 
         odd = lax.rem(seq_index, 2) == 1
@@ -186,7 +186,7 @@
 
 
 def attention(
-    head, kv_local, heads, place, vertical, columns, offsets, queries, grad_out, kv_own, kv_column, kv_other,
+    head, kv_local, heads, place, vertical, columns, offsets, queries, grad_out, kv_own, kv_column, kv_other, first_even, first_odd,
     kv_back, kv_even, kv_odd
 ):
     seq_len = queries.shape[0]
@@ -213,11 +213,11 @@
     far_shapes = [(vert_total // 2 + 1, *block_shape)] * 2 if last else [(vert_total, 2, *block_shape)]
     flops = 2 * 5 * seq_len * group * 6 * BLK * HD
     outs = pl.pallas_call(
-        functools.partial(attention_kernel, (local_blocks, group, vert_total, heads, last)),
+        functools.partial(attention_kernel, (local_blocks, group, vert_total, heads, head, last)),
         grid_spec=pltpu.PrefetchScalarGridSpec(
             num_scalar_prefetch=4,
             grid=(local_blocks // together,),
-            in_specs=[by_block, by_block] + [anywhere] * 6,
+            in_specs=[by_block, by_block] + [anywhere] * 8,
             out_specs=[share_spec(k) for k in range(heads)]
             + [whole(*near_shape)] * 3
             + [whole(*shape) for shape in far_shapes],
@@ -239,7 +239,7 @@
             flops=4 * flops, bytes_accessed=20 * 1024 * 1024, transcendentals=seq_len * group * 6 * BLK
         ),
         name="attention",
-    )(place, vertical, columns, offsets, queries, grad_out, kv_own, kv_column, kv_other, kv_back, kv_even, kv_odd)
+    )(place, vertical, columns, offsets, queries, grad_out, kv_own, kv_column, kv_other, first_even, first_odd, kv_back, kv_even, kv_odd)
     return outs[:heads], *outs[heads:]
 
 
@@ -312,7 +312,6 @@
     head_index = lax.axis_index("head")
     place = jnp.stack([seq_index, head_index]).astype(jnp.int32)
     odd = seq_index % 2 == 1
-    levels = [1 << level for level in range(int(math.log2(seq_size)))]
 
     def along(array, pairs, name):
         with jax.named_scope(name):
@@ -340,26 +339,24 @@
             wide = jnp.broadcast_to(block, (seq_size // 2, *block.shape))
             return lax.all_to_all(wide, "seq", split_axis=0, concat_axis=0, axis_index_groups=groups)
 
-    first = sink
-    for hop in reversed(levels[1:]):
-        got = along(first, [(i, i + hop) for i in range(0, seq_size, 2 * hop)], f"in_first{hop}")
-        first = jnp.where(seq_index % (2 * hop) == hop, got, first)
-
-    column = column_of(mine, "in_column")
-    kv_columns = [jnp.concatenate([column[:, head], first[None, head]]) for head in range(kv_local)]
+    first = jnp.where(seq_index == 0, sink, 0.0).astype(sink.dtype)
+    first = sum((along(sink, [(0, at)], f"in_first{at}") for at in range(2, seq_size, 2)), first)
+    first_other = along(first, [(at, at + 1) for at in range(0, seq_size, 2)], "in_first_pair")
 
     fetched = []
     for head, kv in enumerate(kvs):
-        kv_column = kv_columns[head]
+        block = mine[head]
         if head:
-            kv, kv_column = after((kv, kv_column), fetched[-1][1], fetched[-1][5])
-        kv_other = along(kv_column, exchange, f"in_column_pair{head}")
-        if head:
+            kv, block = after((kv, block), fetched[-1][1], fetched[-1][4])
             back, even = along(kv, shift(2), f"in_back{head}"), along(kv, shift(1), f"in_prev{head}")
             odd_prev = even
         else:
             back, even = along(kv, shift(2), f"in_back{head}"), along(kv, shift(1, 0), f"in_even{head}")
-            odd_prev = along(after(back, kv_other), shift(-1, 1), f"in_odd{head}")
+            odd_prev = along(back, shift(-1, 1), f"in_odd{head}")
+        kv_column = column_of(block, f"in_column{head}")
+        if not head:
+            kv_column = after(kv_column, back)
+        kv_other = along(kv_column, exchange, f"in_column_pair{head}")
         fetched.append((kv, back, even, odd_prev, kv_column, kv_other))
 
     planes = seq_size // 2
@@ -371,7 +368,8 @@
     for head, (kv, back, even, odd_prev, kv_column, kv_other) in enumerate(fetched):
         last = head + 1 == kv_local
         dqs, own, prev, back, *table = attention(
-            head, kv_local, heads, place, vertical, columns, offsets, queries, grad_out, kv, kv_column, kv_other, back, even, odd_prev
+            head, kv_local, heads, place, vertical, columns, offsets, queries, grad_out, kv, kv_column, kv_other, first, first_other,
+            back, even, odd_prev
         )
         if not last:
             with jax.named_scope(f"out_far{head}"):
@@ -389,7 +387,8 @@
         for k in range(2, heads):
             query_pieces[k, head] = across(dqs[k], k, f"out_query{head}_{k}")
         sent = [onward(back_before, side_before) for _, side_before, back_before in results]
-        side = along(after(prev, sent), exchange, f"out_pair{head}")
+        side = along(prev, exchange, f"out_pair{head}")
+        side = after(side, [query_pieces[k, head] for k in range(2, heads)])
         results = [
             (own_before, side_before, along(piece, shift(-2), f"out_onward{at}"))
             for at, ((own_before, side_before, _), piece) in enumerate(zip(results, sent))

time: 238 us -> 228 us (0.958)
  waiting for transfers between devices: 81.3 us -> 69.4 us
    ppermute x14 -> x16, waiting for transfers between devices: 51.1 us -> 31.7 us  [along(): return lax.ppermute(array, 'seq', pairs)]
    all_to_all x1 -> x2, waiting for transfers between devices: 1.84 us -> 9.36 us  [column_of(): lax.all_to_all(wide, 'seq', split_axis=0, concat_axis=0, axis_index_group...]
    all_to_all x1 -> x2, starting transfers between devices: 3.47 us -> 8.28 us  [column_of(): lax.all_to_all(wide, 'seq', split_axis=0, concat_axis=0, axis_index_group...]
    ppermute x14 -> x16, starting transfers between devices: 37.1 us -> 33.6 us  [along(): return lax.ppermute(array, 'seq', pairs)]
  transfers between devices with their start and end apart: 29 -> 32, of which waited for: 14 -> 13; matrix products, arithmetic and copies ran while one was open for 7% -> 7% of each run, Pallas kernels for 27% -> 29%
where the time goes in v4:
time: 228 us; the launch traced here: 226 us
  waiting for transfers between devices  69.4 us (30%)
  Pallas kernels  68.1 us (30%)
  starting transfers between devices  60.1 us (26%)
  other arithmetic  14 us (6%)
  local copies, waits for them, and re-layouts  12.5 us (5%)
    pallas_call x2, Pallas kernels, attention(): pl.pallas_call(functools.partial(attention_kernel, (local_blocks, group,...  59 us
    ppermute x16, starting transfers between devices, along(): return lax.ppermute(array, 'seq', pairs)  33.6 us
    ppermute x16, waiting for transfers between devices, along(): return lax.ppermute(array, 'seq', pairs)  31.7 us
    ppermute x12, waiting for transfers between devices, across(): lax.ppermute(array, 'head', [(i, i ^ k) for i in range(heads)])  24.5 us
    all_to_all x2, waiting for transfers between devices, column_of(): lax.all_to_all(wide, 'seq', split_axis=0, concat_axis=0, axis_index_group...  9.36 us
    all_to_all x2, starting transfers between devices, column_of(): lax.all_to_all(wide, 'seq', split_axis=0, concat_axis=0, axis_index_group...  8.28 us
    all_to_all x1, starting transfers between devices, shards(): fars.append(lax.all_to_all(table[0], 'seq', split_axis=0, concat_axis=0))  6.52 us
    ppermute x12, starting transfers between devices, across(): lax.ppermute(array, 'head', [(i, i ^ k) for i in range(heads)])  6.2 us
  transfers between devices with their start and end apart: 32, of which 13 were waited for; matrix products, arithmetic and copies ran while one was open for 7% of the time, Pallas kernels for 29%

profile of v4, /device:TPU:0, one launch (start us, length us, event | category | flops | bytes accessed | tf_op | source)
XLA Modules:
  0.0 225.8 jit_solution(6885467361467488826)
XLA Ops:
  0.6 1.7 slice_bitcast_fusion
  2.3 1.1 pad_maximum_fusion.refs_2_
  3.4 6.0 %collective-permute-start = (bf16[2,2048,128]{2,1,0:T(8,128)(2,1)}, bf16[2,2048,128]{2,1,0:T(8,128)(2,1)}, u32[]{:S(2)}, u32[]{:S(2)}) collective-permute-start(bf16[2,2048,128]{2,1,0:T(8,128)(2,1)} %pad_maximum_fusion.refs_2_), channel_id=1, source_target_pairs={{0,8},{4,12},{8,16},{12,20},{16,24},{20,28},{1,9},{5,13},{9,17},{1... | collective-permute-start | bytes 3145736 | tf_op jit(solution)/shard_map/in_back0/ppermute | solution.py:318
  9.4 0.6 dynamic_slice.34
  10.7 2.3 %collective-permute-start.4 = (bf16[2,2,128,128]{3,2,1,0:T(8,128)(2,1)S(1)}, bf16[2,2,128,128]{3,2,1,0:T(8,128)(2,1)S(1)}, u32[]{:S(2)}, u32[]{:S(2)}) collective-permute-start(bf16[2,2,128,128]{3,2,1,0:T(8,128)(2,1)S(1)} %pad_maximum_fusion.3), channel_id=1, source_target_pairs={{0,24},{1,25},{2,26},{3,27}} | collective-permute-start | bytes 393224 | tf_op jit(solution)/shard_map/in_first6/ppermute | solution.py:318
  13.0 1.9 collective-permute-start.3
  14.8 1.3 collective-permute-start.2
  16.1 2.3 %collective-permute-start.6 = (bf16[2,2048,128]{2,1,0:T(8,128)(2,1)}, bf16[2,2048,128]{2,1,0:T(8,128)(2,1)}, u32[]{:S(2)}, u32[]{:S(2)}) collective-permute-start(bf16[2,2048,128]{2,1,0:T(8,128)(2,1)} %pad_maximum_fusion.refs_2_), channel_id=1, source_target_pairs={{0,4},{8,12},{16,20},{24,28},{1,5},{9,13},{17,21},{25,29},{2,6},{1... | collective-permute-start | bytes 3145736 | tf_op jit(solution)/shard_map/in_even0/ppermute | solution.py:318
  18.5 0.7 broadcast_in_dim.92
  19.2 3.5 %all-to-all-start = ((bf16[4,2,128,128]{3,2,1,0:T(8,128)(2,1)}), bf16[4,2,128,128]{3,2,1,0:T(8,128)(2,1)S(1)}, u32[]{:S(2)}, u32[]{:S(2)}) async-start(bf16[4,2,128,128]{3,2,1,0:T(8,128)(2,1)} %broadcast_in_dim.92), calls=%async_computation | async-start | bytes 524288 | tf_op jit(solution)/shard_map/in_column0/all_to_all | solution.py:340
  22.7 9.4 %collective-permute-done.refs_7_ = bf16[2,2048,128]{2,1,0:T(8,128)(2,1)} collective-permute-done((bf16[2,2048,128]{2,1,0:T(8,128)(2,1)}, bf16[2,2048,128]{2,1,0:T(8,128)(2,1)}, u32[]{:S(2)}, u32[]{:S(2)}) %collective-permute-start) | collective-permute-done | bytes 1048608 | tf_op jit(solution)/shard_map/in_back0/ppermute | solution.py:318
  32.2 1.3 collective-permute-start.7
  33.7 0.7 fusion.21
  34.4 9.4 %all-to-all-done.refs_3_ = bf16[4,2,128,128]{3,2,1,0:T(8,128)(2,1)S(1)} async-done(((bf16[4,2,128,128]{3,2,1,0:T(8,128)(2,1)}), bf16[4,2,128,128]{3,2,1,0:T(8,128)(2,1)S(1)}, u32[]{:S(2)}, u32[]{:S(2)}) %all-to-all-start) | async-done | bytes 262176 | tf_op jit(solution)/shard_map/in_column0/all_to_all | solution.py:340
  43.7 0.7 broadcast_in_dim.94
  44.4 4.7 %all-to-all-start.1 = ((bf16[4,2,128,128]{3,2,1,0:T(8,128)(2,1)}), bf16[4,2,128,128]{3,2,1,0:T(8,128)(2,1)S(1)}, u32[]{:S(2)}, u32[]{:S(2)}) async-start(bf16[4,2,128,128]{3,2,1,0:T(8,128)(2,1)} %broadcast_in_dim.94), calls=%async_computation.1 | async-start | bytes 524288 | tf_op jit(solution)/shard_map/in_column1/all_to_all | solution.py:340
  49.2 1.8 collective-permute-start.5
  51.5 4.9 %collective-permute-start.9 = (bf16[2,2048,128]{2,1,0:T(8,128)(2,1)S(1)}, bf16[2,2048,128]{2,1,0:T(8,128)(2,1)}, u32[]{:S(2)}, u32[]{:S(2)}) collective-permute-start(bf16[2,2048,128]{2,1,0:T(8,128)(2,1)S(1)} %pad_maximum_fusion.1.refs_2_), channel_id=1, source_target_pairs={{0,8},{4,12},{8,16},{12,20},{16,24},{20,28},{1,9},{5,13},{9,17},{1... | collective-permute-start | bytes 3145736 | tf_op jit(solution)/shard_map/in_back1/ppermute | solution.py:318
  56.4 4.9 %collective-permute-start.10 = (bf16[2,2048,128]{2,1,0:T(8,128)(2,1)S(1)}, bf16[2,2048,128]{2,1,0:T(8,128)(2,1)}, u32[]{:S(2)}, u32[]{:S(2)}) collective-permute-start(bf16[2,2048,128]{2,1,0:T(8,128)(2,1)S(1)} %pad_maximum_fusion.1.refs_2_), channel_id=1, source_target_pairs={{0,4},{4,8},{8,12},{12,16},{16,20},{20,24},{24,28},{1,5},{5,9},{9,... | collective-permute-start | bytes 3145736 | tf_op jit(solution)/shard_map/in_prev1/ppermute | solution.py:318
  61.3 3.8 %collective-permute-done.1.refs_4_ = bf16[4,2,128,128]{3,2,1,0:T(8,128)(2,1)S(1)} collective-permute-done((bf16[4,2,128,128]{3,2,1,0:T(8,128)(2,1)S(1)}, bf16[4,2,128,128]{3,2,1,0:T(8,128)(2,1)S(1)}, u32[]{:S(2)}, u32[]{:S(2)}) %collective-permute-start.1) | collective-permute-done | bytes 262176 | tf_op jit(solution)/shard_map/in_column_pair0/ppermute | solution.py:318
  65.0 29.8 %attention.2 = (bf16[512,512]{1,0:T(8,128)(2,1)S(1)}, bf16[512,512]{1,0:T(8,128)(2,1)}, bf16[512,512]{1,0:T(8,128)(2,1)}, bf16[512,512]{1,0:T(8,128)(2,1)}, f32[...) custom-call(s32[2]{0:T(128)S(1)} %pad_add_fusion.place, ...), custom_call_target="tpu_custom_call" | custom-call | flops 32212254720 | bytes 20971520 | tf_op jit(solution)/shard_map/attention/pallas_call | solution.py:215
  94.9 0.8 copy-done
  95.6 1.5 collective-permute-start.12
  97.1 6.5 %all-to-all-start.2 = ((bf16[8,2,2,128,128]{4,3,2,1,0:T(8,128)(2,1)}), bf16[8,2,2,128,128]{4,3,2,1,0:T(8,128)(2,1)}, u32[]{:S(2)}, u32[]{:S(2)}) async-start(bf16[8,2,2,128,128]{4,3,2,1,0:T(8,128)(2,1)} %get-tuple-element.51), calls=%async_computation.2 | async-start | bytes 2097152 | tf_op jit(solution)/shard_map/out_far0/all_to_all | solution.py:376
  103.7 0.7 copy-done.4
  104.5 1.9 collective-permute-start.14
  106.4 0.9 copy-done.5
  107.4 29.2 %attention.3 = (bf16[512,512]{1,0:T(8,128)(2,1)S(1)}, bf16[512,512]{1,0:T(8,128)(2,1)S(1)}, bf16[512,512]{1,0:T(8,128)(2,1)S(1)}, bf16[512,512]{1,0:T(8,128)(2,1...) custom-call(s32[2]{0:T(128)S(1)} %pad_add_fusion.place, ...), custom_call_target="tpu_custom_call" | custom-call | flops 32212254720 | bytes 20971520 | tf_op jit(solution)/shard_map/attention/pallas_call | solution.py:215
  136.6 0.8 copy-done.1
  137.4 0.7 copy-done.3
  138.1 2.1 collective-permute-done.14
  140.6 0.5 collective-permute-start.17
  141.1 2.9 %fusion.3 = bf16[2,2048,128]{2,1,0:T(8,128)(2,1)} fusion(bf16[2,2048,128]{2,1,0:T(8,128)(2,1)} %collective-permute-done.14, bf16[2,2048,128]{2,1,0:T(8,128)(2,1)} %get-tuple-element.58, pred[]{:T(512)S(6)} %eq.33), kind=kLoop, calls=%fused_computation.7 | loop fusion | flops 2621440 | bytes 3145729 | tf_op jit(solution)/shard_map/convert_element_type | solution.py:366
  144.0 1.3 collective-permute-start.19
  145.3 1.8 collective-permute-start.20
  147.1 2.2 collective-permute-done.15
  149.6 1.4 convert_reduce_fusion
  151.0 0.9 copy.24
  151.9 5.5 %all-to-all-start.3 = ((bf16[4,2,2,128,128]{4,3,2,1,0:T(8,128)(2,1)}), bf16[4,2,2,128,128]{4,3,2,1,0:T(8,128)(2,1)}, u32[]{:S(2)}, u32[]{:S(2)}) async-start(bf16[4,2,2,128,128]{4,3,2,1,0:T(8,128)(2,1)} %copy.24), calls=%async_computation.3 | async-start | bytes 1048576 | tf_op jit(solution)/shard_map/out_far/all_to_all | solution.py:399
  157.4 5.6 %collective-permute-done.18.refs_7_ = bf16[512,512]{1,0:T(8,128)(2,1)} collective-permute-done((bf16[512,512]{1,0:T(8,128)(2,1)S(1)}, bf16[512,512]{1,0:T(8,128)(2,1)}, u32[]{:S(2)}, u32[]{:S(2)}) %collective-permute-start.18) | collective-permute-done | bytes 524320 | tf_op jit(solution)/shard_map/out_query1_3/ppermute | solution.py:322
  163.0 5.6 %assemble_queries.1 = bf16[512,4096]{1,0:T(8,128)(2,1)} custom-call(s32[2]{0:T(128)} %copy-done.2, bf16[512,512]{1,0:T(8,128)(2,1)} %copy-done, bf16[512,512]{1,0:T(8,128)(2,1)} %copy-done.1, bf16[512,512]{1,0:T(8,128)(2,1)} %collective-permute-done.11.refs_2_, bf16[512,512]{1,0:T(8,128)(2,1)} %collective-permute-done.16.refs_3_, ...), custom_call_target="tpu_custom_call" | custom-call | tf_op jit(solution)/shard_map/assemble_queries/pallas_call | solution.py:259
  168.6 2.5 %collective-permute-done.20 = bf16[2,2048,128]{2,1,0:T(8,128)(2,1)S(1)} collective-permute-done((bf16[2,2048,128]{2,1,0:T(8,128)(2,1)}, bf16[2,2048,128]{2,1,0:T(8,128)(2,1)S(1)}, u32[]{:S(2)}, u32[]{:S(2)}) %collective-permute-start.20) | collective-permute-done | bytes 1048608 | tf_op jit(solution)/shard_map/out_pair1/ppermute | solution.py:318
  171.1 1.3 fusion.7
  172.4 1.5 collective-permute-start.21
  173.9 1.9 fusion.1
  176.4 0.8 fusion.12
  177.2 1.0 dynamic-slice_bitcast_fusion.4
  178.2 0.8 collective-permute-start.22
  179.0 0.8 collective-permute-start.23
  179.8 0.5 collective-permute-start.24
  180.4 3.8 %all-to-all-done.3 = bf16[4,2,2,128,128]{4,3,2,1,0:T(8,128)(2,1)} async-done(((bf16[4,2,2,128,128]{4,3,2,1,0:T(8,128)(2,1)}), bf16[4,2,2,128,128]{4,3,2,1,0:T(8,128)(2,1)}, u32[]{:S(2)}, u32[]{:S(2)}) %all-to-all-start.3) | async-done | bytes 524320 | tf_op jit(solution)/shard_map/out_far/all_to_all | solution.py:399
  184.1 1.1 convert_reduce_fusion.1
  185.3 3.2 %collective-permute-done.23.refs_4_ = bf16[2,512,128]{2,1,0:T(8,128)(2,1)} collective-permute-done((bf16[2,512,128]{2,1,0:T(8,128)(2,1)}, bf16[2,512,128]{2,1,0:T(8,128)(2,1)}, u32[]{:S(2)}, u32[]{:S(2)}) %collective-permute-start.23) | collective-permute-done | bytes 262176 | tf_op jit(solution)/shard_map/out_pairs0_2/ppermute | solution.py:322
  188.5 3.7 %collective-permute-done.24.refs_6_ = bf16[2,512,128]{2,1,0:T(8,128)(2,1)} collective-permute-done((bf16[2,512,128]{2,1,0:T(8,128)(2,1)}, bf16[2,512,128]{2,1,0:T(8,128)(2,1)}, u32[]{:S(2)}, u32[]{:S(2)}) %collective-permute-start.24) | collective-permute-done | bytes 262176 | tf_op jit(solution)/shard_map/out_pairs0_3/ppermute | solution.py:322
  192.2 11.7 %collective-permute-done.21 = bf16[2,2048,128]{2,1,0:T(8,128)(2,1)} collective-permute-done((bf16[2,2048,128]{2,1,0:T(8,128)(2,1)}, bf16[2,2048,128]{2,1,0:T(8,128)(2,1)}, u32[]{:S(2)}, u32[]{:S(2)}) %collective-permute-start.21) | collective-permute-done | bytes 1048608 | tf_op jit(solution)/shard_map/out_onward1/ppermute | solution.py:318
  203.9 1.6 fusion.5
  206.0 0.8 fusion.9
  206.8 0.8 dynamic-slice_bitcast_fusion
  207.6 0.5 collective-permute-start.26
  208.1 1.3 collective-permute-start.27
  209.4 7.2 %collective-permute-done.26.refs_5_ = bf16[2,512,128]{2,1,0:T(8,128)(2,1)S(1)} collective-permute-done((bf16[2,512,128]{2,1,0:T(8,128)(2,1)S(1)}, bf16[2,512,128]{2,1,0:T(8,128)(2,1)S(1)}, u32[]{:S(2)}, u32[]{:S(2)}) %collective-permute-start.26) | collective-permute-done | bytes 262176 | tf_op jit(solution)/shard_map/out_pairs1_2/ppermute | solution.py:322
  216.7 4.8 %collective-permute-done.27.refs_7_ = bf16[2,512,128]{2,1,0:T(8,128)(2,1)S(1)} collective-permute-done((bf16[2,512,128]{2,1,0:T(8,128)(2,1)S(1)}, bf16[2,512,128]{2,1,0:T(8,128)(2,1)S(1)}, u32[]{:S(2)}, u32[]{:S(2)}) %collective-permute-start.27) | collective-permute-done | bytes 262176 | tf_op jit(solution)/shard_map/out_pairs1_3/ppermute | solution.py:322
  221.5 0.7 copy-done.14
  222.2 3.6 %assemble_pairs.1 = (bf16[512,1024]{1,0:T(8,128)(2,1)}, bf16[512,1024]{1,0:T(8,128)(2,1)}) custom-call(s32[2]{0:T(128)} %copy-done.2, bf16[2,512,128]{2,1,0:T(8,128)(2,1)} %get-tuple-element.80.refs_0_, bf16[2,512,128]{2,1,0:T(8,128)(2,1)} %get-tuple-element.76.refs_1_, bf16[2,512,128]{2,1,0:T(8,128)(2,1)} %copy-done.11, bf16[2,512,128]{2,1,0:T(8,128)(2,1)} %copy-done.12, ...), custom_call_target="tpu_custom_call" | custom-call | tf_op jit(solution)/shard_map/assemble_pairs/pallas_call | solution.py:288
  (78 shorter events, 2.5 us)
Async XLA Ops:
  2.3 7.0 %copy-start.6 = (s32[8]{0:T(128)S(1)}, s32[8]{0:T(128)}, u32[]{:S(2)}) copy-start(s32[8]{0:T(128)} %vertical.3) | copy-start | bytes 100
  3.4 28.8 %collective-permute-start = (bf16[2,2048,128]{2,1,0:T(8,128)(2,1)}, bf16[2,2048,128]{2,1,0:T(8,128)(2,1)}, u32[]{:S(2)}, u32[]{:S(2)}) collective-permute-start(bf16[2,2048,128]{2,1,0:T(8,128)(2,1)} %pad_maximum_fusion.refs_2_), channel_id=1, source_target_pairs={{0,8},{4,12},{8,16},{12,20},{16,24},{20,28},{1,9},{5,13},{9,17},{1... | collective-permute-start | bytes 3145736 | tf_op jit(solution)/shard_map/in_back0/ppermute | solution.py:318
  10.7 38.5 %collective-permute-start.4 = (bf16[2,2,128,128]{3,2,1,0:T(8,128)(2,1)S(1)}, bf16[2,2,128,128]{3,2,1,0:T(8,128)(2,1)S(1)}, u32[]{:S(2)}, u32[]{:S(2)}) collective-permute-start(bf16[2,2,128,128]{3,2,1,0:T(8,128)(2,1)S(1)} %pad_maximum_fusion.3), channel_id=1, source_target_pairs={{0,24},{1,25},{2,26},{3,27}} | collective-permute-start | bytes 393224 | tf_op jit(solution)/shard_map/in_first6/ppermute | solution.py:318
  13.0 36.2 %collective-permute-start.3 = (bf16[2,2,128,128]{3,2,1,0:T(8,128)(2,1)S(1)}, bf16[2,2,128,128]{3,2,1,0:T(8,128)(2,1)S(1)}, u32[]{:S(2)}, u32[]{:S(2)}) collective-permute-start(bf16[2,2,128,128]{3,2,1,0:T(8,128)(2,1)S(1)} %pad_maximum_fusion.3), channel_id=1, source_target_pairs={{0,16},{1,17},{2,18},{3,19}} | collective-permute-start | bytes 393224 | tf_op jit(solution)/shard_map/in_first4/ppermute | solution.py:318
  14.8 34.4 %collective-permute-start.2 = (bf16[2,2,128,128]{3,2,1,0:T(8,128)(2,1)S(1)}, bf16[2,2,128,128]{3,2,1,0:T(8,128)(2,1)S(1)}, u32[]{:S(2)}, u32[]{:S(2)}) collective-permute-start(bf16[2,2,128,128]{3,2,1,0:T(8,128)(2,1)S(1)} %pad_maximum_fusion.3), channel_id=1, source_target_pairs={{0,8},{1,9},{2,10},{3,11}} | collective-permute-start | bytes 393224 | tf_op jit(solution)/shard_map/in_first2/ppermute | solution.py:318
  16.1 45.1 %collective-permute-start.6 = (bf16[2,2048,128]{2,1,0:T(8,128)(2,1)}, bf16[2,2048,128]{2,1,0:T(8,128)(2,1)}, u32[]{:S(2)}, u32[]{:S(2)}) collective-permute-start(bf16[2,2048,128]{2,1,0:T(8,128)(2,1)} %pad_maximum_fusion.refs_2_), channel_id=1, source_target_pairs={{0,4},{8,12},{16,20},{24,28},{1,5},{9,13},{17,21},{25,29},{2,6},{1... | collective-permute-start | bytes 3145736 | tf_op jit(solution)/shard_map/in_even0/ppermute | solution.py:318
  19.2 32.0 %copy-start.15 = (s32[16,2]{0,1:T(2,128)S(1)}, s32[16,2]{0,1:T(2,128)}, u32[]{:S(2)}) copy-start(s32[16,2]{0,1:T(2,128)} %param.12) | copy-start | bytes 388
  19.2 32.1 %copy-start.16 = (s32[16,2]{0,1:T(2,128)S(1)}, s32[16,2]{0,1:T(2,128)}, u32[]{:S(2)}) copy-start(s32[16,2]{0,1:T(2,128)} %param.13) | copy-start | bytes 388
  19.2 24.5 %all-to-all-start = ((bf16[4,2,128,128]{3,2,1,0:T(8,128)(2,1)}), bf16[4,2,128,128]{3,2,1,0:T(8,128)(2,1)S(1)}, u32[]{:S(2)}, u32[]{:S(2)}) async-start(bf16[4,2,128,128]{3,2,1,0:T(8,128)(2,1)} %broadcast_in_dim.92), calls=%async_computation | async-start | bytes 524288 | tf_op jit(solution)/shard_map/in_column0/all_to_all | solution.py:340
  32.2 32.9 %collective-permute-start.7 = (bf16[2,2048,128]{2,1,0:T(8,128)(2,1)}, bf16[2,2048,128]{2,1,0:T(8,128)(2,1)}, u32[]{:S(2)}, u32[]{:S(2)}) collective-permute-start(bf16[2,2048,128]{2,1,0:T(8,128)(2,1)} %collective-permute-done.refs_7_), channel_id=1, source_target_pairs={{4,0},{12,8},{20,16},{28,24},{5,1},{13,9},{21,17},{29,25},{6,2},{1... | collective-permute-start | bytes 3145736 | tf_op jit(solution)/shard_map/in_odd0/ppermute | solution.py:318
  33.6 61.3 %copy-start.9 = (bf16[2,2048,128]{2,1,0:T(8,128)(2,1)}, bf16[2,2048,128]{2,1,0:T(8,128)(2,1)S(1)}, u32[]{:S(2)}) copy-start(bf16[2,2048,128]{2,1,0:T(8,128)(2,1)S(1)} %pad_maximum_fusion.1.refs_2_) | copy-start | bytes 3145732
  44.4 16.8 %all-to-all-start.1 = ((bf16[4,2,128,128]{3,2,1,0:T(8,128)(2,1)}), bf16[4,2,128,128]{3,2,1,0:T(8,128)(2,1)S(1)}, u32[]{:S(2)}, u32[]{:S(2)}) async-start(bf16[4,2,128,128]{3,2,1,0:T(8,128)(2,1)} %broadcast_in_dim.94), calls=%async_computation.1 | async-start | bytes 524288 | tf_op jit(solution)/shard_map/in_column1/all_to_all | solution.py:340
  49.2 7.1 %collective-permute-start.5 = (bf16[2,2,128,128]{3,2,1,0:T(8,128)(2,1)S(1)}, bf16[2,2,128,128]{3,2,1,0:T(8,128)(2,1)S(1)}, u32[]{:S(2)}, u32[]{:S(2)}) collective-permute-start(bf16[2,2,128,128]{3,2,1,0:T(8,128)(2,1)S(1)} %add_add_fusion.refs_5_), channel_id=1, source_target_pairs={{0,4},{8,12},{16,20},{24,28},{1,5},{9,13},{17,21},{25,29},{2,6},{1... | collective-permute-start | bytes 393224 | tf_op jit(solution)/shard_map/in_first_pair/ppermute | solution.py:318
  51.1 14.0 %collective-permute-start.1 = (bf16[4,2,128,128]{3,2,1,0:T(8,128)(2,1)S(1)}, bf16[4,2,128,128]{3,2,1,0:T(8,128)(2,1)S(1)}, u32[]{:S(2)}, u32[]{:S(2)}) collective-permute-start(bf16[4,2,128,128]{3,2,1,0:T(8,128)(2,1)S(1)} %all-to-all-done.refs_3_), channel_id=1, source_target_pairs={{0,4},{4,0},{8,12},{12,8},{16,20},{20,16},{24,28},{28,24},{1,5},{5... | collective-permute-start | bytes 786440 | tf_op jit(solution)/shard_map/in_column_pair0/ppermute | solution.py:318
  51.5 54.9 %copy-start.2 = (s32[2]{0:T(128)}, s32[2]{0:T(128)S(1)}, u32[]{:S(2)}) copy-start(s32[2]{0:T(128)S(1)} %pad_add_fusion.place) | copy-start | bytes 28
  51.5 53.0 %collective-permute-start.9 = (bf16[2,2048,128]{2,1,0:T(8,128)(2,1)S(1)}, bf16[2,2048,128]{2,1,0:T(8,128)(2,1)}, u32[]{:S(2)}, u32[]{:S(2)}) collective-permute-start(bf16[2,2048,128]{2,1,0:T(8,128)(2,1)S(1)} %pad_maximum_fusion.1.refs_2_), channel_id=1, source_target_pairs={{0,8},{4,12},{8,16},{12,20},{16,24},{20,28},{1,9},{5,13},{9,17},{1... | collective-permute-start | bytes 3145736 | tf_op jit(solution)/shard_map/in_back1/ppermute | solution.py:318
  56.4 50.0 %collective-permute-start.10 = (bf16[2,2048,128]{2,1,0:T(8,128)(2,1)S(1)}, bf16[2,2048,128]{2,1,0:T(8,128)(2,1)}, u32[]{:S(2)}, u32[]{:S(2)}) collective-permute-start(bf16[2,2048,128]{2,1,0:T(8,128)(2,1)S(1)} %pad_maximum_fusion.1.refs_2_), channel_id=1, source_target_pairs={{0,4},{4,8},{8,12},{12,16},{16,20},{20,24},{24,28},{1,5},{5,9},{9,... | collective-permute-start | bytes 3145736 | tf_op jit(solution)/shard_map/in_prev1/ppermute | solution.py:318
  61.3 42.4 %collective-permute-start.8 = (bf16[4,2,128,128]{3,2,1,0:T(8,128)(2,1)S(1)}, bf16[4,2,128,128]{3,2,1,0:T(8,128)(2,1)S(1)}, u32[]{:S(2)}, u32[]{:S(2)}) collective-permute-start(bf16[4,2,128,128]{3,2,1,0:T(8,128)(2,1)S(1)} %all-to-all-done.1.refs_3_), channel_id=1, source_target_pairs={{0,4},{4,0},{8,12},{12,8},{16,20},{20,16},{24,28},{28,24},{1,5},{5... | collective-permute-start | bytes 786440 | tf_op jit(solution)/shard_map/in_column_pair1/ppermute | solution.py:318
  94.8 0.8 copy-start
  95.6 44.6 %collective-permute-start.11 = (bf16[512,512]{1,0:T(8,128)(2,1)}, bf16[512,512]{1,0:T(8,128)(2,1)}, u32[]{:S(2)}, u32[]{:S(2)}) collective-permute-start(bf16[512,512]{1,0:T(8,128)(2,1)} %get-tuple-element.48), channel_id=1, source_target_pairs={{0,1},{1,0},{2,3},{3,2},{4,5},{5,4},{6,7},{7,6},{8,9},{9,8},{10,11... | collective-permute-start | bytes 1572872 | tf_op jit(solution)/shard_map/out_query0_1/ppermute | solution.py:322
  95.6 44.6 %collective-permute-start.12 = (bf16[512,512]{1,0:T(8,128)(2,1)}, bf16[512,512]{1,0:T(8,128)(2,1)}, u32[]{:S(2)}, u32[]{:S(2)}) collective-permute-start(bf16[512,512]{1,0:T(8,128)(2,1)} %get-tuple-element.49), channel_id=1, source_target_pairs={{0,2},{1,3},{2,0},{3,1},{4,6},{5,7},{6,4},{7,5},{8,10},{9,11},{10,... | collective-permute-start | bytes 1572872 | tf_op jit(solution)/shard_map/out_query0_2/ppermute | solution.py:322
  97.1 43.1 %all-to-all-start.2 = ((bf16[8,2,2,128,128]{4,3,2,1,0:T(8,128)(2,1)}), bf16[8,2,2,128,128]{4,3,2,1,0:T(8,128)(2,1)}, u32[]{:S(2)}, u32[]{:S(2)}) async-start(bf16[8,2,2,128,128]{4,3,2,1,0:T(8,128)(2,1)} %get-tuple-element.51), calls=%async_computation.2 | async-start | bytes 2097152 | tf_op jit(solution)/shard_map/out_far0/all_to_all | solution.py:376
  103.7 0.7 copy-start.4
  104.4 35.9 %collective-permute-start.13 = (bf16[512,512]{1,0:T(8,128)(2,1)}, bf16[512,512]{1,0:T(8,128)(2,1)}, u32[]{:S(2)}, u32[]{:S(2)}) collective-permute-start(bf16[512,512]{1,0:T(8,128)(2,1)} %get-tuple-element.50), channel_id=1, source_target_pairs={{0,3},{1,2},{2,1},{3,0},{4,7},{5,6},{6,5},{7,4},{8,11},{9,10},{10,... | collective-permute-start | bytes 1572872 | tf_op jit(solution)/shard_map/out_query0_3/ppermute | solution.py:322
  104.5 35.8 %collective-permute-start.14 = (bf16[2,2048,128]{2,1,0:T(8,128)(2,1)S(1)}, bf16[2,2048,128]{2,1,0:T(8,128)(2,1)}, u32[]{:S(2)}, u32[]{:S(2)}) collective-permute-start(bf16[2,2048,128]{2,1,0:T(8,128)(2,1)S(1)} %get-tuple-element.53), channel_id=1, source_target_pairs={{0,4},{4,0},{8,12},{12,8},{16,20},{20,16},{24,28},{28,24},{1,5},{5... | collective-permute-start | bytes 3145736 | tf_op jit(solution)/shard_map/out_pair0/ppermute | solution.py:318
  106.4 1.0 copy-start.5
  136.6 0.8 copy-start.1
  137.4 0.7 copy-start.3
  140.2 9.0 %collective-permute-start.15 = (bf16[5,2,128,128]{3,2,1,0:T(8,128)(2,1)}, bf16[5,2,128,128]{3,2,1,0:T(8,128)(2,1)S(1)}, u32[]{:S(2)}, u32[]{:S(2)}) collective-permute-start(bf16[5,2,128,128]{3,2,1,0:T(8,128)(2,1)} %copy-done.3), channel_id=1, source_target_pairs={{0,4},{4,0},{8,12},{12,8},{16,20},{20,16},{24,28},{28,24},{1,5},{5... | collective-permute-start | bytes 983048 | tf_op jit(solution)/shard_map/out_far_pair1/ppermute | solution.py:318
  140.6 16.8 %collective-permute-start.17 = (bf16[512,512]{1,0:T(8,128)(2,1)S(1)}, bf16[512,512]{1,0:T(8,128)(2,1)}, u32[]{:S(2)}, u32[]{:S(2)}) collective-permute-start(bf16[512,512]{1,0:T(8,128)(2,1)S(1)} %get-tuple-element.64), channel_id=1, source_target_pairs={{0,2},{1,3},{2,0},{3,1},{4,6},{5,7},{6,4},{7,5},{8,10},{9,11},{10,... | collective-permute-start | bytes 1572872 | tf_op jit(solution)/shard_map/out_query1_2/ppermute | solution.py:322
  141.1 21.9 %collective-permute-start.18 = (bf16[512,512]{1,0:T(8,128)(2,1)S(1)}, bf16[512,512]{1,0:T(8,128)(2,1)}, u32[]{:S(2)}, u32[]{:S(2)}) collective-permute-start(bf16[512,512]{1,0:T(8,128)(2,1)S(1)} %get-tuple-element.65), channel_id=1, source_target_pairs={{0,3},{1,2},{2,1},{3,0},{4,7},{5,6},{6,5},{7,4},{8,11},{9,10},{10,... | collective-permute-start | bytes 1572872 | tf_op jit(solution)/shard_map/out_query1_3/ppermute | solution.py:322
  144.0 29.9 %collective-permute-start.19 = (bf16[2,2048,128]{2,1,0:T(8,128)(2,1)}, bf16[2,2048,128]{2,1,0:T(8,128)(2,1)}, u32[]{:S(2)}, u32[]{:S(2)}) collective-permute-start(bf16[2,2048,128]{2,1,0:T(8,128)(2,1)} %fusion.3), channel_id=1, source_target_pairs={{8,0},{12,4},{16,8},{20,12},{24,16},{28,20},{9,1},{13,5},{17,9},{2... | collective-permute-start | bytes 3145736 | tf_op jit(solution)/shard_map/out_onward0/ppermute | solution.py:318
  145.3 25.8 %collective-permute-start.20 = (bf16[2,2048,128]{2,1,0:T(8,128)(2,1)}, bf16[2,2048,128]{2,1,0:T(8,128)(2,1)S(1)}, u32[]{:S(2)}, u32[]{:S(2)}) collective-permute-start(bf16[2,2048,128]{2,1,0:T(8,128)(2,1)} %get-tuple-element.67), channel_id=1, source_target_pairs={{0,4},{4,0},{8,12},{12,8},{16,20},{20,16},{24,28},{28,24},{1,5},{5... | collective-permute-start | bytes 3145736 | tf_op jit(solution)/shard_map/out_pair1/ppermute | solution.py:318
  149.5 13.5 %collective-permute-start.16 = (bf16[512,512]{1,0:T(8,128)(2,1)S(1)}, bf16[512,512]{1,0:T(8,128)(2,1)}, u32[]{:S(2)}, u32[]{:S(2)}) collective-permute-start(bf16[512,512]{1,0:T(8,128)(2,1)S(1)} %get-tuple-element.63), channel_id=1, source_target_pairs={{0,1},{1,0},{2,3},{3,2},{4,5},{5,4},{6,7},{7,6},{8,9},{9,8},{10,11... | collective-permute-start | bytes 1572872 | tf_op jit(solution)/shard_map/out_query1_1/ppermute | solution.py:322
  151.9 32.2 %all-to-all-start.3 = ((bf16[4,2,2,128,128]{4,3,2,1,0:T(8,128)(2,1)}), bf16[4,2,2,128,128]{4,3,2,1,0:T(8,128)(2,1)}, u32[]{:S(2)}, u32[]{:S(2)}) async-start(bf16[4,2,2,128,128]{4,3,2,1,0:T(8,128)(2,1)} %copy.24), calls=%async_computation.3 | async-start | bytes 1048576 | tf_op jit(solution)/shard_map/out_far/all_to_all | solution.py:399
  163.0 8.1 %copy-start.10 = (bf16[2,2048,128]{2,1,0:T(8,128)(2,1)S(1)}, bf16[2,2048,128]{2,1,0:T(8,128)(2,1)}, u32[]{:S(2)}) copy-start(bf16[2,2048,128]{2,1,0:T(8,128)(2,1)} %get-tuple-element.69) | copy-start | bytes 3145732
  168.5 5.4 %copy-start.8 = (f32[2,2048,128]{2,1,0:T(8,128)S(1)}, f32[2,2048,128]{2,1,0:T(8,128)}, u32[]{:S(2)}) copy-start(f32[2,2048,128]{2,1,0:T(8,128)} %get-tuple-element.56) | copy-start | bytes 6291460
  172.4 31.5 %collective-permute-start.21 = (bf16[2,2048,128]{2,1,0:T(8,128)(2,1)}, bf16[2,2048,128]{2,1,0:T(8,128)(2,1)}, u32[]{:S(2)}, u32[]{:S(2)}) collective-permute-start(bf16[2,2048,128]{2,1,0:T(8,128)(2,1)} %fusion.7), channel_id=1, source_target_pairs={{8,0},{12,4},{16,8},{20,12},{24,16},{28,20},{9,1},{13,5},{17,9},{2... | collective-permute-start | bytes 3145736 | tf_op jit(solution)/shard_map/out_onward1/ppermute | solution.py:318
  177.2 26.7 %copy-start.7 = (f32[2,2048,128]{2,1,0:T(8,128)S(1)}, f32[2,2048,128]{2,1,0:T(8,128)}, u32[]{:S(2)}) copy-start(f32[2,2048,128]{2,1,0:T(8,128)} %get-tuple-element.66) | copy-start | bytes 6291460
  178.2 7.1 %collective-permute-start.22 = (bf16[2,512,128]{2,1,0:T(8,128)(2,1)}, bf16[2,512,128]{2,1,0:T(8,128)(2,1)S(1)}, u32[]{:S(2)}, u32[]{:S(2)}) collective-permute-start(bf16[2,512,128]{2,1,0:T(8,128)(2,1)} %get-tuple-element.79), channel_id=1, source_target_pairs={{0,1},{1,0},{2,3},{3,2},{4,5},{5,4},{6,7},{7,6},{8,9},{9,8},{10,11... | collective-permute-start | bytes 786440 | tf_op jit(solution)/shard_map/out_pairs0_1/ppermute | solution.py:322
  179.0 9.5 %collective-permute-start.23 = (bf16[2,512,128]{2,1,0:T(8,128)(2,1)}, bf16[2,512,128]{2,1,0:T(8,128)(2,1)}, u32[]{:S(2)}, u32[]{:S(2)}) collective-permute-start(bf16[2,512,128]{2,1,0:T(8,128)(2,1)} %get-tuple-element.78), channel_id=1, source_target_pairs={{0,2},{1,3},{2,0},{3,1},{4,6},{5,7},{6,4},{7,5},{8,10},{9,11},{10,... | collective-permute-start | bytes 786440 | tf_op jit(solution)/shard_map/out_pairs0_2/ppermute | solution.py:322
  179.8 12.3 %collective-permute-start.24 = (bf16[2,512,128]{2,1,0:T(8,128)(2,1)}, bf16[2,512,128]{2,1,0:T(8,128)(2,1)}, u32[]{:S(2)}, u32[]{:S(2)}) collective-permute-start(bf16[2,512,128]{2,1,0:T(8,128)(2,1)} %get-tuple-element.77), channel_id=1, source_target_pairs={{0,3},{1,2},{2,1},{3,0},{4,7},{5,6},{6,5},{7,4},{8,11},{9,10},{10,... | collective-permute-start | bytes 786440 | tf_op jit(solution)/shard_map/out_pairs0_3/ppermute | solution.py:322
  185.3 20.2 %copy-start.11 = (bf16[2,512,128]{2,1,0:T(8,128)(2,1)}, bf16[2,512,128]{2,1,0:T(8,128)(2,1)S(1)}, u32[]{:S(2)}) copy-start(bf16[2,512,128]{2,1,0:T(8,128)(2,1)S(1)} %collective-permute-done.22.refs_2_) | copy-start | bytes 786436
  207.6 1.9 collective-permute-start.25
  207.6 9.1 %collective-permute-start.26 = (bf16[2,512,128]{2,1,0:T(8,128)(2,1)S(1)}, bf16[2,512,128]{2,1,0:T(8,128)(2,1)S(1)}, u32[]{:S(2)}, u32[]{:S(2)}) collective-permute-start(bf16[2,512,128]{2,1,0:T(8,128)(2,1)S(1)} %get-tuple-element.74), channel_id=1, source_target_pairs={{0,2},{1,3},{2,0},{3,1},{4,6},{5,7},{6,4},{7,5},{8,10},{9,11},{10,... | collective-permute-start | bytes 786440 | tf_op jit(solution)/shard_map/out_pairs1_2/ppermute | solution.py:322
  208.1 13.4 %collective-permute-start.27 = (bf16[2,512,128]{2,1,0:T(8,128)(2,1)S(1)}, bf16[2,512,128]{2,1,0:T(8,128)(2,1)S(1)}, u32[]{:S(2)}, u32[]{:S(2)}) collective-permute-start(bf16[2,512,128]{2,1,0:T(8,128)(2,1)S(1)} %get-tuple-element.73), channel_id=1, source_target_pairs={{0,3},{1,2},{2,1},{3,0},{4,7},{5,6},{6,5},{7,4},{8,11},{9,10},{10,... | collective-permute-start | bytes 786440 | tf_op jit(solution)/shard_map/out_pairs1_3/ppermute | solution.py:322
  209.4 12.1 %copy-start.12 = (bf16[2,512,128]{2,1,0:T(8,128)(2,1)}, bf16[2,512,128]{2,1,0:T(8,128)(2,1)S(1)}, u32[]{:S(2)}) copy-start(bf16[2,512,128]{2,1,0:T(8,128)(2,1)S(1)} %collective-permute-done.25.refs_3_) | copy-start | bytes 786436
  216.7 4.8 %copy-start.13 = (bf16[2,512,128]{2,1,0:T(8,128)(2,1)}, bf16[2,512,128]{2,1,0:T(8,128)(2,1)S(1)}, u32[]{:S(2)}) copy-start(bf16[2,512,128]{2,1,0:T(8,128)(2,1)S(1)} %collective-permute-done.26.refs_5_) | copy-start | bytes 786436
  221.5 0.7 copy-start.14

commit v5 on v4

--- a/solution.py
+++ b/solution.py
@@ -132,9 +132,9 @@
         inverse = 1.0 / total
         delta = delta * inverse
         for number in range(6):
-            prob = weights[number] * inverse
-            dscores.append((prob * (product[number * BLK : (number + 1) * BLK] - delta)).astype(jnp.bfloat16))
-            probs.append(prob.astype(jnp.bfloat16))
+            prob = (weights[number] * inverse).astype(jnp.bfloat16)
+            dscores.append(prob * (product[number * BLK : (number + 1) * BLK] - delta).astype(jnp.bfloat16))
+            probs.append(prob)
         return jnp.concatenate(probs, axis=0), jnp.concatenate(dscores, axis=0)
 
     def finish(sub, spots, queries, grads, keys, prob, dscore):
@@ -167,7 +167,7 @@
         for side, (acc, factor) in enumerate(((acc_k, scale), (acc_v, 1.0))):
             prev_ref[side] = (acc[rows : 2 * rows, :] * factor).astype(jnp.bfloat16)
             back_ref[side] = (acc[2 * rows : 3 * rows, :] * factor).astype(jnp.bfloat16)
-            own_ref[side] = acc[:rows, :] * factor
+            own_ref[side] = (acc[:rows, :] * factor).astype(jnp.bfloat16)
 
             def far_block(number):
                 start = pl.multiple_of((3 * local_blocks + number) * BLK, BLK)
@@ -231,8 +231,7 @@
             ],
         ),
         out_shape=[jax.ShapeDtypeStruct((seq_len // heads, width), jnp.bfloat16)] * heads
-        + [jax.ShapeDtypeStruct(near_shape, jnp.float32)]
-        + [jax.ShapeDtypeStruct(near_shape, jnp.bfloat16)] * 2
+        + [jax.ShapeDtypeStruct(near_shape, jnp.bfloat16)] * 3
         + [jax.ShapeDtypeStruct(shape, jnp.bfloat16) for shape in far_shapes],
         compiler_params=pltpu.CompilerParams(vmem_limit_bytes=50 * 1024 * 1024),
         cost_estimate=pl.CostEstimate(

time: 228 us -> 225 us (0.987)
  waiting for transfers between devices: 69.4 us -> 65.7 us
  Pallas kernels: 68.1 us -> 65.3 us
  starting transfers between devices: 60.1 us -> 62.9 us
    ppermute x16, waiting for transfers between devices: 31.7 us -> 28.3 us  [along(): return lax.ppermute(array, 'seq', pairs)]
    pallas_call x2, Pallas kernels: 59 us -> 56.2 us  [attention(): pl.pallas_call(functools.partial(attention_kernel, (local_blocks, group,...]
    unnamed x38 -> x42, local copies, waits for them, and re-layouts: 5.03 us -> 5.07 us
  transfers between devices with their start and end apart: 32 -> 32, of which waited for: 13 -> 13; matrix products, arithmetic and copies ran while one was open for 7% -> 8% of each run, Pallas kernels for 29% -> 28%
where the time goes in v5:
time: 225 us; the launch traced here: 224 us
  waiting for transfers between devices  65.7 us (29%)
  Pallas kernels  65.3 us (29%)
  starting transfers between devices  62.9 us (28%)
  other arithmetic  14.9 us (7%)
  local copies, waits for them, and re-layouts  13.1 us (6%)
    pallas_call x2, Pallas kernels, attention(): pl.pallas_call(functools.partial(attention_kernel, (local_blocks, group,...  56.2 us
    ppermute x16, starting transfers between devices, along(): return lax.ppermute(array, 'seq', pairs)  35.4 us
    ppermute x16, waiting for transfers between devices, along(): return lax.ppermute(array, 'seq', pairs)  28.3 us
    ppermute x12, waiting for transfers between devices, across(): lax.ppermute(array, 'head', [(i, i ^ k) for i in range(heads)])  26.4 us
    all_to_all x2, waiting for transfers between devices, column_of(): lax.all_to_all(wide, 'seq', split_axis=0, concat_axis=0, axis_index_group...  8.54 us
    all_to_all x2, starting transfers between devices, column_of(): lax.all_to_all(wide, 'seq', split_axis=0, concat_axis=0, axis_index_group...  8.28 us
    all_to_all x1, starting transfers between devices, shards(): fars.append(lax.all_to_all(table[0], 'seq', split_axis=0, concat_axis=0))  7.72 us
    ppermute x12, starting transfers between devices, across(): lax.ppermute(array, 'head', [(i, i ^ k) for i in range(heads)])  5.99 us
  transfers between devices with their start and end apart: 32, of which 13 were waited for; matrix products, arithmetic and copies ran while one was open for 8% of the time, Pallas kernels for 28%

profile of v5, /device:TPU:0, one launch (start us, length us, event | category | flops | bytes accessed | tf_op | source)
XLA Modules:
  0.0 223.6 jit_solution(10983982433961194810)
XLA Ops:
  0.6 1.7 slice_bitcast_fusion
  2.4 5.9 %collective-permute-start = (bf16[2,2048,128]{2,1,0:T(8,128)(2,1)S(1)}, bf16[2,2048,128]{2,1,0:T(8,128)(2,1)}, u32[]{:S(2)}, u32[]{:S(2)}) collective-permute-start(bf16[2,2048,128]{2,1,0:T(8,128)(2,1)S(1)} %pad_maximum_fusion.refs_2_), channel_id=1, source_target_pairs={{0,8},{4,12},{8,16},{12,20},{16,24},{20,28},{1,9},{5,13},{9,17},{1... | collective-permute-start | bytes 3145736 | tf_op jit(solution)/shard_map/in_back0/ppermute | solution.py:317
  8.4 0.6 dynamic_slice.34
  9.7 2.3 %collective-permute-start.4 = (bf16[2,2,128,128]{3,2,1,0:T(8,128)(2,1)S(1)}, bf16[2,2,128,128]{3,2,1,0:T(8,128)(2,1)S(1)}, u32[]{:S(2)}, u32[]{:S(2)}) collective-permute-start(bf16[2,2,128,128]{3,2,1,0:T(8,128)(2,1)S(1)} %pad_maximum_fusion.3), channel_id=1, source_target_pairs={{0,24},{1,25},{2,26},{3,27}} | collective-permute-start | bytes 393224 | tf_op jit(solution)/shard_map/in_first6/ppermute | solution.py:317
  12.0 1.9 collective-permute-start.3
  13.9 2.0 collective-permute-start.2
  15.9 2.3 %collective-permute-start.6 = (bf16[2,2048,128]{2,1,0:T(8,128)(2,1)S(1)}, bf16[2,2048,128]{2,1,0:T(8,128)(2,1)}, u32[]{:S(2)}, u32[]{:S(2)}) collective-permute-start(bf16[2,2048,128]{2,1,0:T(8,128)(2,1)S(1)} %pad_maximum_fusion.refs_2_), channel_id=1, source_target_pairs={{0,4},{8,12},{16,20},{24,28},{1,5},{9,13},{17,21},{25,29},{2,6},{1... | collective-permute-start | bytes 3145736 | tf_op jit(solution)/shard_map/in_even0/ppermute | solution.py:317
  18.1 0.7 broadcast_in_dim.92
  18.9 3.5 %all-to-all-start = ((bf16[4,2,128,128]{3,2,1,0:T(8,128)(2,1)}), bf16[4,2,128,128]{3,2,1,0:T(8,128)(2,1)S(1)}, u32[]{:S(2)}, u32[]{:S(2)}) async-start(bf16[4,2,128,128]{3,2,1,0:T(8,128)(2,1)} %broadcast_in_dim.92), calls=%async_computation | async-start | bytes 524288 | tf_op jit(solution)/shard_map/in_column0/all_to_all | solution.py:339
  22.4 8.5 %collective-permute-done.refs_7_ = bf16[2,2048,128]{2,1,0:T(8,128)(2,1)} collective-permute-done((bf16[2,2048,128]{2,1,0:T(8,128)(2,1)S(1)}, bf16[2,2048,128]{2,1,0:T(8,128)(2,1)}, u32[]{:S(2)}, u32[]{:S(2)}) %collective-permute-start) | collective-permute-done | bytes 1048608 | tf_op jit(solution)/shard_map/in_back0/ppermute | solution.py:317
  30.9 1.3 collective-permute-start.7
  32.2 1.1 pad_maximum_fusion.1.refs_2_
  33.4 0.7 fusion.21
  34.0 8.5 %all-to-all-done.refs_3_ = bf16[4,2,128,128]{3,2,1,0:T(8,128)(2,1)S(1)} async-done(((bf16[4,2,128,128]{3,2,1,0:T(8,128)(2,1)}), bf16[4,2,128,128]{3,2,1,0:T(8,128)(2,1)S(1)}, u32[]{:S(2)}, u32[]{:S(2)}) %all-to-all-start) | async-done | bytes 262176 | tf_op jit(solution)/shard_map/in_column0/all_to_all | solution.py:339
  42.6 0.7 broadcast_in_dim.94
  43.3 4.7 %all-to-all-start.1 = ((bf16[4,2,128,128]{3,2,1,0:T(8,128)(2,1)}), bf16[4,2,128,128]{3,2,1,0:T(8,128)(2,1)S(1)}, u32[]{:S(2)}, u32[]{:S(2)}) async-start(bf16[4,2,128,128]{3,2,1,0:T(8,128)(2,1)} %broadcast_in_dim.94), calls=%async_computation.1 | async-start | bytes 524288 | tf_op jit(solution)/shard_map/in_column1/all_to_all | solution.py:339
  48.1 0.9 add_add_fusion.refs_5_
  49.0 2.7 %collective-permute-start.5 = (bf16[2,2,128,128]{3,2,1,0:T(8,128)(2,1)S(1)}, bf16[2,2,128,128]{3,2,1,0:T(8,128)(2,1)S(1)}, u32[]{:S(2)}, u32[]{:S(2)}) collective-permute-start(bf16[2,2,128,128]{3,2,1,0:T(8,128)(2,1)S(1)} %add_add_fusion.refs_5_), channel_id=1, source_target_pairs={{0,4},{8,12},{16,20},{24,28},{1,5},{9,13},{17,21},{25,29},{2,6},{1... | collective-permute-start | bytes 393224 | tf_op jit(solution)/shard_map/in_first_pair/ppermute | solution.py:317
  52.2 4.9 %collective-permute-start.9 = (bf16[2,2048,128]{2,1,0:T(8,128)(2,1)}, bf16[2,2048,128]{2,1,0:T(8,128)(2,1)}, u32[]{:S(2)}, u32[]{:S(2)}) collective-permute-start(bf16[2,2048,128]{2,1,0:T(8,128)(2,1)} %pad_maximum_fusion.1.refs_2_), channel_id=1, source_target_pairs={{0,8},{4,12},{8,16},{12,20},{16,24},{20,28},{1,9},{5,13},{9,17},{1... | collective-permute-start | bytes 3145736 | tf_op jit(solution)/shard_map/in_back1/ppermute | solution.py:317
  57.1 5.0 %collective-permute-start.10 = (bf16[2,2048,128]{2,1,0:T(8,128)(2,1)}, bf16[2,2048,128]{2,1,0:T(8,128)(2,1)}, u32[]{:S(2)}, u32[]{:S(2)}) collective-permute-start(bf16[2,2048,128]{2,1,0:T(8,128)(2,1)} %pad_maximum_fusion.1.refs_2_), channel_id=1, source_target_pairs={{0,4},{4,8},{8,12},{12,16},{16,20},{20,24},{24,28},{1,5},{5,9},{9,... | collective-permute-start | bytes 3145736 | tf_op jit(solution)/shard_map/in_prev1/ppermute | solution.py:317
  62.0 0.7 collective-permute-done.1.refs_4_
  62.7 28.4 %attention.2 = (bf16[512,512]{1,0:T(8,128)(2,1)S(1)}, bf16[512,512]{1,0:T(8,128)(2,1)}, bf16[512,512]{1,0:T(8,128)(2,1)}, bf16[512,512]{1,0:T(8,128)(2,1)}, bf16...) custom-call(s32[2]{0:T(128)S(1)} %pad_add_fusion.place, ...), custom_call_target="tpu_custom_call" | custom-call | flops 32212254720 | bytes 20971520 | tf_op jit(solution)/shard_map/attention/pallas_call | solution.py:215
  91.1 0.8 copy-done
  91.9 1.5 collective-permute-start.12
  93.4 7.7 %all-to-all-start.2 = ((bf16[8,2,2,128,128]{4,3,2,1,0:T(8,128)(2,1)}), bf16[8,2,2,128,128]{4,3,2,1,0:T(8,128)(2,1)}, u32[]{:S(2)}, u32[]{:S(2)}) async-start(bf16[8,2,2,128,128]{4,3,2,1,0:T(8,128)(2,1)} %get-tuple-element.51), calls=%async_computation.2 | async-start | bytes 2097152 | tf_op jit(solution)/shard_map/out_far0/all_to_all | solution.py:375
  101.1 0.7 copy-done.4
  101.9 1.9 collective-permute-start.14
  103.9 0.9 copy-done.5
  104.8 27.8 %attention.3 = (bf16[512,512]{1,0:T(8,128)(2,1)S(1)}, bf16[512,512]{1,0:T(8,128)(2,1)S(1)}, bf16[512,512]{1,0:T(8,128)(2,1)S(1)}, bf16[512,512]{1,0:T(8,128)(2,1...) custom-call(s32[2]{0:T(128)S(1)} %pad_add_fusion.place, ...), custom_call_target="tpu_custom_call" | custom-call | flops 32212254720 | bytes 20971520 | tf_op jit(solution)/shard_map/attention/pallas_call | solution.py:215
  132.6 0.8 copy-done.1
  133.4 0.8 copy-done.3
  134.2 3.5 %collective-permute-done.14 = bf16[2,2048,128]{2,1,0:T(8,128)(2,1)} collective-permute-done((bf16[2,2048,128]{2,1,0:T(8,128)(2,1)}, bf16[2,2048,128]{2,1,0:T(8,128)(2,1)}, u32[]{:S(2)}, u32[]{:S(2)}) %collective-permute-start.14) | collective-permute-done | bytes 1048608 | tf_op jit(solution)/shard_map/out_pair0/ppermute | solution.py:317
  138.1 0.5 collective-permute-start.17
  138.6 2.9 %fusion.3 = bf16[2,2048,128]{2,1,0:T(8,128)(2,1)} fusion(bf16[2,2048,128]{2,1,0:T(8,128)(2,1)} %collective-permute-done.14, bf16[2,2048,128]{2,1,0:T(8,128)(2,1)} %get-tuple-element.58, pred[]{:T(512)S(6)} %eq.33), kind=kLoop, calls=%fused_computation.7 | loop fusion | flops 2621440 | bytes 3145729 | tf_op jit(solution)/shard_map/convert_element_type | solution.py:365
  141.4 1.3 collective-permute-start.19
  142.7 1.8 collective-permute-start.20
  144.5 2.2 collective-permute-done.15
  147.0 1.4 convert_reduce_fusion
  148.4 0.7 slice_bitcast_fusion.8
  149.1 0.8 copy.24
  149.9 5.5 %all-to-all-start.3 = ((bf16[4,2,2,128,128]{4,3,2,1,0:T(8,128)(2,1)}), bf16[4,2,2,128,128]{4,3,2,1,0:T(8,128)(2,1)S(1)}, u32[]{:S(2)}, u32[]{:S(2)}) async-start(bf16[4,2,2,128,128]{4,3,2,1,0:T(8,128)(2,1)} %copy.24), calls=%async_computation.3 | async-start | bytes 1048576 | tf_op jit(solution)/shard_map/out_far/all_to_all | solution.py:398
  155.4 5.0 %collective-permute-done.18.refs_7_ = bf16[512,512]{1,0:T(8,128)(2,1)} collective-permute-done((bf16[512,512]{1,0:T(8,128)(2,1)S(1)}, bf16[512,512]{1,0:T(8,128)(2,1)}, u32[]{:S(2)}, u32[]{:S(2)}) %collective-permute-start.18) | collective-permute-done | bytes 524320 | tf_op jit(solution)/shard_map/out_query1_3/ppermute | solution.py:321
  160.4 5.6 %assemble_queries.1 = bf16[512,4096]{1,0:T(8,128)(2,1)} custom-call(s32[2]{0:T(128)} %copy-done.2, bf16[512,512]{1,0:T(8,128)(2,1)} %copy-done, bf16[512,512]{1,0:T(8,128)(2,1)} %copy-done.1, bf16[512,512]{1,0:T(8,128)(2,1)} %collective-permute-done.11.refs_2_, bf16[512,512]{1,0:T(8,128)(2,1)} %collective-permute-done.16.refs_3_, ...), custom_call_target="tpu_custom_call" | custom-call | tf_op jit(solution)/shard_map/assemble_queries/pallas_call | solution.py:258
  166.0 2.7 %collective-permute-done.20 = bf16[2,2048,128]{2,1,0:T(8,128)(2,1)} collective-permute-done((bf16[2,2048,128]{2,1,0:T(8,128)(2,1)}, bf16[2,2048,128]{2,1,0:T(8,128)(2,1)}, u32[]{:S(2)}, u32[]{:S(2)}) %collective-permute-start.20) | collective-permute-done | bytes 1048608 | tf_op jit(solution)/shard_map/out_pair1/ppermute | solution.py:317
  168.7 2.5 %fusion.7 = bf16[2,2048,128]{2,1,0:T(8,128)(2,1)} fusion(bf16[2,2048,128]{2,1,0:T(8,128)(2,1)} %collective-permute-done.20, bf16[2,2048,128]{2,1,0:T(8,128)(2,1)S(1)} %copy-done.8, pred[]{:T(512)S(6)} %eq.33), kind=kLoop, calls=%fused_computation.11 | loop fusion | flops 2621440 | bytes 3145729 | tf_op jit(solution)/shard_map/convert_element_type | solution.py:365
  171.2 1.6 collective-permute-start.21
  172.9 2.0 fusion.1
  175.3 0.7 fusion.12
  176.0 1.0 dynamic-slice_bitcast_fusion.4
  177.1 0.6 collective-permute-start.22
  177.7 1.0 collective-permute-start.23
  179.0 2.5 %all-to-all-done.3 = bf16[4,2,2,128,128]{4,3,2,1,0:T(8,128)(2,1)S(1)} async-done(((bf16[4,2,2,128,128]{4,3,2,1,0:T(8,128)(2,1)}), bf16[4,2,2,128,128]{4,3,2,1,0:T(8,128)(2,1)S(1)}, u32[]{:S(2)}, u32[]{:S(2)}) %all-to-all-start.3) | async-done | bytes 524320 | tf_op jit(solution)/shard_map/out_far/all_to_all | solution.py:398
  181.6 5.4 %collective-permute-done.23.refs_4_ = bf16[2,512,128]{2,1,0:T(8,128)(2,1)S(1)} collective-permute-done((bf16[2,512,128]{2,1,0:T(8,128)(2,1)}, bf16[2,512,128]{2,1,0:T(8,128)(2,1)S(1)}, u32[]{:S(2)}, u32[]{:S(2)}) %collective-permute-start.23) | collective-permute-done | bytes 262176 | tf_op jit(solution)/shard_map/out_pairs0_2/ppermute | solution.py:321
  187.0 3.8 %collective-permute-done.24.refs_6_ = bf16[2,512,128]{2,1,0:T(8,128)(2,1)S(1)} collective-permute-done((bf16[2,512,128]{2,1,0:T(8,128)(2,1)}, bf16[2,512,128]{2,1,0:T(8,128)(2,1)S(1)}, u32[]{:S(2)}, u32[]{:S(2)}) %collective-permute-start.24) | collective-permute-done | bytes 262176 | tf_op jit(solution)/shard_map/out_pairs0_3/ppermute | solution.py:321
  190.9 10.8 %collective-permute-done.21 = bf16[2,2048,128]{2,1,0:T(8,128)(2,1)S(1)} collective-permute-done((bf16[2,2048,128]{2,1,0:T(8,128)(2,1)}, bf16[2,2048,128]{2,1,0:T(8,128)(2,1)S(1)}, u32[]{:S(2)}, u32[]{:S(2)}) %collective-permute-start.21) | collective-permute-done | bytes 1048608 | tf_op jit(solution)/shard_map/out_onward1/ppermute | solution.py:317
  201.7 1.6 fusion.5
  203.8 0.7 fusion.9
  204.5 0.8 dynamic-slice_bitcast_fusion
  205.4 1.1 collective-permute-start.26
  206.5 0.7 collective-permute-start.27
  207.2 7.2 %collective-permute-done.26.refs_5_ = bf16[2,512,128]{2,1,0:T(8,128)(2,1)S(1)} collective-permute-done((bf16[2,512,128]{2,1,0:T(8,128)(2,1)S(1)}, bf16[2,512,128]{2,1,0:T(8,128)(2,1)S(1)}, u32[]{:S(2)}, u32[]{:S(2)}) %collective-permute-start.26) | collective-permute-done | bytes 262176 | tf_op jit(solution)/shard_map/out_pairs1_2/ppermute | solution.py:321
  214.5 4.8 %collective-permute-done.27.refs_7_ = bf16[2,512,128]{2,1,0:T(8,128)(2,1)S(1)} collective-permute-done((bf16[2,512,128]{2,1,0:T(8,128)(2,1)S(1)}, bf16[2,512,128]{2,1,0:T(8,128)(2,1)S(1)}, u32[]{:S(2)}, u32[]{:S(2)}) %collective-permute-start.27) | collective-permute-done | bytes 262176 | tf_op jit(solution)/shard_map/out_pairs1_3/ppermute | solution.py:321
  219.3 0.7 copy-done.16
  220.0 3.6 %assemble_pairs.1 = (bf16[512,1024]{1,0:T(8,128)(2,1)}, bf16[512,1024]{1,0:T(8,128)(2,1)}) custom-call(s32[2]{0:T(128)} %copy-done.2, bf16[2,512,128]{2,1,0:T(8,128)(2,1)} %get-tuple-element.80.refs_0_, bf16[2,512,128]{2,1,0:T(8,128)(2,1)} %get-tuple-element.76.refs_1_, bf16[2,512,128]{2,1,0:T(8,128)(2,1)} %copy-done.11, bf16[2,512,128]{2,1,0:T(8,128)(2,1)} %copy-done.14, ...), custom_call_target="tpu_custom_call" | custom-call | tf_op jit(solution)/shard_map/assemble_pairs/pallas_call | solution.py:287
  (82 shorter events, 2.8 us)
Async XLA Ops:
  2.3 6.1 %copy-start.6 = (s32[8]{0:T(128)S(1)}, s32[8]{0:T(128)}, u32[]{:S(2)}) copy-start(s32[8]{0:T(128)} %vertical.3) | copy-start | bytes 100
  2.4 30.9 %copy-start.7 = (bf16[2,2048,128]{2,1,0:T(8,128)(2,1)}, bf16[2,2048,128]{2,1,0:T(8,128)(2,1)S(1)}, u32[]{:S(2)}) copy-start(bf16[2,2048,128]{2,1,0:T(8,128)(2,1)S(1)} %pad_maximum_fusion.refs_2_) | copy-start | bytes 3145732
  2.4 28.5 %collective-permute-start = (bf16[2,2048,128]{2,1,0:T(8,128)(2,1)S(1)}, bf16[2,2048,128]{2,1,0:T(8,128)(2,1)}, u32[]{:S(2)}, u32[]{:S(2)}) collective-permute-start(bf16[2,2048,128]{2,1,0:T(8,128)(2,1)S(1)} %pad_maximum_fusion.refs_2_), channel_id=1, source_target_pairs={{0,8},{4,12},{8,16},{12,20},{16,24},{20,28},{1,9},{5,13},{9,17},{1... | collective-permute-start | bytes 3145736 | tf_op jit(solution)/shard_map/in_back0/ppermute | solution.py:317
  9.7 38.4 %collective-permute-start.4 = (bf16[2,2,128,128]{3,2,1,0:T(8,128)(2,1)S(1)}, bf16[2,2,128,128]{3,2,1,0:T(8,128)(2,1)S(1)}, u32[]{:S(2)}, u32[]{:S(2)}) collective-permute-start(bf16[2,2,128,128]{3,2,1,0:T(8,128)(2,1)S(1)} %pad_maximum_fusion.3), channel_id=1, source_target_pairs={{0,24},{1,25},{2,26},{3,27}} | collective-permute-start | bytes 393224 | tf_op jit(solution)/shard_map/in_first6/ppermute | solution.py:317
  12.0 36.0 %collective-permute-start.3 = (bf16[2,2,128,128]{3,2,1,0:T(8,128)(2,1)S(1)}, bf16[2,2,128,128]{3,2,1,0:T(8,128)(2,1)S(1)}, u32[]{:S(2)}, u32[]{:S(2)}) collective-permute-start(bf16[2,2,128,128]{3,2,1,0:T(8,128)(2,1)S(1)} %pad_maximum_fusion.3), channel_id=1, source_target_pairs={{0,16},{1,17},{2,18},{3,19}} | collective-permute-start | bytes 393224 | tf_op jit(solution)/shard_map/in_first4/ppermute | solution.py:317
  13.9 34.2 %collective-permute-start.2 = (bf16[2,2,128,128]{3,2,1,0:T(8,128)(2,1)S(1)}, bf16[2,2,128,128]{3,2,1,0:T(8,128)(2,1)}, u32[]{:S(2)}, u32[]{:S(2)}) collective-permute-start(bf16[2,2,128,128]{3,2,1,0:T(8,128)(2,1)S(1)} %pad_maximum_fusion.3), channel_id=1, source_target_pairs={{0,8},{1,9},{2,10},{3,11}} | collective-permute-start | bytes 393224 | tf_op jit(solution)/shard_map/in_first2/ppermute | solution.py:317
  15.9 46.2 %collective-permute-start.6 = (bf16[2,2048,128]{2,1,0:T(8,128)(2,1)S(1)}, bf16[2,2048,128]{2,1,0:T(8,128)(2,1)}, u32[]{:S(2)}, u32[]{:S(2)}) collective-permute-start(bf16[2,2048,128]{2,1,0:T(8,128)(2,1)S(1)} %pad_maximum_fusion.refs_2_), channel_id=1, source_target_pairs={{0,4},{8,12},{16,20},{24,28},{1,5},{9,13},{17,21},{25,29},{2,6},{1... | collective-permute-start | bytes 3145736 | tf_op jit(solution)/shard_map/in_even0/ppermute | solution.py:317
  18.9 33.0 %copy-start.17 = (s32[16,2]{0,1:T(2,128)S(1)}, s32[16,2]{0,1:T(2,128)}, u32[]{:S(2)}) copy-start(s32[16,2]{0,1:T(2,128)} %param.12) | copy-start | bytes 388
  18.9 33.1 %copy-start.18 = (s32[16,2]{0,1:T(2,128)S(1)}, s32[16,2]{0,1:T(2,128)}, u32[]{:S(2)}) copy-start(s32[16,2]{0,1:T(2,128)} %param.13) | copy-start | bytes 388
  18.9 23.7 %all-to-all-start = ((bf16[4,2,128,128]{3,2,1,0:T(8,128)(2,1)}), bf16[4,2,128,128]{3,2,1,0:T(8,128)(2,1)S(1)}, u32[]{:S(2)}, u32[]{:S(2)}) async-start(bf16[4,2,128,128]{3,2,1,0:T(8,128)(2,1)} %broadcast_in_dim.92), calls=%async_computation | async-start | bytes 524288 | tf_op jit(solution)/shard_map/in_column0/all_to_all | solution.py:339
  30.9 31.8 %collective-permute-start.7 = (bf16[2,2048,128]{2,1,0:T(8,128)(2,1)}, bf16[2,2048,128]{2,1,0:T(8,128)(2,1)}, u32[]{:S(2)}, u32[]{:S(2)}) collective-permute-start(bf16[2,2048,128]{2,1,0:T(8,128)(2,1)} %collective-permute-done.refs_7_), channel_id=1, source_target_pairs={{4,0},{12,8},{20,16},{28,24},{5,1},{13,9},{21,17},{29,25},{6,2},{1... | collective-permute-start | bytes 3145736 | tf_op jit(solution)/shard_map/in_odd0/ppermute | solution.py:317
  43.3 18.7 %all-to-all-start.1 = ((bf16[4,2,128,128]{3,2,1,0:T(8,128)(2,1)}), bf16[4,2,128,128]{3,2,1,0:T(8,128)(2,1)S(1)}, u32[]{:S(2)}, u32[]{:S(2)}) async-start(bf16[4,2,128,128]{3,2,1,0:T(8,128)(2,1)} %broadcast_in_dim.94), calls=%async_computation.1 | async-start | bytes 524288 | tf_op jit(solution)/shard_map/in_column1/all_to_all | solution.py:339
  49.0 8.1 %collective-permute-start.5 = (bf16[2,2,128,128]{3,2,1,0:T(8,128)(2,1)S(1)}, bf16[2,2,128,128]{3,2,1,0:T(8,128)(2,1)S(1)}, u32[]{:S(2)}, u32[]{:S(2)}) collective-permute-start(bf16[2,2,128,128]{3,2,1,0:T(8,128)(2,1)S(1)} %add_add_fusion.refs_5_), channel_id=1, source_target_pairs={{0,4},{8,12},{16,20},{24,28},{1,5},{9,13},{17,21},{25,29},{2,6},{1... | collective-permute-start | bytes 393224 | tf_op jit(solution)/shard_map/in_first_pair/ppermute | solution.py:317
  51.8 10.9 %collective-permute-start.1 = (bf16[4,2,128,128]{3,2,1,0:T(8,128)(2,1)S(1)}, bf16[4,2,128,128]{3,2,1,0:T(8,128)(2,1)S(1)}, u32[]{:S(2)}, u32[]{:S(2)}) collective-permute-start(bf16[4,2,128,128]{3,2,1,0:T(8,128)(2,1)S(1)} %all-to-all-done.refs_3_), channel_id=1, source_target_pairs={{0,4},{4,0},{8,12},{12,8},{16,20},{20,16},{24,28},{28,24},{1,5},{5... | collective-permute-start | bytes 786440 | tf_op jit(solution)/shard_map/in_column_pair0/ppermute | solution.py:317
  52.2 51.7 %copy-start.2 = (s32[2]{0:T(128)}, s32[2]{0:T(128)S(1)}, u32[]{:S(2)}) copy-start(s32[2]{0:T(128)S(1)} %pad_add_fusion.place) | copy-start | bytes 28
  52.2 49.7 %collective-permute-start.9 = (bf16[2,2048,128]{2,1,0:T(8,128)(2,1)}, bf16[2,2048,128]{2,1,0:T(8,128)(2,1)}, u32[]{:S(2)}, u32[]{:S(2)}) collective-permute-start(bf16[2,2048,128]{2,1,0:T(8,128)(2,1)} %pad_maximum_fusion.1.refs_2_), channel_id=1, source_target_pairs={{0,8},{4,12},{8,16},{12,20},{16,24},{20,28},{1,9},{5,13},{9,17},{1... | collective-permute-start | bytes 3145736 | tf_op jit(solution)/shard_map/in_back1/ppermute | solution.py:317
  57.1 46.8 %collective-permute-start.10 = (bf16[2,2048,128]{2,1,0:T(8,128)(2,1)}, bf16[2,2048,128]{2,1,0:T(8,128)(2,1)}, u32[]{:S(2)}, u32[]{:S(2)}) collective-permute-start(bf16[2,2048,128]{2,1,0:T(8,128)(2,1)} %pad_maximum_fusion.1.refs_2_), channel_id=1, source_target_pairs={{0,4},{4,8},{8,12},{12,16},{16,20},{20,24},{24,28},{1,5},{5,9},{9,... | collective-permute-start | bytes 3145736 | tf_op jit(solution)/shard_map/in_prev1/ppermute | solution.py:317
  62.0 39.1 %collective-permute-start.8 = (bf16[4,2,128,128]{3,2,1,0:T(8,128)(2,1)S(1)}, bf16[4,2,128,128]{3,2,1,0:T(8,128)(2,1)S(1)}, u32[]{:S(2)}, u32[]{:S(2)}) collective-permute-start(bf16[4,2,128,128]{3,2,1,0:T(8,128)(2,1)S(1)} %all-to-all-done.1.refs_3_), channel_id=1, source_target_pairs={{0,4},{4,0},{8,12},{12,8},{16,20},{20,16},{24,28},{28,24},{1,5},{5... | collective-permute-start | bytes 786440 | tf_op jit(solution)/shard_map/in_column_pair1/ppermute | solution.py:317
  91.1 0.8 copy-start
  91.9 45.8 %collective-permute-start.11 = (bf16[512,512]{1,0:T(8,128)(2,1)}, bf16[512,512]{1,0:T(8,128)(2,1)}, u32[]{:S(2)}, u32[]{:S(2)}) collective-permute-start(bf16[512,512]{1,0:T(8,128)(2,1)} %get-tuple-element.48), channel_id=1, source_target_pairs={{0,1},{1,0},{2,3},{3,2},{4,5},{5,4},{6,7},{7,6},{8,9},{9,8},{10,11... | collective-permute-start | bytes 1572872 | tf_op jit(solution)/shard_map/out_query0_1/ppermute | solution.py:321
  91.9 45.8 %collective-permute-start.12 = (bf16[512,512]{1,0:T(8,128)(2,1)}, bf16[512,512]{1,0:T(8,128)(2,1)}, u32[]{:S(2)}, u32[]{:S(2)}) collective-permute-start(bf16[512,512]{1,0:T(8,128)(2,1)} %get-tuple-element.49), channel_id=1, source_target_pairs={{0,2},{1,3},{2,0},{3,1},{4,6},{5,7},{6,4},{7,5},{8,10},{9,11},{10,... | collective-permute-start | bytes 1572872 | tf_op jit(solution)/shard_map/out_query0_2/ppermute | solution.py:321
  93.4 44.3 %all-to-all-start.2 = ((bf16[8,2,2,128,128]{4,3,2,1,0:T(8,128)(2,1)}), bf16[8,2,2,128,128]{4,3,2,1,0:T(8,128)(2,1)}, u32[]{:S(2)}, u32[]{:S(2)}) async-start(bf16[8,2,2,128,128]{4,3,2,1,0:T(8,128)(2,1)} %get-tuple-element.51), calls=%async_computation.2 | async-start | bytes 2097152 | tf_op jit(solution)/shard_map/out_far0/all_to_all | solution.py:375
  101.1 0.7 copy-start.4
  101.8 35.9 %collective-permute-start.13 = (bf16[512,512]{1,0:T(8,128)(2,1)}, bf16[512,512]{1,0:T(8,128)(2,1)}, u32[]{:S(2)}, u32[]{:S(2)}) collective-permute-start(bf16[512,512]{1,0:T(8,128)(2,1)} %get-tuple-element.50), channel_id=1, source_target_pairs={{0,3},{1,2},{2,1},{3,0},{4,7},{5,6},{6,5},{7,4},{8,11},{9,10},{10,... | collective-permute-start | bytes 1572872 | tf_op jit(solution)/shard_map/out_query0_3/ppermute | solution.py:321
  101.9 35.8 %collective-permute-start.14 = (bf16[2,2048,128]{2,1,0:T(8,128)(2,1)}, bf16[2,2048,128]{2,1,0:T(8,128)(2,1)}, u32[]{:S(2)}, u32[]{:S(2)}) collective-permute-start(bf16[2,2048,128]{2,1,0:T(8,128)(2,1)} %get-tuple-element.53), channel_id=1, source_target_pairs={{0,4},{4,0},{8,12},{12,8},{16,20},{20,16},{24,28},{28,24},{1,5},{5... | collective-permute-start | bytes 3145736 | tf_op jit(solution)/shard_map/out_pair0/ppermute | solution.py:317
  103.9 1.0 copy-start.5
  132.6 0.8 copy-start.1
  133.4 0.8 copy-start.3
  137.7 9.0 %collective-permute-start.15 = (bf16[5,2,128,128]{3,2,1,0:T(8,128)(2,1)}, bf16[5,2,128,128]{3,2,1,0:T(8,128)(2,1)S(1)}, u32[]{:S(2)}, u32[]{:S(2)}) collective-permute-start(bf16[5,2,128,128]{3,2,1,0:T(8,128)(2,1)} %copy-done.3), channel_id=1, source_target_pairs={{0,4},{4,0},{8,12},{12,8},{16,20},{20,16},{24,28},{28,24},{1,5},{5... | collective-permute-start | bytes 983048 | tf_op jit(solution)/shard_map/out_far_pair1/ppermute | solution.py:317
  138.1 17.4 %collective-permute-start.17 = (bf16[512,512]{1,0:T(8,128)(2,1)S(1)}, bf16[512,512]{1,0:T(8,128)(2,1)}, u32[]{:S(2)}, u32[]{:S(2)}) collective-permute-start(bf16[512,512]{1,0:T(8,128)(2,1)S(1)} %get-tuple-element.64), channel_id=1, source_target_pairs={{0,2},{1,3},{2,0},{3,1},{4,6},{5,7},{6,4},{7,5},{8,10},{9,11},{10,... | collective-permute-start | bytes 1572872 | tf_op jit(solution)/shard_map/out_query1_2/ppermute | solution.py:321
  138.6 21.9 %collective-permute-start.18 = (bf16[512,512]{1,0:T(8,128)(2,1)S(1)}, bf16[512,512]{1,0:T(8,128)(2,1)}, u32[]{:S(2)}, u32[]{:S(2)}) collective-permute-start(bf16[512,512]{1,0:T(8,128)(2,1)S(1)} %get-tuple-element.65), channel_id=1, source_target_pairs={{0,3},{1,2},{2,1},{3,0},{4,7},{5,6},{6,5},{7,4},{8,11},{9,10},{10,... | collective-permute-start | bytes 1572872 | tf_op jit(solution)/shard_map/out_query1_3/ppermute | solution.py:321
  141.4 31.4 %collective-permute-start.19 = (bf16[2,2048,128]{2,1,0:T(8,128)(2,1)}, bf16[2,2048,128]{2,1,0:T(8,128)(2,1)}, u32[]{:S(2)}, u32[]{:S(2)}) collective-permute-start(bf16[2,2048,128]{2,1,0:T(8,128)(2,1)} %fusion.3), channel_id=1, source_target_pairs={{8,0},{12,4},{16,8},{20,12},{24,16},{28,20},{9,1},{13,5},{17,9},{2... | collective-permute-start | bytes 3145736 | tf_op jit(solution)/shard_map/out_onward0/ppermute | solution.py:317
  142.7 25.9 %collective-permute-start.20 = (bf16[2,2048,128]{2,1,0:T(8,128)(2,1)}, bf16[2,2048,128]{2,1,0:T(8,128)(2,1)}, u32[]{:S(2)}, u32[]{:S(2)}) collective-permute-start(bf16[2,2048,128]{2,1,0:T(8,128)(2,1)} %get-tuple-element.67), channel_id=1, source_target_pairs={{0,4},{4,0},{8,12},{12,8},{16,20},{20,16},{24,28},{28,24},{1,5},{5... | collective-permute-start | bytes 3145736 | tf_op jit(solution)/shard_map/out_pair1/ppermute | solution.py:317
  146.9 13.5 %collective-permute-start.16 = (bf16[512,512]{1,0:T(8,128)(2,1)S(1)}, bf16[512,512]{1,0:T(8,128)(2,1)}, u32[]{:S(2)}, u32[]{:S(2)}) collective-permute-start(bf16[512,512]{1,0:T(8,128)(2,1)S(1)} %get-tuple-element.63), channel_id=1, source_target_pairs={{0,1},{1,0},{2,3},{3,2},{4,5},{5,4},{6,7},{7,6},{8,9},{9,8},{10,11... | collective-permute-start | bytes 1572872 | tf_op jit(solution)/shard_map/out_query1_1/ppermute | solution.py:321
  149.9 31.5 %all-to-all-start.3 = ((bf16[4,2,2,128,128]{4,3,2,1,0:T(8,128)(2,1)}), bf16[4,2,2,128,128]{4,3,2,1,0:T(8,128)(2,1)S(1)}, u32[]{:S(2)}, u32[]{:S(2)}) async-start(bf16[4,2,2,128,128]{4,3,2,1,0:T(8,128)(2,1)} %copy.24), calls=%async_computation.3 | async-start | bytes 1048576 | tf_op jit(solution)/shard_map/out_far/all_to_all | solution.py:398
  160.4 8.2 %copy-start.8 = (bf16[2,2048,128]{2,1,0:T(8,128)(2,1)S(1)}, bf16[2,2048,128]{2,1,0:T(8,128)(2,1)}, u32[]{:S(2)}) copy-start(bf16[2,2048,128]{2,1,0:T(8,128)(2,1)} %get-tuple-element.69) | copy-start | bytes 3145732
  171.2 3.6 %copy-start.10 = (f32[2,128,128]{2,1,0:T(8,128)S(1)}, f32[2,128,128]{2,1,0:T(8,128)}, u32[]{:S(2)}) copy-start(f32[2,128,128]{2,1,0:T(8,128)} %get-tuple-element.92) | copy-start | bytes 393220
  171.2 30.4 %collective-permute-start.21 = (bf16[2,2048,128]{2,1,0:T(8,128)(2,1)}, bf16[2,2048,128]{2,1,0:T(8,128)(2,1)S(1)}, u32[]{:S(2)}, u32[]{:S(2)}) collective-permute-start(bf16[2,2048,128]{2,1,0:T(8,128)(2,1)} %fusion.7), channel_id=1, source_target_pairs={{8,0},{12,4},{16,8},{20,12},{24,16},{28,20},{9,1},{13,5},{17,9},{2... | collective-permute-start | bytes 3145736 | tf_op jit(solution)/shard_map/out_onward1/ppermute | solution.py:317
  176.0 25.6 %copy-start.9 = (bf16[2,2048,128]{2,1,0:T(8,128)(2,1)S(1)}, bf16[2,2048,128]{2,1,0:T(8,128)(2,1)}, u32[]{:S(2)}) copy-start(bf16[2,2048,128]{2,1,0:T(8,128)(2,1)} %get-tuple-element.66) | copy-start | bytes 3145732
  177.1 4.5 %collective-permute-start.22 = (bf16[2,512,128]{2,1,0:T(8,128)(2,1)}, bf16[2,512,128]{2,1,0:T(8,128)(2,1)S(1)}, u32[]{:S(2)}, u32[]{:S(2)}) collective-permute-start(bf16[2,512,128]{2,1,0:T(8,128)(2,1)} %get-tuple-element.79), channel_id=1, source_target_pairs={{0,1},{1,0},{2,3},{3,2},{4,5},{5,4},{6,7},{7,6},{8,9},{9,8},{10,11... | collective-permute-start | bytes 786440 | tf_op jit(solution)/shard_map/out_pairs0_1/ppermute | solution.py:321
  177.7 9.4 %collective-permute-start.23 = (bf16[2,512,128]{2,1,0:T(8,128)(2,1)}, bf16[2,512,128]{2,1,0:T(8,128)(2,1)S(1)}, u32[]{:S(2)}, u32[]{:S(2)}) collective-permute-start(bf16[2,512,128]{2,1,0:T(8,128)(2,1)} %get-tuple-element.78), channel_id=1, source_target_pairs={{0,2},{1,3},{2,0},{3,1},{4,6},{5,7},{6,4},{7,5},{8,10},{9,11},{10,... | collective-permute-start | bytes 786440 | tf_op jit(solution)/shard_map/out_pairs0_2/ppermute | solution.py:321
  178.7 12.2 %collective-permute-start.24 = (bf16[2,512,128]{2,1,0:T(8,128)(2,1)}, bf16[2,512,128]{2,1,0:T(8,128)(2,1)S(1)}, u32[]{:S(2)}, u32[]{:S(2)}) collective-permute-start(bf16[2,512,128]{2,1,0:T(8,128)(2,1)} %get-tuple-element.77), channel_id=1, source_target_pairs={{0,3},{1,2},{2,1},{3,0},{4,7},{5,6},{6,5},{7,4},{8,11},{9,10},{10,... | collective-permute-start | bytes 786440 | tf_op jit(solution)/shard_map/out_pairs0_3/ppermute | solution.py:321
  181.6 21.7 %copy-start.11 = (bf16[2,512,128]{2,1,0:T(8,128)(2,1)}, bf16[2,512,128]{2,1,0:T(8,128)(2,1)S(1)}, u32[]{:S(2)}) copy-start(bf16[2,512,128]{2,1,0:T(8,128)(2,1)S(1)} %collective-permute-done.22.refs_2_) | copy-start | bytes 786436
  187.0 16.3 %copy-start.12 = (bf16[2,512,128]{2,1,0:T(8,128)(2,1)}, bf16[2,512,128]{2,1,0:T(8,128)(2,1)S(1)}, u32[]{:S(2)}) copy-start(bf16[2,512,128]{2,1,0:T(8,128)(2,1)S(1)} %collective-permute-done.23.refs_4_) | copy-start | bytes 786436
  190.9 12.5 %copy-start.13 = (bf16[2,512,128]{2,1,0:T(8,128)(2,1)}, bf16[2,512,128]{2,1,0:T(8,128)(2,1)S(1)}, u32[]{:S(2)}) copy-start(bf16[2,512,128]{2,1,0:T(8,128)(2,1)S(1)} %collective-permute-done.24.refs_6_) | copy-start | bytes 786436
  205.4 1.9 collective-permute-start.25
  205.4 9.1 %collective-permute-start.26 = (bf16[2,512,128]{2,1,0:T(8,128)(2,1)S(1)}, bf16[2,512,128]{2,1,0:T(8,128)(2,1)S(1)}, u32[]{:S(2)}, u32[]{:S(2)}) collective-permute-start(bf16[2,512,128]{2,1,0:T(8,128)(2,1)S(1)} %get-tuple-element.74), channel_id=1, source_target_pairs={{0,2},{1,3},{2,0},{3,1},{4,6},{5,7},{6,4},{7,5},{8,10},{9,11},{10,... | collective-permute-start | bytes 786440 | tf_op jit(solution)/shard_map/out_pairs1_2/ppermute | solution.py:321
  206.5 12.8 %collective-permute-start.27 = (bf16[2,512,128]{2,1,0:T(8,128)(2,1)S(1)}, bf16[2,512,128]{2,1,0:T(8,128)(2,1)S(1)}, u32[]{:S(2)}, u32[]{:S(2)}) collective-permute-start(bf16[2,512,128]{2,1,0:T(8,128)(2,1)S(1)} %get-tuple-element.73), channel_id=1, source_target_pairs={{0,3},{1,2},{2,1},{3,0},{4,7},{5,6},{6,5},{7,4},{8,11},{9,10},{10,... | collective-permute-start | bytes 786440 | tf_op jit(solution)/shard_map/out_pairs1_3/ppermute | solution.py:321
  207.2 12.1 %copy-start.14 = (bf16[2,512,128]{2,1,0:T(8,128)(2,1)}, bf16[2,512,128]{2,1,0:T(8,128)(2,1)S(1)}, u32[]{:S(2)}) copy-start(bf16[2,512,128]{2,1,0:T(8,128)(2,1)S(1)} %collective-permute-done.25.refs_3_) | copy-start | bytes 786436
  214.5 4.9 %copy-start.15 = (bf16[2,512,128]{2,1,0:T(8,128)(2,1)}, bf16[2,512,128]{2,1,0:T(8,128)(2,1)S(1)}, u32[]{:S(2)}) copy-start(bf16[2,512,128]{2,1,0:T(8,128)(2,1)S(1)} %collective-permute-done.26.refs_5_) | copy-start | bytes 786436
  219.3 0.7 copy-start.16

commit v6 on v5

--- a/solution.py
+++ b/solution.py
@@ -393,10 +393,13 @@
             for at, ((own_before, side_before, _), piece) in enumerate(zip(results, sent))
         ]
         far_sum = (keep.astype(jnp.float32) + got.astype(jnp.float32)).astype(jnp.bfloat16)
-        far_sum = jnp.stack([far_sum[:planes], jnp.broadcast_to(far_sum[planes], far_sum[:planes].shape)], axis=1)
         with jax.named_scope("out_far"):
-            fars.append(lax.all_to_all(far_sum, "seq", split_axis=0, concat_axis=0, axis_index_groups=groups))
+            far = lax.all_to_all(far_sum[:planes], "seq", split_axis=0, concat_axis=0, axis_index_groups=groups)
+        first = far_sum[planes].astype(jnp.float32)
+        for at in range(2, seq_size, 2):
+            first = first + along(far_sum[planes], [(at, 0)], f"out_first{at}").astype(jnp.float32)
         fars = [jnp.sum(terms.astype(jnp.float32), axis=0) for terms in fars]
+        fars.append((jnp.sum(far.astype(jnp.float32), axis=0), first))
         if heads > 1:
             query_pieces[1, head] = across(after(dqs[1], far_sum), 1, f"out_query{head}_1")
         query_pieces[0, head] = dqs[0]

time: 225 us -> 225 us (level)
  starting transfers between devices: 62.9 us -> 65.4 us
    ppermute x12, waiting for transfers between devices: 26.4 us -> 21 us  [across(): lax.ppermute(array, 'head', [(i, i ^ k) for i in range(heads)])]
    ppermute x16 -> x19, waiting for transfers between devices: 28.3 us -> 32.9 us  [along(): return lax.ppermute(array, 'seq', pairs)]
    all_to_all x1, waiting for transfers between devices: 2.46 us -> 0.01 us  [shards(): lax.all_to_all(far_sum[:planes], 'seq', split_axis=0, concat_axis=0, axis...]
    ppermute x16 -> x19, starting transfers between devices: 35.4 us -> 37.6 us  [along(): return lax.ppermute(array, 'seq', pairs)]
    unnamed x42 -> x34, local copies, waits for them, and re-layouts: 5.07 us -> 5.03 us
  transfers between devices with their start and end apart: 32 -> 35, of which waited for: 13 -> 13; matrix products, arithmetic and copies ran while one was open for 8% -> 8% of each run, Pallas kernels for 28% -> 28%
where the time goes in v6:
time: 225 us; the launch traced here: 224 us
  starting transfers between devices  65.4 us (29%)
  Pallas kernels  65.4 us (29%)
  waiting for transfers between devices  64.2 us (29%)
  other arithmetic  14.5 us (6%)
  local copies, waits for them, and re-layouts  12.9 us (6%)
    pallas_call x2, Pallas kernels, attention(): pl.pallas_call(functools.partial(attention_kernel, (local_blocks, group,...  56.2 us
    ppermute x19, starting transfers between devices, along(): return lax.ppermute(array, 'seq', pairs)  37.6 us
    ppermute x19, waiting for transfers between devices, along(): return lax.ppermute(array, 'seq', pairs)  32.9 us
    ppermute x12, waiting for transfers between devices, across(): lax.ppermute(array, 'head', [(i, i ^ k) for i in range(heads)])  21 us
    all_to_all x2, waiting for transfers between devices, column_of(): lax.all_to_all(wide, 'seq', split_axis=0, concat_axis=0, axis_index_group...  10.2 us
    all_to_all x2, starting transfers between devices, column_of(): lax.all_to_all(wide, 'seq', split_axis=0, concat_axis=0, axis_index_group...  8.28 us
    all_to_all x1, starting transfers between devices, shards(): fars.append(lax.all_to_all(table[0], 'seq', split_axis=0, concat_axis=0))  7.6 us
    ppermute x12, starting transfers between devices, across(): lax.ppermute(array, 'head', [(i, i ^ k) for i in range(heads)])  6.15 us
  transfers between devices with their start and end apart: 35, of which 13 were waited for; matrix products, arithmetic and copies ran while one was open for 8% of the time, Pallas kernels for 28%

profile of v6, /device:TPU:0, one launch (start us, length us, event | category | flops | bytes accessed | tf_op | source)
XLA Modules:
  0.0 224.0 jit_solution(8721526792263348547)
XLA Ops:
  0.6 1.7 slice_bitcast_fusion
  2.4 5.9 %collective-permute-start = (bf16[2,2048,128]{2,1,0:T(8,128)(2,1)S(1)}, bf16[2,2048,128]{2,1,0:T(8,128)(2,1)}, u32[]{:S(2)}, u32[]{:S(2)}) collective-permute-start(bf16[2,2048,128]{2,1,0:T(8,128)(2,1)S(1)} %pad_maximum_fusion.refs_2_), channel_id=1, source_target_pairs={{0,8},{4,12},{8,16},{12,20},{16,24},{20,28},{1,9},{5,13},{9,17},{1... | collective-permute-start | bytes 3145736 | tf_op jit(solution)/shard_map/in_back0/ppermute | solution.py:317
  9.7 2.4 %collective-permute-start.4 = (bf16[2,2,128,128]{3,2,1,0:T(8,128)(2,1)S(1)}, bf16[2,2,128,128]{3,2,1,0:T(8,128)(2,1)S(1)}, u32[]{:S(2)}, u32[]{:S(2)}) collective-permute-start(bf16[2,2,128,128]{3,2,1,0:T(8,128)(2,1)S(1)} %pad_maximum_fusion.2), channel_id=1, source_target_pairs={{0,24},{1,25},{2,26},{3,27}} | collective-permute-start | bytes 393224 | tf_op jit(solution)/shard_map/in_first6/ppermute | solution.py:317
  12.0 1.9 collective-permute-start.3
  13.9 2.0 collective-permute-start.2
  15.8 2.3 %collective-permute-start.6 = (bf16[2,2048,128]{2,1,0:T(8,128)(2,1)S(1)}, bf16[2,2048,128]{2,1,0:T(8,128)(2,1)}, u32[]{:S(2)}, u32[]{:S(2)}) collective-permute-start(bf16[2,2048,128]{2,1,0:T(8,128)(2,1)S(1)} %pad_maximum_fusion.refs_2_), channel_id=1, source_target_pairs={{0,4},{8,12},{16,20},{24,28},{1,5},{9,13},{17,21},{25,29},{2,6},{1... | collective-permute-start | bytes 3145736 | tf_op jit(solution)/shard_map/in_even0/ppermute | solution.py:317
  18.2 0.7 broadcast_in_dim.90
  18.9 3.5 %all-to-all-start = ((bf16[4,2,128,128]{3,2,1,0:T(8,128)(2,1)}), bf16[4,2,128,128]{3,2,1,0:T(8,128)(2,1)S(1)}, u32[]{:S(2)}, u32[]{:S(2)}) async-start(bf16[4,2,128,128]{3,2,1,0:T(8,128)(2,1)} %broadcast_in_dim.90), calls=%async_computation | async-start | bytes 524288 | tf_op jit(solution)/shard_map/in_column0/all_to_all | solution.py:339
  22.4 0.7 fusion.21
  23.1 1.1 pad_maximum_fusion.1.refs_2_
  24.2 6.7 %collective-permute-done.refs_7_ = bf16[2,2048,128]{2,1,0:T(8,128)(2,1)} collective-permute-done((bf16[2,2048,128]{2,1,0:T(8,128)(2,1)S(1)}, bf16[2,2048,128]{2,1,0:T(8,128)(2,1)}, u32[]{:S(2)}, u32[]{:S(2)}) %collective-permute-start) | collective-permute-done | bytes 1048608 | tf_op jit(solution)/shard_map/in_back0/ppermute | solution.py:317
  30.9 1.3 collective-permute-start.7
  32.4 10.2 %all-to-all-done.refs_3_ = bf16[4,2,128,128]{3,2,1,0:T(8,128)(2,1)S(1)} async-done(((bf16[4,2,128,128]{3,2,1,0:T(8,128)(2,1)}), bf16[4,2,128,128]{3,2,1,0:T(8,128)(2,1)S(1)}, u32[]{:S(2)}, u32[]{:S(2)}) %all-to-all-start) | async-done | bytes 262176 | tf_op jit(solution)/shard_map/in_column0/all_to_all | solution.py:339
  42.6 0.7 broadcast_in_dim.92
  43.3 4.7 %all-to-all-start.1 = ((bf16[4,2,128,128]{3,2,1,0:T(8,128)(2,1)}), bf16[4,2,128,128]{3,2,1,0:T(8,128)(2,1)S(1)}, u32[]{:S(2)}, u32[]{:S(2)}) async-start(bf16[4,2,128,128]{3,2,1,0:T(8,128)(2,1)} %broadcast_in_dim.92), calls=%async_computation.1 | async-start | bytes 524288 | tf_op jit(solution)/shard_map/in_column1/all_to_all | solution.py:339
  48.1 0.9 add_add_fusion.refs_5_
  49.0 1.3 collective-permute-start.5
  50.7 4.9 %collective-permute-start.9 = (bf16[2,2048,128]{2,1,0:T(8,128)(2,1)}, bf16[2,2048,128]{2,1,0:T(8,128)(2,1)}, u32[]{:S(2)}, u32[]{:S(2)}) collective-permute-start(bf16[2,2048,128]{2,1,0:T(8,128)(2,1)} %pad_maximum_fusion.1.refs_2_), channel_id=1, source_target_pairs={{0,8},{4,12},{8,16},{12,20},{16,24},{20,28},{1,9},{5,13},{9,17},{1... | collective-permute-start | bytes 3145736 | tf_op jit(solution)/shard_map/in_back1/ppermute | solution.py:317
  55.6 4.9 %collective-permute-start.10 = (bf16[2,2048,128]{2,1,0:T(8,128)(2,1)}, bf16[2,2048,128]{2,1,0:T(8,128)(2,1)}, u32[]{:S(2)}, u32[]{:S(2)}) collective-permute-start(bf16[2,2048,128]{2,1,0:T(8,128)(2,1)} %pad_maximum_fusion.1.refs_2_), channel_id=1, source_target_pairs={{0,4},{4,8},{8,12},{12,16},{16,20},{20,24},{24,28},{1,5},{5,9},{9,... | collective-permute-start | bytes 3145736 | tf_op jit(solution)/shard_map/in_prev1/ppermute | solution.py:317
  60.5 2.4 %collective-permute-done.1.refs_4_ = bf16[4,2,128,128]{3,2,1,0:T(8,128)(2,1)S(1)} collective-permute-done((bf16[4,2,128,128]{3,2,1,0:T(8,128)(2,1)S(1)}, bf16[4,2,128,128]{3,2,1,0:T(8,128)(2,1)S(1)}, u32[]{:S(2)}, u32[]{:S(2)}) %collective-permute-start.1) | collective-permute-done | bytes 262176 | tf_op jit(solution)/shard_map/in_column_pair0/ppermute | solution.py:317
  62.8 28.3 %attention.2 = (bf16[512,512]{1,0:T(8,128)(2,1)S(1)}, bf16[512,512]{1,0:T(8,128)(2,1)}, bf16[512,512]{1,0:T(8,128)(2,1)}, bf16[512,512]{1,0:T(8,128)(2,1)}, bf16...) custom-call(s32[2]{0:T(128)S(1)} %pad_add_fusion.place, ...), custom_call_target="tpu_custom_call" | custom-call | flops 32212254720 | bytes 20971520 | tf_op jit(solution)/shard_map/attention/pallas_call | solution.py:215
  91.2 0.8 copy-done
  92.0 1.5 collective-permute-start.12
  93.5 7.6 %all-to-all-start.2 = ((bf16[8,2,2,128,128]{4,3,2,1,0:T(8,128)(2,1)}), bf16[8,2,2,128,128]{4,3,2,1,0:T(8,128)(2,1)}, u32[]{:S(2)}, u32[]{:S(2)}) async-start(bf16[8,2,2,128,128]{4,3,2,1,0:T(8,128)(2,1)} %get-tuple-element.51), calls=%async_computation.2 | async-start | bytes 2097152 | tf_op jit(solution)/shard_map/out_far0/all_to_all | solution.py:375
  101.1 0.7 copy-done.4
  101.9 1.9 collective-permute-start.14
  103.8 0.9 copy-done.5
  104.8 27.9 %attention.3 = (bf16[512,512]{1,0:T(8,128)(2,1)S(1)}, bf16[512,512]{1,0:T(8,128)(2,1)S(1)}, bf16[512,512]{1,0:T(8,128)(2,1)S(1)}, bf16[512,512]{1,0:T(8,128)(2,1...) custom-call(s32[2]{0:T(128)S(1)} %pad_add_fusion.place, ...), custom_call_target="tpu_custom_call" | custom-call | flops 32212254720 | bytes 20971520 | tf_op jit(solution)/shard_map/attention/pallas_call | solution.py:215
  132.7 0.8 copy-done.1
  133.5 0.7 copy-done.3
  134.2 3.4 %collective-permute-done.14 = bf16[2,2048,128]{2,1,0:T(8,128)(2,1)} collective-permute-done((bf16[2,2048,128]{2,1,0:T(8,128)(2,1)}, bf16[2,2048,128]{2,1,0:T(8,128)(2,1)}, u32[]{:S(2)}, u32[]{:S(2)}) %collective-permute-start.14) | collective-permute-done | bytes 1048608 | tf_op jit(solution)/shard_map/out_pair0/ppermute | solution.py:317
  138.6 1.7 collective-permute-start.20
  140.3 2.9 %fusion.3 = bf16[2,2048,128]{2,1,0:T(8,128)(2,1)} fusion(bf16[2,2048,128]{2,1,0:T(8,128)(2,1)} %collective-permute-done.14, bf16[2,2048,128]{2,1,0:T(8,128)(2,1)} %get-tuple-element.58, pred[]{:T(512)S(6)} %eq.33), kind=kLoop, calls=%fused_computation.7 | loop fusion | flops 2621440 | bytes 3145729 | tf_op jit(solution)/shard_map/convert_element_type | solution.py:365
  143.1 1.3 collective-permute-start.19
  144.4 1.4 convert_reduce_fusion
  145.8 0.7 slice_bitcast_fusion.5
  146.5 2.1 collective-permute-done.15
  148.7 0.7 slice.49
  149.4 1.3 collective-permute-start.27
  150.7 5.7 %all-to-all-start.3 = ((bf16[4,2,128,128]{3,2,1,0:T(8,128)(2,1)}), bf16[4,2,128,128]{3,2,1,0:T(8,128)(2,1)S(1)}, u32[]{:S(2)}, u32[]{:S(2)}) async-start(bf16[4,2,128,128]{3,2,1,0:T(8,128)(2,1)} %slice.49), calls=%async_computation.3 | async-start | bytes 524288 | tf_op jit(solution)/shard_map/out_far/all_to_all | solution.py:397
  156.4 1.3 collective-permute-start.26
  157.7 2.7 %collective-permute-done.18.refs_7_ = bf16[512,512]{1,0:T(8,128)(2,1)} collective-permute-done((bf16[512,512]{1,0:T(8,128)(2,1)S(1)}, bf16[512,512]{1,0:T(8,128)(2,1)}, u32[]{:S(2)}, u32[]{:S(2)}) %collective-permute-start.18) | collective-permute-done | bytes 524320 | tf_op jit(solution)/shard_map/out_query1_3/ppermute | solution.py:321
  160.4 1.3 collective-permute-start.25
  161.7 7.5 %collective-permute-done.20 = bf16[2,2048,128]{2,1,0:T(8,128)(2,1)} collective-permute-done((bf16[2,2048,128]{2,1,0:T(8,128)(2,1)}, bf16[2,2048,128]{2,1,0:T(8,128)(2,1)}, u32[]{:S(2)}, u32[]{:S(2)}) %collective-permute-start.20) | collective-permute-done | bytes 1048608 | tf_op jit(solution)/shard_map/out_pair1/ppermute | solution.py:317
  169.2 1.9 fusion.7
  171.1 1.6 collective-permute-start.21
  172.8 2.0 fusion.1
  175.2 0.7 fusion.12
  176.0 1.0 dynamic-slice_bitcast_fusion.4
  177.5 3.0 %collective-permute-done.26 = bf16[2,128,128]{2,1,0:T(8,128)(2,1)S(1)} collective-permute-done((bf16[2,128,128]{2,1,0:T(8,128)(2,1)S(1)}, bf16[2,128,128]{2,1,0:T(8,128)(2,1)S(1)}, u32[]{:S(2)}, u32[]{:S(2)}) %collective-permute-start.26) | collective-permute-done | bytes 65568 | tf_op jit(solution)/shard_map/out_first4/ppermute | solution.py:317
  180.4 1.7 collective-permute-start.23
  182.2 5.6 %assemble_queries.1 = bf16[512,4096]{1,0:T(8,128)(2,1)} custom-call(s32[2]{0:T(128)} %copy-done.2, bf16[512,512]{1,0:T(8,128)(2,1)} %copy-done, bf16[512,512]{1,0:T(8,128)(2,1)} %copy-done.1, bf16[512,512]{1,0:T(8,128)(2,1)} %collective-permute-done.11.refs_2_, bf16[512,512]{1,0:T(8,128)(2,1)} %collective-permute-done.16.refs_3_, ...), custom_call_target="tpu_custom_call" | custom-call | tf_op jit(solution)/shard_map/assemble_queries/pallas_call | solution.py:258
  187.8 2.1 collective-permute-done.23.refs_4_
  189.9 4.3 %collective-permute-done.24.refs_6_ = bf16[2,512,128]{2,1,0:T(8,128)(2,1)} collective-permute-done((bf16[2,512,128]{2,1,0:T(8,128)(2,1)}, bf16[2,512,128]{2,1,0:T(8,128)(2,1)}, u32[]{:S(2)}, u32[]{:S(2)}) %collective-permute-start.24) | collective-permute-done | bytes 262176 | tf_op jit(solution)/shard_map/out_pairs0_3/ppermute | solution.py:321
  194.2 7.8 %collective-permute-done.21 = bf16[2,2048,128]{2,1,0:T(8,128)(2,1)} collective-permute-done((bf16[2,2048,128]{2,1,0:T(8,128)(2,1)S(1)}, bf16[2,2048,128]{2,1,0:T(8,128)(2,1)}, u32[]{:S(2)}, u32[]{:S(2)}) %collective-permute-start.21) | collective-permute-done | bytes 1048608 | tf_op jit(solution)/shard_map/out_onward1/ppermute | solution.py:317
  202.0 1.9 fusion.5
  204.4 0.7 fusion.9
  205.2 0.8 dynamic-slice_bitcast_fusion
  206.1 1.1 collective-permute-start.29
  207.1 0.7 collective-permute-start.30
  207.8 7.4 %collective-permute-done.29.refs_5_ = bf16[2,512,128]{2,1,0:T(8,128)(2,1)S(1)} collective-permute-done((bf16[2,512,128]{2,1,0:T(8,128)(2,1)S(1)}, bf16[2,512,128]{2,1,0:T(8,128)(2,1)S(1)}, u32[]{:S(2)}, u32[]{:S(2)}) %collective-permute-start.29) | collective-permute-done | bytes 262176 | tf_op jit(solution)/shard_map/out_pairs1_2/ppermute | solution.py:321
  215.2 4.5 %collective-permute-done.30.refs_7_ = bf16[2,512,128]{2,1,0:T(8,128)(2,1)S(1)} collective-permute-done((bf16[2,512,128]{2,1,0:T(8,128)(2,1)S(1)}, bf16[2,512,128]{2,1,0:T(8,128)(2,1)S(1)}, u32[]{:S(2)}, u32[]{:S(2)}) %collective-permute-start.30) | collective-permute-done | bytes 262176 | tf_op jit(solution)/shard_map/out_pairs1_3/ppermute | solution.py:321
  219.7 0.7 copy-done.12
  220.4 3.6 %assemble_pairs.1 = (bf16[512,1024]{1,0:T(8,128)(2,1)}, bf16[512,1024]{1,0:T(8,128)(2,1)}) custom-call(s32[2]{0:T(128)} %copy-done.2, bf16[2,512,128]{2,1,0:T(8,128)(2,1)} %get-tuple-element.80.refs_0_, bf16[2,512,128]{2,1,0:T(8,128)(2,1)} %get-tuple-element.76.refs_1_, bf16[2,512,128]{2,1,0:T(8,128)(2,1)} %collective-permute-done.22.refs_2_, ...), custom_call_target="tpu_custom_call" | custom-call | tf_op jit(solution)/shard_map/assemble_pairs/pallas_call | solution.py:287
  (77 shorter events, 4.0 us)
Async XLA Ops:
  2.3 6.0 %copy-start.6 = (s32[8]{0:T(128)S(1)}, s32[8]{0:T(128)}, u32[]{:S(2)}) copy-start(s32[8]{0:T(128)} %vertical.3) | copy-start | bytes 100
  2.4 21.7 %copy-start.7 = (bf16[2,2048,128]{2,1,0:T(8,128)(2,1)}, bf16[2,2048,128]{2,1,0:T(8,128)(2,1)S(1)}, u32[]{:S(2)}) copy-start(bf16[2,2048,128]{2,1,0:T(8,128)(2,1)S(1)} %pad_maximum_fusion.refs_2_) | copy-start | bytes 3145732
  2.4 28.5 %collective-permute-start = (bf16[2,2048,128]{2,1,0:T(8,128)(2,1)S(1)}, bf16[2,2048,128]{2,1,0:T(8,128)(2,1)}, u32[]{:S(2)}, u32[]{:S(2)}) collective-permute-start(bf16[2,2048,128]{2,1,0:T(8,128)(2,1)S(1)} %pad_maximum_fusion.refs_2_), channel_id=1, source_target_pairs={{0,8},{4,12},{8,16},{12,20},{16,24},{20,28},{1,9},{5,13},{9,17},{1... | collective-permute-start | bytes 3145736 | tf_op jit(solution)/shard_map/in_back0/ppermute | solution.py:317
  9.7 38.4 %collective-permute-start.4 = (bf16[2,2,128,128]{3,2,1,0:T(8,128)(2,1)S(1)}, bf16[2,2,128,128]{3,2,1,0:T(8,128)(2,1)S(1)}, u32[]{:S(2)}, u32[]{:S(2)}) collective-permute-start(bf16[2,2,128,128]{3,2,1,0:T(8,128)(2,1)S(1)} %pad_maximum_fusion.2), channel_id=1, source_target_pairs={{0,24},{1,25},{2,26},{3,27}} | collective-permute-start | bytes 393224 | tf_op jit(solution)/shard_map/in_first6/ppermute | solution.py:317
  12.0 36.0 %collective-permute-start.3 = (bf16[2,2,128,128]{3,2,1,0:T(8,128)(2,1)S(1)}, bf16[2,2,128,128]{3,2,1,0:T(8,128)(2,1)S(1)}, u32[]{:S(2)}, u32[]{:S(2)}) collective-permute-start(bf16[2,2,128,128]{3,2,1,0:T(8,128)(2,1)S(1)} %pad_maximum_fusion.2), channel_id=1, source_target_pairs={{0,16},{1,17},{2,18},{3,19}} | collective-permute-start | bytes 393224 | tf_op jit(solution)/shard_map/in_first4/ppermute | solution.py:317
  13.9 34.2 %collective-permute-start.2 = (bf16[2,2,128,128]{3,2,1,0:T(8,128)(2,1)S(1)}, bf16[2,2,128,128]{3,2,1,0:T(8,128)(2,1)}, u32[]{:S(2)}, u32[]{:S(2)}) collective-permute-start(bf16[2,2,128,128]{3,2,1,0:T(8,128)(2,1)S(1)} %pad_maximum_fusion.2), channel_id=1, source_target_pairs={{0,8},{1,9},{2,10},{3,11}} | collective-permute-start | bytes 393224 | tf_op jit(solution)/shard_map/in_first2/ppermute | solution.py:317
  15.8 44.6 %collective-permute-start.6 = (bf16[2,2048,128]{2,1,0:T(8,128)(2,1)S(1)}, bf16[2,2048,128]{2,1,0:T(8,128)(2,1)}, u32[]{:S(2)}, u32[]{:S(2)}) collective-permute-start(bf16[2,2048,128]{2,1,0:T(8,128)(2,1)S(1)} %pad_maximum_fusion.refs_2_), channel_id=1, source_target_pairs={{0,4},{8,12},{16,20},{24,28},{1,5},{9,13},{17,21},{25,29},{2,6},{1... | collective-permute-start | bytes 3145736 | tf_op jit(solution)/shard_map/in_even0/ppermute | solution.py:317
  18.9 31.5 %copy-start.13 = (s32[16,2]{0,1:T(2,128)S(1)}, s32[16,2]{0,1:T(2,128)}, u32[]{:S(2)}) copy-start(s32[16,2]{0,1:T(2,128)} %param.12) | copy-start | bytes 388
  18.9 31.6 %copy-start.14 = (s32[16,2]{0,1:T(2,128)S(1)}, s32[16,2]{0,1:T(2,128)}, u32[]{:S(2)}) copy-start(s32[16,2]{0,1:T(2,128)} %param.13) | copy-start | bytes 388
  18.9 23.7 %all-to-all-start = ((bf16[4,2,128,128]{3,2,1,0:T(8,128)(2,1)}), bf16[4,2,128,128]{3,2,1,0:T(8,128)(2,1)S(1)}, u32[]{:S(2)}, u32[]{:S(2)}) async-start(bf16[4,2,128,128]{3,2,1,0:T(8,128)(2,1)} %broadcast_in_dim.90), calls=%async_computation | async-start | bytes 524288 | tf_op jit(solution)/shard_map/in_column0/all_to_all | solution.py:339
  30.9 31.9 %collective-permute-start.7 = (bf16[2,2048,128]{2,1,0:T(8,128)(2,1)}, bf16[2,2048,128]{2,1,0:T(8,128)(2,1)}, u32[]{:S(2)}, u32[]{:S(2)}) collective-permute-start(bf16[2,2048,128]{2,1,0:T(8,128)(2,1)} %collective-permute-done.refs_7_), channel_id=1, source_target_pairs={{4,0},{12,8},{20,16},{28,24},{5,1},{13,9},{21,17},{29,25},{6,2},{1... | collective-permute-start | bytes 3145736 | tf_op jit(solution)/shard_map/in_odd0/ppermute | solution.py:317
  43.3 17.2 %all-to-all-start.1 = ((bf16[4,2,128,128]{3,2,1,0:T(8,128)(2,1)}), bf16[4,2,128,128]{3,2,1,0:T(8,128)(2,1)S(1)}, u32[]{:S(2)}, u32[]{:S(2)}) async-start(bf16[4,2,128,128]{3,2,1,0:T(8,128)(2,1)} %broadcast_in_dim.92), calls=%async_computation.1 | async-start | bytes 524288 | tf_op jit(solution)/shard_map/in_column1/all_to_all | solution.py:339
  49.0 6.6 %collective-permute-start.5 = (bf16[2,2,128,128]{3,2,1,0:T(8,128)(2,1)S(1)}, bf16[2,2,128,128]{3,2,1,0:T(8,128)(2,1)S(1)}, u32[]{:S(2)}, u32[]{:S(2)}) collective-permute-start(bf16[2,2,128,128]{3,2,1,0:T(8,128)(2,1)S(1)} %add_add_fusion.refs_5_), channel_id=1, source_target_pairs={{0,4},{8,12},{16,20},{24,28},{1,5},{9,13},{17,21},{25,29},{2,6},{1... | collective-permute-start | bytes 393224 | tf_op jit(solution)/shard_map/in_first_pair/ppermute | solution.py:317
  50.3 12.5 %collective-permute-start.1 = (bf16[4,2,128,128]{3,2,1,0:T(8,128)(2,1)S(1)}, bf16[4,2,128,128]{3,2,1,0:T(8,128)(2,1)S(1)}, u32[]{:S(2)}, u32[]{:S(2)}) collective-permute-start(bf16[4,2,128,128]{3,2,1,0:T(8,128)(2,1)S(1)} %all-to-all-done.refs_3_), channel_id=1, source_target_pairs={{0,4},{4,0},{8,12},{12,8},{16,20},{20,16},{24,28},{28,24},{1,5},{5... | collective-permute-start | bytes 786440 | tf_op jit(solution)/shard_map/in_column_pair0/ppermute | solution.py:317
  50.7 53.2 %copy-start.2 = (s32[2]{0:T(128)}, s32[2]{0:T(128)S(1)}, u32[]{:S(2)}) copy-start(s32[2]{0:T(128)S(1)} %pad_add_fusion.place) | copy-start | bytes 28
  50.7 51.2 %collective-permute-start.9 = (bf16[2,2048,128]{2,1,0:T(8,128)(2,1)}, bf16[2,2048,128]{2,1,0:T(8,128)(2,1)}, u32[]{:S(2)}, u32[]{:S(2)}) collective-permute-start(bf16[2,2048,128]{2,1,0:T(8,128)(2,1)} %pad_maximum_fusion.1.refs_2_), channel_id=1, source_target_pairs={{0,8},{4,12},{8,16},{12,20},{16,24},{20,28},{1,9},{5,13},{9,17},{1... | collective-permute-start | bytes 3145736 | tf_op jit(solution)/shard_map/in_back1/ppermute | solution.py:317
  55.6 48.2 %collective-permute-start.10 = (bf16[2,2048,128]{2,1,0:T(8,128)(2,1)}, bf16[2,2048,128]{2,1,0:T(8,128)(2,1)}, u32[]{:S(2)}, u32[]{:S(2)}) collective-permute-start(bf16[2,2048,128]{2,1,0:T(8,128)(2,1)} %pad_maximum_fusion.1.refs_2_), channel_id=1, source_target_pairs={{0,4},{4,8},{8,12},{12,16},{16,20},{20,24},{24,28},{1,5},{5,9},{9,... | collective-permute-start | bytes 3145736 | tf_op jit(solution)/shard_map/in_prev1/ppermute | solution.py:317
  60.5 40.6 %collective-permute-start.8 = (bf16[4,2,128,128]{3,2,1,0:T(8,128)(2,1)S(1)}, bf16[4,2,128,128]{3,2,1,0:T(8,128)(2,1)S(1)}, u32[]{:S(2)}, u32[]{:S(2)}) collective-permute-start(bf16[4,2,128,128]{3,2,1,0:T(8,128)(2,1)S(1)} %all-to-all-done.1.refs_3_), channel_id=1, source_target_pairs={{0,4},{4,0},{8,12},{12,8},{16,20},{20,16},{24,28},{28,24},{1,5},{5... | collective-permute-start | bytes 786440 | tf_op jit(solution)/shard_map/in_column_pair1/ppermute | solution.py:317
  91.2 0.8 copy-start
  92.0 45.7 %collective-permute-start.11 = (bf16[512,512]{1,0:T(8,128)(2,1)}, bf16[512,512]{1,0:T(8,128)(2,1)}, u32[]{:S(2)}, u32[]{:S(2)}) collective-permute-start(bf16[512,512]{1,0:T(8,128)(2,1)} %get-tuple-element.48), channel_id=1, source_target_pairs={{0,1},{1,0},{2,3},{3,2},{4,5},{5,4},{6,7},{7,6},{8,9},{9,8},{10,11... | collective-permute-start | bytes 1572872 | tf_op jit(solution)/shard_map/out_query0_1/ppermute | solution.py:321
  92.0 45.7 %collective-permute-start.12 = (bf16[512,512]{1,0:T(8,128)(2,1)}, bf16[512,512]{1,0:T(8,128)(2,1)}, u32[]{:S(2)}, u32[]{:S(2)}) collective-permute-start(bf16[512,512]{1,0:T(8,128)(2,1)} %get-tuple-element.49), channel_id=1, source_target_pairs={{0,2},{1,3},{2,0},{3,1},{4,6},{5,7},{6,4},{7,5},{8,10},{9,11},{10,... | collective-permute-start | bytes 1572872 | tf_op jit(solution)/shard_map/out_query0_2/ppermute | solution.py:321
  93.5 44.2 %all-to-all-start.2 = ((bf16[8,2,2,128,128]{4,3,2,1,0:T(8,128)(2,1)}), bf16[8,2,2,128,128]{4,3,2,1,0:T(8,128)(2,1)}, u32[]{:S(2)}, u32[]{:S(2)}) async-start(bf16[8,2,2,128,128]{4,3,2,1,0:T(8,128)(2,1)} %get-tuple-element.51), calls=%async_computation.2 | async-start | bytes 2097152 | tf_op jit(solution)/shard_map/out_far0/all_to_all | solution.py:375
  101.1 0.7 copy-start.4
  101.8 35.9 %collective-permute-start.13 = (bf16[512,512]{1,0:T(8,128)(2,1)}, bf16[512,512]{1,0:T(8,128)(2,1)}, u32[]{:S(2)}, u32[]{:S(2)}) collective-permute-start(bf16[512,512]{1,0:T(8,128)(2,1)} %get-tuple-element.50), channel_id=1, source_target_pairs={{0,3},{1,2},{2,1},{3,0},{4,7},{5,6},{6,5},{7,4},{8,11},{9,10},{10,... | collective-permute-start | bytes 1572872 | tf_op jit(solution)/shard_map/out_query0_3/ppermute | solution.py:321
  101.9 35.8 %collective-permute-start.14 = (bf16[2,2048,128]{2,1,0:T(8,128)(2,1)}, bf16[2,2048,128]{2,1,0:T(8,128)(2,1)}, u32[]{:S(2)}, u32[]{:S(2)}) collective-permute-start(bf16[2,2048,128]{2,1,0:T(8,128)(2,1)} %get-tuple-element.53), channel_id=1, source_target_pairs={{0,4},{4,0},{8,12},{12,8},{16,20},{20,16},{24,28},{28,24},{1,5},{5... | collective-permute-start | bytes 3145736 | tf_op jit(solution)/shard_map/out_pair0/ppermute | solution.py:317
  103.8 1.0 copy-start.5
  132.7 0.8 copy-start.1
  133.5 0.7 copy-start.3
  137.7 10.9 %collective-permute-start.15 = (bf16[5,2,128,128]{3,2,1,0:T(8,128)(2,1)}, bf16[5,2,128,128]{3,2,1,0:T(8,128)(2,1)S(1)}, u32[]{:S(2)}, u32[]{:S(2)}) collective-permute-start(bf16[5,2,128,128]{3,2,1,0:T(8,128)(2,1)} %copy-done.3), channel_id=1, source_target_pairs={{0,4},{4,0},{8,12},{12,8},{16,20},{20,16},{24,28},{28,24},{1,5},{5... | collective-permute-start | bytes 983048 | tf_op jit(solution)/shard_map/out_far_pair1/ppermute | solution.py:317
  138.0 18.4 %collective-permute-start.17 = (bf16[512,512]{1,0:T(8,128)(2,1)S(1)}, bf16[512,512]{1,0:T(8,128)(2,1)}, u32[]{:S(2)}, u32[]{:S(2)}) collective-permute-start(bf16[512,512]{1,0:T(8,128)(2,1)S(1)} %get-tuple-element.64), channel_id=1, source_target_pairs={{0,2},{1,3},{2,0},{3,1},{4,6},{5,7},{6,4},{7,5},{8,10},{9,11},{10,... | collective-permute-start | bytes 1572872 | tf_op jit(solution)/shard_map/out_query1_2/ppermute | solution.py:321
  138.5 21.9 %collective-permute-start.18 = (bf16[512,512]{1,0:T(8,128)(2,1)S(1)}, bf16[512,512]{1,0:T(8,128)(2,1)}, u32[]{:S(2)}, u32[]{:S(2)}) collective-permute-start(bf16[512,512]{1,0:T(8,128)(2,1)S(1)} %get-tuple-element.65), channel_id=1, source_target_pairs={{0,3},{1,2},{2,1},{3,0},{4,7},{5,6},{6,5},{7,4},{8,11},{9,10},{10,... | collective-permute-start | bytes 1572872 | tf_op jit(solution)/shard_map/out_query1_3/ppermute | solution.py:321
  138.6 30.7 %collective-permute-start.20 = (bf16[2,2048,128]{2,1,0:T(8,128)(2,1)}, bf16[2,2048,128]{2,1,0:T(8,128)(2,1)}, u32[]{:S(2)}, u32[]{:S(2)}) collective-permute-start(bf16[2,2048,128]{2,1,0:T(8,128)(2,1)} %get-tuple-element.67), channel_id=1, source_target_pairs={{0,4},{4,0},{8,12},{12,8},{16,20},{20,16},{24,28},{28,24},{1,5},{5... | collective-permute-start | bytes 3145736 | tf_op jit(solution)/shard_map/out_pair1/ppermute | solution.py:317
  143.1 28.0 %collective-permute-start.19 = (bf16[2,2048,128]{2,1,0:T(8,128)(2,1)}, bf16[2,2048,128]{2,1,0:T(8,128)(2,1)}, u32[]{:S(2)}, u32[]{:S(2)}) collective-permute-start(bf16[2,2048,128]{2,1,0:T(8,128)(2,1)} %fusion.3), channel_id=1, source_target_pairs={{8,0},{12,4},{16,8},{20,12},{24,16},{28,20},{9,1},{13,5},{17,9},{2... | collective-permute-start | bytes 3145736 | tf_op jit(solution)/shard_map/out_onward0/ppermute | solution.py:317
  149.4 27.5 %collective-permute-start.27 = (bf16[2,128,128]{2,1,0:T(8,128)(2,1)S(1)}, bf16[2,128,128]{2,1,0:T(8,128)(2,1)S(1)}, u32[]{:S(2)}, u32[]{:S(2)}) collective-permute-start(bf16[2,128,128]{2,1,0:T(8,128)(2,1)S(1)} %slice_bitcast_fusion.6), channel_id=1, source_target_pairs={{24,0},{25,1},{26,2},{27,3}} | collective-permute-start | bytes 196616 | tf_op jit(solution)/shard_map/out_first6/ppermute | solution.py:317
  150.7 31.5 %all-to-all-start.3 = ((bf16[4,2,128,128]{3,2,1,0:T(8,128)(2,1)}), bf16[4,2,128,128]{3,2,1,0:T(8,128)(2,1)S(1)}, u32[]{:S(2)}, u32[]{:S(2)}) async-start(bf16[4,2,128,128]{3,2,1,0:T(8,128)(2,1)} %slice.49), calls=%async_computation.3 | async-start | bytes 524288 | tf_op jit(solution)/shard_map/out_far/all_to_all | solution.py:397
  156.4 24.0 %collective-permute-start.26 = (bf16[2,128,128]{2,1,0:T(8,128)(2,1)S(1)}, bf16[2,128,128]{2,1,0:T(8,128)(2,1)S(1)}, u32[]{:S(2)}, u32[]{:S(2)}) collective-permute-start(bf16[2,128,128]{2,1,0:T(8,128)(2,1)S(1)} %slice_bitcast_fusion.6), channel_id=1, source_target_pairs={{16,0},{17,1},{18,2},{19,3}} | collective-permute-start | bytes 196616 | tf_op jit(solution)/shard_map/out_first4/ppermute | solution.py:317
  160.4 21.7 %collective-permute-start.25 = (bf16[2,128,128]{2,1,0:T(8,128)(2,1)S(1)}, bf16[2,128,128]{2,1,0:T(8,128)(2,1)S(1)}, u32[]{:S(2)}, u32[]{:S(2)}) collective-permute-start(bf16[2,128,128]{2,1,0:T(8,128)(2,1)S(1)} %slice_bitcast_fusion.6), channel_id=1, source_target_pairs={{8,0},{9,1},{10,2},{11,3}} | collective-permute-start | bytes 196616 | tf_op jit(solution)/shard_map/out_first2/ppermute | solution.py:317
  169.2 13.0 %collective-permute-start.16 = (bf16[512,512]{1,0:T(8,128)(2,1)S(1)}, bf16[512,512]{1,0:T(8,128)(2,1)}, u32[]{:S(2)}, u32[]{:S(2)}) collective-permute-start(bf16[512,512]{1,0:T(8,128)(2,1)S(1)} %get-tuple-element.63), channel_id=1, source_target_pairs={{0,1},{1,0},{2,3},{3,2},{4,5},{5,4},{6,7},{7,6},{8,9},{9,8},{10,11... | collective-permute-start | bytes 1572872 | tf_op jit(solution)/shard_map/out_query1_1/ppermute | solution.py:321
  171.1 3.6 %copy-start.9 = (f32[2,128,128]{2,1,0:T(8,128)S(1)}, f32[2,128,128]{2,1,0:T(8,128)}, u32[]{:S(2)}) copy-start(f32[2,128,128]{2,1,0:T(8,128)} %get-tuple-element.90) | copy-start | bytes 393220
  171.1 30.8 %collective-permute-start.21 = (bf16[2,2048,128]{2,1,0:T(8,128)(2,1)S(1)}, bf16[2,2048,128]{2,1,0:T(8,128)(2,1)}, u32[]{:S(2)}, u32[]{:S(2)}) collective-permute-start(bf16[2,2048,128]{2,1,0:T(8,128)(2,1)S(1)} %fusion.7), channel_id=1, source_target_pairs={{8,0},{12,4},{16,8},{20,12},{24,16},{28,20},{9,1},{13,5},{17,9},{2... | collective-permute-start | bytes 3145736 | tf_op jit(solution)/shard_map/out_onward1/ppermute | solution.py:317
  177.0 10.8 %collective-permute-start.22 = (bf16[2,512,128]{2,1,0:T(8,128)(2,1)}, bf16[2,512,128]{2,1,0:T(8,128)(2,1)}, u32[]{:S(2)}, u32[]{:S(2)}) collective-permute-start(bf16[2,512,128]{2,1,0:T(8,128)(2,1)} %get-tuple-element.79), channel_id=1, source_target_pairs={{0,1},{1,0},{2,3},{3,2},{4,5},{5,4},{6,7},{7,6},{8,9},{9,8},{10,11... | collective-permute-start | bytes 786440 | tf_op jit(solution)/shard_map/out_pairs0_1/ppermute | solution.py:321
  180.4 9.5 %collective-permute-start.23 = (bf16[2,512,128]{2,1,0:T(8,128)(2,1)}, bf16[2,512,128]{2,1,0:T(8,128)(2,1)}, u32[]{:S(2)}, u32[]{:S(2)}) collective-permute-start(bf16[2,512,128]{2,1,0:T(8,128)(2,1)} %get-tuple-element.78), channel_id=1, source_target_pairs={{0,2},{1,3},{2,0},{3,1},{4,6},{5,7},{6,4},{7,5},{8,10},{9,11},{10,... | collective-permute-start | bytes 786440 | tf_op jit(solution)/shard_map/out_pairs0_2/ppermute | solution.py:321
  182.1 12.1 %collective-permute-start.24 = (bf16[2,512,128]{2,1,0:T(8,128)(2,1)}, bf16[2,512,128]{2,1,0:T(8,128)(2,1)}, u32[]{:S(2)}, u32[]{:S(2)}) collective-permute-start(bf16[2,512,128]{2,1,0:T(8,128)(2,1)} %get-tuple-element.77), channel_id=1, source_target_pairs={{0,3},{1,2},{2,1},{3,0},{4,7},{5,6},{6,5},{7,4},{8,11},{9,10},{10,... | collective-permute-start | bytes 786440 | tf_op jit(solution)/shard_map/out_pairs0_3/ppermute | solution.py:321
  182.2 19.8 %copy-start.8 = (bf16[2,2048,128]{2,1,0:T(8,128)(2,1)S(1)}, bf16[2,2048,128]{2,1,0:T(8,128)(2,1)}, u32[]{:S(2)}) copy-start(bf16[2,2048,128]{2,1,0:T(8,128)(2,1)} %get-tuple-element.66) | copy-start | bytes 3145732
  205.9 1.9 collective-permute-start.28
  206.1 9.2 %collective-permute-start.29 = (bf16[2,512,128]{2,1,0:T(8,128)(2,1)S(1)}, bf16[2,512,128]{2,1,0:T(8,128)(2,1)S(1)}, u32[]{:S(2)}, u32[]{:S(2)}) collective-permute-start(bf16[2,512,128]{2,1,0:T(8,128)(2,1)S(1)} %get-tuple-element.74), channel_id=1, source_target_pairs={{0,2},{1,3},{2,0},{3,1},{4,6},{5,7},{6,4},{7,5},{8,10},{9,11},{10,... | collective-permute-start | bytes 786440 | tf_op jit(solution)/shard_map/out_pairs1_2/ppermute | solution.py:321
  207.1 12.6 %collective-permute-start.30 = (bf16[2,512,128]{2,1,0:T(8,128)(2,1)S(1)}, bf16[2,512,128]{2,1,0:T(8,128)(2,1)S(1)}, u32[]{:S(2)}, u32[]{:S(2)}) collective-permute-start(bf16[2,512,128]{2,1,0:T(8,128)(2,1)S(1)} %get-tuple-element.73), channel_id=1, source_target_pairs={{0,3},{1,2},{2,1},{3,0},{4,7},{5,6},{6,5},{7,4},{8,11},{9,10},{10,... | collective-permute-start | bytes 786440 | tf_op jit(solution)/shard_map/out_pairs1_3/ppermute | solution.py:321
  207.8 11.9 %copy-start.10 = (bf16[2,512,128]{2,1,0:T(8,128)(2,1)}, bf16[2,512,128]{2,1,0:T(8,128)(2,1)S(1)}, u32[]{:S(2)}) copy-start(bf16[2,512,128]{2,1,0:T(8,128)(2,1)S(1)} %collective-permute-done.28.refs_3_) | copy-start | bytes 786436
  215.2 4.5 %copy-start.11 = (bf16[2,512,128]{2,1,0:T(8,128)(2,1)}, bf16[2,512,128]{2,1,0:T(8,128)(2,1)S(1)}, u32[]{:S(2)}) copy-start(bf16[2,512,128]{2,1,0:T(8,128)(2,1)S(1)} %collective-permute-done.29.refs_5_) | copy-start | bytes 786436
  219.7 0.7 copy-start.12
